TPU v7x, 32 devices: a whole 2x2x4 slice. The times are simulated.
32 devices in a mesh: fsdp: 32 (over z, y, x, core).
Axes of the slice: x: 2, y: 2, z: 4, core: 2. Of those that a mesh axis runs over, the one named last changes fastest.
Arguments:
- token_ids: int32 [32768], P('fsdp'), may hold values from 0 to 31999
- segment_ids: int32 [32768], P('fsdp'), may hold values from 0 to 15, as said below
- parent_segments: int32 [32, 16], P('fsdp'), may hold values from 0 to 14, as said below
- expert_choice: int32 [32768, 2], P('fsdp'), may hold values from 0 to 7, all different within a row
- drop_order: int32 [32, 2048], P('fsdp'), may hold values from 0 to 2047, each once within a row
- loss_positions: int32 [4096], P('fsdp'), may hold values from 0 to 1023
- target_ids: int32 [4096, 2], P('fsdp'), may hold values from 0 to 31999
- embedding: bfloat16 [32000, 768], P('fsdp'), may hold values from -0.3125 to 0.3125
- attention_weights: bfloat16 [3072, 768], P('fsdp'), may hold values from -2 to 2
- router_weights: bfloat16 [6144], P('fsdp'), may hold values from -0.4375 to 0.4375
- small_params: bfloat16 [2688], P('fsdp'), may hold values from -3 to 3
- inward_weights: bfloat16 [32, 768, 768], P('fsdp'), may hold values from -0.21875 to 0.21875
- outward_weights: bfloat16 [32, 768, 768], P('fsdp'), may hold values from -0.109375 to 0.109375
- embedding_moment: float32 [32000, 768], P('fsdp'), may hold values from -0.00083921955 to 0.00083921955
- embedding_square: float32 [32000, 768], P('fsdp'), may hold values from 2.4152587e-09 to 9.661035e-09
- attention_moment: float32 [3072, 768], P('fsdp'), may hold values from -0.00083921955 to 0.00083921955
- attention_square: float32 [3072, 768], P('fsdp'), may hold values from 2.4152587e-09 to 9.661035e-09
- router_moment: float32 [6144], P('fsdp'), may hold values from -0.00083921955 to 0.00083921955
- router_square: float32 [6144], P('fsdp'), may hold values from 2.4152587e-09 to 9.661035e-09
- params_moment: float32 [2688], P('fsdp'), may hold values from -0.00083921955 to 0.00083921955
- params_square: float32 [2688], P('fsdp'), may hold values from 2.4152587e-09 to 9.661035e-09
- inward_moment: float32 [32, 768, 768], P('fsdp'), may hold values from -1.8649323e-06 to 1.8649323e-06
- inward_square: float32 [32, 768, 768], P('fsdp'), may hold values from 6.038147e-13 to 2.4152587e-12
- outward_moment: float32 [32, 768, 768], P('fsdp'), may hold values from -1.8649323e-06 to 1.8649323e-06
- outward_square: float32 [32, 768, 768], P('fsdp'), may hold values from 6.038147e-13 to 2.4152587e-12
Outputs:
- loss_parts: float32 [32], P('fsdp')
- grad_norm: float32 [], replicated
- embedding_moment_next: float32 [32000, 768], P('fsdp')
- embedding_square_next: float32 [32000, 768], P('fsdp')
- embedding_update: float32 [32000, 768], P('fsdp')
- attention_moment_next: float32 [3072, 768], P('fsdp')
- attention_square_next: float32 [3072, 768], P('fsdp')
- attention_update: float32 [3072, 768], P('fsdp')
- router_moment_next: float32 [6144], P('fsdp')
- router_square_next: float32 [6144], P('fsdp')
- router_update: float32 [6144], P('fsdp')
- params_moment_next: float32 [2688], P('fsdp')
- params_square_next: float32 [2688], P('fsdp')
- params_update: float32 [2688], P('fsdp')
- inward_moment_next: float32 [32, 768, 768], P('fsdp')
- inward_square_next: float32 [32, 768, 768], P('fsdp')
- inward_update: float32 [32, 768, 768], P('fsdp')
- outward_moment_next: float32 [32, 768, 768], P('fsdp')
- outward_square_next: float32 [32, 768, 768], P('fsdp')
- outward_update: float32 [32, 768, 768], P('fsdp')
Inputs may be any that keep to these rules, and one draw needn't show every extreme that they name: `segment_ids`: on each device the first 256 tokens are segment 0, then the ids rise by one at each new segment up to 15; every segment holds at least one token. `parent_segments`: segment 0's parent is 0; every other segment's parent is a lower segment.
All inputs are finite; a program needn't handle non-finite values.
Results may differ from a plain program's by a relative error of at most 0.0024.
The roundings to bfloat16 on the way count: a program that leaves them out, or rounds other values in their place, can miss the bound.
Values may be sent and summed in bfloat16 or wider, within the bound.
A program may use at most 576 MiB of HBM per device.

v0:
```python
import math

import jax
import jax.numpy as jnp
from jax import lax
from jax.sharding import PartitionSpec as P

HEADS = 12
NB = 32
SPLIT = 4
STEP = 10


bucket_marks = (16, 23, 32, 45, 64, 91, 128, 181, 256, 362, 512, 724, 1024, 1448, 2048, 2896)
learn_rate = 0.02
weight_decay = 0.1
clip_base = 8.0


def rms_norm(values, gains):
    return values * lax.rsqrt(jnp.mean(values * values, axis=-1, keepdims=True) + 1e-06) * gains


def bucket_of(distance):
    distance = jnp.maximum(distance, 0)
    bucket = jnp.minimum(distance, 15)
    for border in bucket_marks:
        bucket = bucket + (distance >= border).astype(jnp.int32)
    return bucket


def tree_layout(segments, parents):
    segment_count = parents.shape[0]
    identity_rows = jnp.eye(segment_count, dtype=jnp.int32)

    def widen(step_index, ancestry):
        return jnp.maximum(ancestry, ancestry[parents])

    ancestry = lax.fori_loop(0, segment_count, widen, identity_rows)
    member = (segments[:, None] == jnp.arange(segment_count, dtype=jnp.int32)[None, :]).astype(
        jnp.int32
    )
    lengths = jnp.sum(member, axis=0)
    starts = jnp.cumsum(lengths) - lengths
    before = jnp.sum((ancestry - identity_rows) * lengths[None, :], axis=1)
    tree_depth = jnp.sum(member * (before - starts)[None, :], axis=1) + jnp.arange(
        segments.shape[0], dtype=jnp.int32
    )
    reach_rows = jnp.dot(member.astype(jnp.float32), ancestry.astype(jnp.float32))
    return (reach_rows, member.astype(jnp.float32), tree_depth)


def block_masks(block_start, block_rows, reach_rows, member, tree_depth):
    length = tree_depth.shape[0]
    linked = jnp.dot(reach_rows[block_start : block_start + block_rows], member.T) > 0.5
    key_order = jnp.arange(length, dtype=jnp.int32)
    query_order = block_start + jnp.arange(block_rows, dtype=jnp.int32)
    allowed = linked & (key_order[None, :] <= query_order[:, None])
    distance = tree_depth[block_start : block_start + block_rows][:, None] - tree_depth[None, :]
    buckets = jnp.where(allowed, bucket_of(distance), NB)
    selector = (jnp.arange(NB, dtype=jnp.int32)[:, None, None] == buckets[None]).astype(
        jnp.bfloat16
    )
    return (allowed, selector)


def block_scores(queries_block, keys_all, selector, bias_low, allowed):
    scores = (
        jnp.einsum("ihd,jhd->hij", queries_block, keys_all, preferred_element_type=jnp.float32)
        * 0.125
    )
    scores = scores + jnp.einsum(
        "bij,hb->hij", selector, bias_low, preferred_element_type=jnp.float32
    )
    return jnp.where(allowed[None], scores, -1e30)


def adam_step(weight, moment, square, gradient, factor):
    clipped = gradient * factor
    moment_next = 0.9 * moment + 0.1 * clipped
    square_next = 0.95 * square + 0.05 * clipped * clipped
    corrected_moment = moment_next / (1.0 - 0.9**STEP)
    corrected_square = square_next / (1.0 - 0.95**STEP)
    update = -learn_rate * (
        corrected_moment / (jnp.sqrt(corrected_square) + 1e-08)
        + weight_decay * weight.astype(jnp.float32)
    )
    return (moment_next, square_next, update)


def local(
    token_ids,
    segment_ids,
    parent_segments,
    expert_choice,
    drop_order,
    loss_positions,
    target_ids,
    embedding,
    attention_weights,
    router_weights,
    small_params,
    inward_weights,
    outward_weights,
    embedding_moment,
    embedding_square,
    attention_moment,
    attention_square,
    router_moment,
    router_square,
    params_moment,
    params_square,
    inward_moment,
    inward_square,
    outward_moment,
    outward_square,
):
    devices = lax.axis_size("fsdp")
    length = token_ids.shape[0]
    model_width = embedding.shape[1]
    head_size = model_width // HEADS
    rows_loss = loss_positions.shape[0]
    experts_all = devices // SPLIT
    capacity = 9 * 2 * length // (8 * experts_all)
    block_rows = min(512, length)
    f32 = jnp.float32
    bf16 = jnp.bfloat16
    table_full, attention_full, router_full, params_full = (
        lax.all_gather(embedding, "fsdp", axis=0, tiled=True),
        lax.all_gather(attention_weights, "fsdp", axis=0, tiled=True),
        lax.all_gather(router_weights, "fsdp", axis=0, tiled=True),
        lax.all_gather(small_params, "fsdp", axis=0, tiled=True),
    )
    embedded = table_full[token_ids].astype(f32) * math.sqrt(model_width)
    gains_all = params_full[: 3 * model_width].astype(f32)
    gain_first = gains_all[:model_width]
    gain_second = gains_all[model_width : 2 * model_width]
    gain_final = gains_all[2 * model_width :]
    bias_low = params_full[3 * model_width :].reshape(HEADS, NB)
    reach_rows, member, tree_depth = tree_layout(segment_ids, parent_segments[0])
    normed_first = rms_norm(embedded, gain_first).astype(bf16)
    queries = (
        jnp.dot(normed_first, attention_full[:model_width], preferred_element_type=f32)
        .astype(bf16)
        .reshape(length, HEADS, head_size)
    )
    keys_all = (
        jnp.dot(
            normed_first, attention_full[model_width : 2 * model_width], preferred_element_type=f32
        )
        .astype(bf16)
        .reshape(length, HEADS, head_size)
    )
    values_all = (
        jnp.dot(
            normed_first,
            attention_full[2 * model_width : 3 * model_width],
            preferred_element_type=f32,
        )
        .astype(bf16)
        .reshape(length, HEADS, head_size)
    )
    log_totals = []
    mixed_parts = []
    for block_start in range(0, length, block_rows):
        allowed, selector = block_masks(block_start, block_rows, reach_rows, member, tree_depth)
        scores = block_scores(
            queries[block_start : block_start + block_rows], keys_all, selector, bias_low, allowed
        )
        row_peak = jnp.max(scores, axis=-1, keepdims=True)
        raised = jnp.exp(scores - row_peak)
        totals = jnp.sum(raised, axis=-1, keepdims=True)
        log_totals.append(row_peak + jnp.log(totals))
        mixed_parts.append(
            jnp.einsum(
                "hij,jhd->ihd",
                (raised / totals).astype(bf16),
                values_all,
                preferred_element_type=f32,
            )
            .astype(bf16)
            .reshape(block_rows, model_width)
        )
    mixed_all = jnp.concatenate(mixed_parts, axis=0)
    after_attn = embedded + jnp.dot(
        mixed_all, attention_full[3 * model_width :], preferred_element_type=f32
    )
    routed_in = rms_norm(after_attn, gain_second).astype(bf16)
    router_matrix = router_full.reshape(model_width, experts_all)
    route_logits = jnp.dot(routed_in, router_matrix, preferred_element_type=f32)
    choice_onehot = (
        expert_choice[:, :, None] == jnp.arange(experts_all, dtype=jnp.int32)[None, None, :]
    ).astype(f32)
    chosen = jnp.sum(choice_onehot * route_logits[:, None, :], axis=-1)
    gate_peak = jnp.max(chosen, axis=1, keepdims=True)
    raised_gate = jnp.exp(chosen - gate_peak)
    gate_weights = raised_gate / jnp.sum(raised_gate, axis=1, keepdims=True)
    drop_rank = drop_order[0]
    flat_choice = expert_choice.reshape(-1)
    ranked = jnp.zeros_like(flat_choice).at[drop_rank].set(flat_choice)
    rank_hits = (ranked[:, None] == jnp.arange(experts_all, dtype=jnp.int32)[None, :]).astype(
        jnp.int32
    )
    ranked_slot = jnp.sum((jnp.cumsum(rank_hits, axis=0) - rank_hits) * rank_hits, axis=1)
    slot_index = ranked_slot[drop_rank].reshape(length, 2)
    target_row = jnp.where(
        slot_index < capacity, expert_choice * capacity + slot_index, experts_all * capacity
    )
    outgoing = (
        jnp.zeros((experts_all * capacity + 1, model_width), bf16)
        .at[target_row.reshape(-1)]
        .set(jnp.repeat(routed_in, 2, axis=0))
    )
    outgoing = jnp.repeat(outgoing[:-1].reshape(experts_all, capacity, model_width), SPLIT, axis=0)
    arrived = lax.all_to_all(outgoing, "fsdp", split_axis=0, concat_axis=0, tiled=True)
    expert_rows = arrived.reshape(devices * capacity, model_width)
    before_act = jnp.dot(expert_rows, inward_weights[0], preferred_element_type=f32)
    hidden = jax.nn.gelu(before_act, approximate=True).astype(bf16)
    partial_out = jnp.dot(hidden, outward_weights[0], preferred_element_type=f32).astype(bf16)
    returned_parts = lax.all_to_all(
        partial_out.reshape(devices, capacity, model_width),
        "fsdp",
        split_axis=0,
        concat_axis=0,
        tiled=True,
    )
    summed = jnp.sum(
        returned_parts.reshape(experts_all, SPLIT, capacity, model_width).astype(f32), axis=1
    )
    summed = jnp.concatenate(
        [summed.reshape(experts_all * capacity, model_width), jnp.zeros((1, model_width), f32)],
        axis=0,
    )
    returned = summed[target_row]
    after_moe = after_attn + jnp.sum(gate_weights[:, :, None] * returned, axis=1)
    normed_final = rms_norm(after_moe, gain_final)
    picked = normed_final[loss_positions].astype(bf16)
    scale_rows = 1.0 / (devices * rows_loss)
    vocab_rows = table_full.shape[0]
    vocab_block = vocab_rows // 8
    block_offsets = jnp.arange(8, dtype=jnp.int32) * vocab_block

    def loss_block(running, inputs):
        row_peak, row_total, target_hits = running
        table_block, offset = inputs
        scores = jnp.einsum("rd,vd->rv", picked, table_block, preferred_element_type=f32)
        new_peak = jnp.maximum(row_peak, jnp.max(scores, axis=1))
        row_total = row_total * jnp.exp(row_peak - new_peak) + jnp.sum(
            jnp.exp(scores - new_peak[:, None]), axis=1
        )
        vocab_ids = offset + jnp.arange(vocab_block, dtype=jnp.int32)
        target_hits = target_hits + jnp.sum(
            jnp.where(vocab_ids[None, None, :] == target_ids[:, :, None], scores[:, None, :], 0.0),
            axis=-1,
        )
        return ((new_peak, row_total, target_hits), None)

    running_init = (
        jnp.full((rows_loss,), -1e30, f32),
        jnp.zeros((rows_loss,), f32),
        jnp.zeros((rows_loss, 2), f32),
    )
    (row_peak, row_total, target_hits), _ = lax.scan(
        loss_block, running_init, (table_full.reshape(8, vocab_block, model_width), block_offsets)
    )
    log_rows = row_peak + jnp.log(row_total)
    loss_local = jnp.sum(log_rows - target_hits[:, 0] + 0.3 * (log_rows - target_hits[:, 1]))
    table_back, attention_back, router_back, params_back = (
        lax.all_gather(embedding, "fsdp", axis=0, tiled=True),
        lax.all_gather(attention_weights, "fsdp", axis=0, tiled=True),
        lax.all_gather(router_weights, "fsdp", axis=0, tiled=True),
        lax.all_gather(small_params, "fsdp", axis=0, tiled=True),
    )

    def grad_block(running, inputs):
        table_block, offset = inputs
        scores = jnp.einsum("rd,vd->rv", picked, table_block, preferred_element_type=f32)
        probs = jnp.exp(scores - log_rows[:, None])
        vocab_ids = offset + jnp.arange(vocab_block, dtype=jnp.int32)
        pull = (
            1.3 * probs
            - (vocab_ids[None, :] == target_ids[:, 0:1]).astype(f32)
            - 0.3 * (vocab_ids[None, :] == target_ids[:, 1:2]).astype(f32)
        )
        pull = (pull * scale_rows).astype(bf16)
        table_part = jnp.einsum("rv,rd->vd", pull, picked, preferred_element_type=f32)
        running = running + jnp.einsum("rv,vd->rd", pull, table_block, preferred_element_type=f32)
        return (running, table_part)

    picked_grad, table_parts = lax.scan(
        grad_block,
        jnp.zeros((rows_loss, model_width), f32),
        (table_back.reshape(8, vocab_block, model_width), block_offsets),
    )
    bias_back = params_back[3 * model_width :].reshape(HEADS, NB)
    grad_normed = jnp.zeros((length, model_width), f32).at[loss_positions].add(picked_grad)
    _, final_back = jax.vjp(rms_norm, after_moe, gain_final)
    grad_after_moe, grad_gain_final = final_back(grad_normed)
    grad_gates = jnp.sum(returned * grad_after_moe[:, None, :], axis=-1)
    grad_chosen = gate_weights * (
        grad_gates - jnp.sum(gate_weights * grad_gates, axis=1, keepdims=True)
    )
    grad_route = jnp.sum(choice_onehot * grad_chosen[:, :, None], axis=1).astype(bf16)
    router_grad = jnp.einsum(
        "td,te->de", routed_in, grad_route, preferred_element_type=f32
    ).reshape(-1)
    grad_routed = jnp.einsum(
        "te,de->td",
        grad_route,
        router_back.reshape(model_width, experts_all),
        preferred_element_type=f32,
    )
    grad_slots = (
        jnp.zeros((experts_all * capacity + 1, model_width), f32)
        .at[target_row.reshape(-1)]
        .add((gate_weights[:, :, None] * grad_after_moe[:, None, :]).reshape(-1, model_width))
    )
    grad_slots = jnp.repeat(
        grad_slots[:-1].astype(bf16).reshape(experts_all, capacity, model_width), SPLIT, axis=0
    )
    grad_arrived = lax.all_to_all(
        grad_slots, "fsdp", split_axis=0, concat_axis=0, tiled=True
    ).reshape(devices * capacity, model_width)
    before_back, hidden_back = (before_act, hidden)
    outward_grad = jnp.einsum("rf,rd->fd", hidden_back, grad_arrived, preferred_element_type=f32)[
        None
    ]
    grad_hidden = jnp.einsum(
        "rd,fd->rf", grad_arrived, outward_weights[0], preferred_element_type=f32
    )
    _, gelu_back = jax.vjp(lambda inside: jax.nn.gelu(inside, approximate=True), before_back)
    grad_before = gelu_back(grad_hidden)[0].astype(bf16)
    inward_grad = jnp.einsum("rd,rf->df", expert_rows, grad_before, preferred_element_type=f32)[
        None
    ]
    grad_rows = jnp.einsum(
        "rf,df->rd", grad_before, inward_weights[0], preferred_element_type=f32
    ).astype(bf16)
    grad_returned = lax.all_to_all(
        grad_rows.reshape(devices, capacity, model_width),
        "fsdp",
        split_axis=0,
        concat_axis=0,
        tiled=True,
    )
    grad_summed = jnp.sum(
        grad_returned.reshape(experts_all, SPLIT, capacity, model_width).astype(f32), axis=1
    )
    grad_summed = jnp.concatenate(
        [
            grad_summed.reshape(experts_all * capacity, model_width),
            jnp.zeros((1, model_width), f32),
        ],
        axis=0,
    )
    grad_routed = grad_routed + jnp.sum(grad_summed[target_row], axis=1)
    _, second_back = jax.vjp(rms_norm, after_attn, gain_second)
    grad_norm_in, grad_gain_second = second_back(grad_routed)
    grad_after_attn = grad_after_moe + grad_norm_in
    grad_attn_low = grad_after_attn.astype(bf16)
    output_grad = jnp.einsum("td,te->de", mixed_all, grad_attn_low, preferred_element_type=f32)
    grad_mixed = (
        jnp.einsum(
            "te,de->td",
            grad_attn_low,
            attention_back[3 * model_width :],
            preferred_element_type=f32,
        )
        .astype(bf16)
        .reshape(length, HEADS, head_size)
    )
    grad_keys = jnp.zeros((length, HEADS, head_size), f32)
    grad_values = jnp.zeros((length, HEADS, head_size), f32)
    grad_bias = jnp.zeros((HEADS, NB), f32)
    grad_query_parts = []
    for block_number, block_start in enumerate(range(0, length, block_rows)):
        allowed, selector = block_masks(block_start, block_rows, reach_rows, member, tree_depth)
        query_block = queries[block_start : block_start + block_rows]
        scores = block_scores(query_block, keys_all, selector, bias_back, allowed)
        probs = jnp.exp(scores - log_totals[block_number])
        grad_out = grad_mixed[block_start : block_start + block_rows]
        grad_probs = jnp.einsum("ihd,jhd->hij", grad_out, values_all, preferred_element_type=f32)
        inner_sum = jnp.sum(probs * grad_probs, axis=-1, keepdims=True)
        grad_scores = (probs * (grad_probs - inner_sum)).astype(bf16)
        grad_query_parts.append(
            jnp.einsum("hij,jhd->ihd", grad_scores, keys_all, preferred_element_type=f32) * 0.125
        )
        grad_keys = (
            grad_keys
            + jnp.einsum("hij,ihd->jhd", grad_scores, query_block, preferred_element_type=f32)
            * 0.125
        )
        grad_values = grad_values + jnp.einsum(
            "hij,ihd->jhd", probs.astype(bf16), grad_out, preferred_element_type=f32
        )
        grad_bias = grad_bias + jnp.einsum(
            "hij,bij->hb", grad_scores, selector, preferred_element_type=f32
        )
    grad_queries_low = (
        jnp.concatenate(grad_query_parts, axis=0).reshape(length, model_width).astype(bf16)
    )
    grad_keys_low = grad_keys.reshape(length, model_width).astype(bf16)
    grad_values_low = grad_values.reshape(length, model_width).astype(bf16)
    projection_grads = []
    grad_normed_first = jnp.zeros((length, model_width), f32)
    for position, gradient_low in enumerate((grad_queries_low, grad_keys_low, grad_values_low)):
        projection_grads.append(
            jnp.einsum("td,te->de", normed_first, gradient_low, preferred_element_type=f32)
        )
        grad_normed_first = grad_normed_first + jnp.einsum(
            "te,de->td",
            gradient_low,
            attention_back[position * model_width : (position + 1) * model_width],
            preferred_element_type=f32,
        )
    attention_grad = jnp.concatenate(projection_grads + [output_grad], axis=0)
    _, first_back = jax.vjp(rms_norm, embedded, gain_first)
    grad_embed_in, grad_gain_first = first_back(grad_normed_first)
    grad_embedded = (grad_after_attn + grad_embed_in) * math.sqrt(model_width)
    params_grad = jnp.concatenate(
        [grad_gain_first, grad_gain_second, grad_gain_final, grad_bias.reshape(-1)]
    )
    table_grad = table_parts.reshape(vocab_rows, model_width).at[token_ids].add(grad_embedded)
    table_share, attention_share, router_share, params_share = (
        lax.psum_scatter(table_grad, "fsdp", scatter_dimension=0, tiled=True),
        lax.psum_scatter(attention_grad, "fsdp", scatter_dimension=0, tiled=True),
        lax.psum_scatter(router_grad, "fsdp", scatter_dimension=0, tiled=True),
        lax.psum_scatter(params_grad, "fsdp", scatter_dimension=0, tiled=True),
    )
    local_square = (
        jnp.sum(table_share * table_share)
        + jnp.sum(attention_share * attention_share)
        + jnp.sum(router_share * router_share)
        + jnp.sum(params_share * params_share)
        + jnp.sum(inward_grad * inward_grad)
        + jnp.sum(outward_grad * outward_grad)
    )
    total_square = lax.psum(local_square, "fsdp")
    grad_norm = jnp.sqrt(total_square)
    threshold = clip_base / math.sqrt(devices * rows_loss)
    factor = jnp.minimum(1.0, threshold / grad_norm)
    loss_parts = (loss_local * scale_rows).reshape(1)
    table_m, table_s, table_u = adam_step(
        embedding, embedding_moment, embedding_square, table_share, factor
    )
    attention_m, attention_s, attention_u = adam_step(
        attention_weights, attention_moment, attention_square, attention_share, factor
    )
    router_m, router_s, router_u = adam_step(
        router_weights, router_moment, router_square, router_share, factor
    )
    params_m, params_s, params_u = adam_step(
        small_params, params_moment, params_square, params_share, factor
    )
    inward_m, inward_s, inward_u = adam_step(
        inward_weights, inward_moment, inward_square, inward_grad, factor
    )
    outward_m, outward_s, outward_u = adam_step(
        outward_weights, outward_moment, outward_square, outward_grad, factor
    )
    return (
        loss_parts,
        grad_norm,
        table_m,
        table_s,
        table_u,
        attention_m,
        attention_s,
        attention_u,
        router_m,
        router_s,
        router_u,
        params_m,
        params_s,
        params_u,
        inward_m,
        inward_s,
        inward_u,
        outward_m,
        outward_s,
        outward_u,
    )


def solution(mesh):
    placed = (
        P("fsdp"),
        P("fsdp"),
        P("fsdp", None),
        P("fsdp", None),
        P("fsdp", None),
        P("fsdp"),
        P("fsdp", None),
        P("fsdp", None),
        P("fsdp", None),
        P("fsdp"),
        P("fsdp"),
        P("fsdp", None, None),
        P("fsdp", None, None),
        P("fsdp", None),
        P("fsdp", None),
        P("fsdp", None),
        P("fsdp", None),
        P("fsdp"),
        P("fsdp"),
        P("fsdp"),
        P("fsdp"),
        P("fsdp", None, None),
        P("fsdp", None, None),
        P("fsdp", None, None),
        P("fsdp", None, None),
    )
    return jax.shard_map(
        local,
        mesh=mesh,
        in_specs=placed,
        out_specs=(
            P("fsdp"),
            P(),
            P("fsdp", None),
            P("fsdp", None),
            P("fsdp", None),
            P("fsdp", None),
            P("fsdp", None),
            P("fsdp", None),
            P("fsdp"),
            P("fsdp"),
            P("fsdp"),
            P("fsdp"),
            P("fsdp"),
            P("fsdp"),
            P("fsdp", None, None),
            P("fsdp", None, None),
            P("fsdp", None, None),
            P("fsdp", None, None),
            P("fsdp", None, None),
            P("fsdp", None, None),
        ),
        check_vma=False,
    )
```

profile of v0, /device:TPU:0, one launch (start us, length us, event | category | flops | bytes accessed | tf_op | source)
XLA Modules:
  0.0 3406.1 jit_solution(6774089395819600789)
XLA Ops:
  13.8 44.9 %all-reduce.8 = (bf16[2688]{0:T(1024)(128)(2,1)S(1)}, bf16[6144]{0:T(1024)(128)(2,1)}) all-reduce(bf16[2688]{0:T(1024)(128)(2,1)S(1)} %dynamic-update-slice, bf16[6144]{0:T(1024)(128)(2,1)S(1)} %dynamic-update-slice.1), channel_id=1, replica_groups=mesh['fsdp'=32] {'fsdp'}, use_global_device_ids=true, to_apply=%add.2 | all-reduce | flops 8832 | bytes 35328
  70.5 11.8 gather_fusion.2
  84.0 9.9 while.38
  102.1 15.0 fusion.46
  117.1 15.2 fusion.44
  132.4 152.2 %all-gather.3.cloned.1.call-done = bf16[32000,768]{1,0:T(8,128)(2,1)} async-done(((bf16[1000,768]{1,0:T(8,128)(2,1)}), bf16[32000,768]{1,0:T(8,128)(2,1)}) %all-gather.3.cloned.1.call-update) | async-done | bytes 49152016 | tf_op jit(solution)/shard_map/all_gather | solution.py:129
  284.6 18.7 gather_fusion.1
  306.7 42.6 %all-gather.5.cloned.1.call-done = bf16[3072,768]{1,0:T(8,128)(2,1)} async-done(((bf16[96,768]{1,0:T(8,128)(2,1)}), bf16[3072,768]{1,0:T(8,128)(2,1)}) %all-gather.5.cloned.1.call-update) | async-done | bytes 4718608 | tf_op jit(solution)/shard_map/all_gather | solution.py:130
  354.0 29.0 fusion.255
  383.1 10.9 fusion.60
  395.6 10.9 fusion.170
  406.6 28.8 fusion.254
  435.3 10.9 fusion.61
  446.3 10.4 fusion.169
  474.1 12.5 scatter_custom_fusion.1
  490.0 311.0 %all_to_all.20 = bf16[32,288,768]{2,1,0:T(8,128)(2,1)} all-to-all(bf16[32,288,768]{2,1,0:T(8,128)(2,1)S(1)} %bitcast.252), channel_id=1, replica_groups=mesh['fsdp'=32] {'fsdp'}, dimensions={0} | all-to-all | bytes 28311552 | tf_op jit(solution)/shard_map/all_to_all | solution.py:215
  801.0 20.4 fusion.179
  821.4 23.0 convolution_convert_fusion.1
  851.9 310.8 %all-to-all-done.1 = bf16[32,288,768]{2,1,0:T(8,128)(2,1)} async-done(((bf16[32,288,768]{2,1,0:T(8,128)(2,1)}), bf16[32,288,768]{2,1,0:T(8,128)(2,1)}, u32[]{:S(2)}, u32[]{:S(2)}) %all-to-all-start.1) | async-done | bytes 14155808 | tf_op jit(solution)/shard_map/all_to_all | solution.py:220
  1173.9 13.7 gather_fusion.3
  1195.7 31.3 multiply_reduce_fusion.3
  1241.1 79.2 %while.39 = (s32[]{:T(128)}, f32[128]{0:T(128)S(1)}, f32[128]{0:T(128)}, f32[128,2]{0,1:T(2,128)}, bf16[8,4000,768]{2,1,0:T(8,128)(2,1)}, /*index=5*/bf16[128,76...) while((s32[]{:T(128)}, f32[128]{0:T(128)S(1)}, f32[128]{0:T(128)}, ...), condition=%wide.region_27.28_spmd.clone, body=%wide.region_23.27_spmd.clone.sunk | while | flops 791044864 | bytes 12540925 | solution.py:263
  1322.3 131.4 %while.40 = (s32[]{:T(128)}, f32[128,768]{1,0:T(8,128)S(1)}, f32[8,4000,768]{2,1,0:T(8,128)}, bf16[8,4000,768]{2,1,0:T(8,128)(2,1)}, bf16[128,768]{1,0:T(8,128)(...) while((s32[]{:T(128)}, f32[128,768]{1,0:T(8,128)S(1)}, ...), condition=%wide.region_30.31_spmd.clone, body=%wide.region_29.30_spmd.clone.sunk | while | flops 2364616704 | bytes 29649840 | solution.py:290
  1473.8 8.5 mul.677
  1482.4 18.8 scatter_custom_fusion.3
  1506.1 310.5 %all_to_all.21 = bf16[32,288,768]{2,1,0:T(8,128)(2,1)} all-to-all(bf16[32,288,768]{2,1,0:T(8,128)(2,1)S(1)} %bitcast.253), channel_id=1, replica_groups=mesh['fsdp'=32] {'fsdp'}, dimensions={0} | all-to-all | bytes 28311552 | tf_op jit(solution)/shard_map/all_to_all | solution.py:321
  1816.6 33.4 fusion.57
  1850.0 17.8 convolution_convert_fusion
  1872.0 18.3 multiply_reduce_fusion.2
  1891.6 294.3 %all-to-all-done.3 = bf16[32,288,768]{2,1,0:T(8,128)(2,1)} async-done(((bf16[32,288,768]{2,1,0:T(8,128)(2,1)}), bf16[32,288,768]{2,1,0:T(8,128)(2,1)}, u32[]{:S(2)}, u32[]{:S(2)}) %all-to-all-start.3) | async-done | bytes 14155808 | tf_op jit(solution)/shard_map/all_to_all | solution.py:339
  2197.2 13.7 gather_fusion.5
  2210.8 8.6 reshape.558
  2219.5 11.9 reduce_sum.370
  2247.5 19.7 multiply_reduce_fusion.1
  2267.2 16.5 multiply_convert_fusion.2
  2296.3 10.5 fusion.66
  2306.8 16.4 multiply_reduce_fusion
  2323.2 10.9 add_convert_fusion
  2337.0 16.9 multiply_convert_fusion.1
  2391.6 131.2 %scatter_fusion = f32[32000,768]{1,0:T(8,128)} fusion(f32[32000,768]{1,0:T(8,128)} %bitcast.29, s32[1024]{0:T(1024)S(1)} %copy-done.95, f32[1024,768]{1,0:T(8,128)S(1)} %copy.158), kind=kCustom, calls=%fused_computation.10 | custom fusion | flops 786432 | bytes 9441280 | tf_op jit(solution)/shard_map/scatter-add | solution.py:423
  2525.0 22.9 multiply_reduce_fusion.12
  2547.9 30.0 multiply_reduce_fusion.11
  2577.9 21.5 fusion.181
  2599.5 16.4 fusion.187
  2616.0 37.4 %all-reduce.7 = (f32[6144]{0:T(1024)S(1)}, f32[2688]{0:T(1024)S(1)}) all-reduce(f32[6144]{0:T(1024)S(1)} %reshape.509, f32[2688]{0:T(1024)S(1)} %pad_maximum_fusion.5), channel_id=4, replica_groups=mesh['fsdp'=32] {'fsdp'}, use_global_device_ids=true, to_apply=%region_48.49.clone | all-reduce | flops 8832 | bytes 70656
  2656.5 672.4 %reduce-scatter.7.cloned.1.call-done = f32[1000,768]{1,0:T(8,128)} async-done(((f32[32000,768]{1,0:T(8,128)}), f32[1000,768]{1,0:T(8,128)}) %reduce-scatter.7.cloned.1.call-update) | async-done | bytes 3072016
  3336.6 39.4 %psum.7 = f32[]{:T(128)} all-reduce(f32[]{:T(128)S(6)} %add.517), channel_id=1, replica_groups=mesh['fsdp'=32] {'fsdp'}, use_global_device_ids=true, to_apply=%region_57.58 | all-reduce | flops 1 | bytes 8 | tf_op jit(solution)/shard_map/psum | solution.py:438
  3378.1 10.9 add_multiply_fusion.1
  (629 shorter events, 448.2 us)
Async XLA Ops:
  7.2 277.4 %all-gather.3.cloned.1.call-start = ((), (), s32[]{:S(2)}) async-start(), calls=%async_computation.6 | async-start | bytes 50688000 | tf_op jit(solution)/shard_map/all_gather | solution.py:129
  7.9 341.4 %all-gather.5.cloned.1.call-start = ((), (), s32[]{:S(2)}) async-start(), calls=%async_computation.7 | async-start | bytes 4866048 | tf_op jit(solution)/shard_map/all_gather | solution.py:130
  95.3 298.7 %copy-start.76 = (f32[768]{0:T(1024)}, f32[768]{0:T(1024)S(1)}, u32[]{:S(2)}) copy-start(f32[768]{0:T(1024)S(1)} %get-tuple-element.266) | copy-start | bytes 9220
  102.1 15.0 copy-start.39
  102.1 15.0 copy-start.37
  305.0 151.7 %copy-start.10 = (bf16[1024,768]{0,1:T(8,128)(2,1)}, bf16[1024,768]{0,1:T(8,128)(2,1)S(1)}, u32[]{:S(2)}) copy-start(bf16[1024,768]{0,1:T(8,128)(2,1)S(1)} %copy.137) | copy-start | bytes 4718596
  306.7 87.3 %copy-start.88 = (f32[1024]{0:T(1024)}, f32[1024]{0:T(1024)S(1)}, u32[]{:S(2)}) copy-start(f32[1024]{0:T(1024)S(1)} %get-tuple-element.268) | copy-start | bytes 12292
  352.5 54.1 %copy-start.17 = (bf16[512,768]{0,1:T(8,128)(2,1)}, bf16[512,768]{0,1:T(8,128)(2,1)S(1)}, u32[]{:S(2)}) copy-start(bf16[512,768]{0,1:T(8,128)(2,1)S(1)} %get-tuple-element.263) | copy-start | bytes 2359300
  354.0 52.6 %copy-start.13 = (bf16[1024,768]{0,1:T(8,128)(2,1)}, bf16[1024,768]{0,1:T(8,128)(2,1)S(1)}, u32[]{:S(2)}) copy-start(bf16[1024,768]{0,1:T(8,128)(2,1)S(1)} %convolution_convert_fusion.3) | copy-start | bytes 4718596
  383.1 12.5 copy-start.49
  395.6 50.7 %copy-start.22 = (bf16[1024,768]{0,1:T(8,128)(2,1)}, bf16[1024,768]{0,1:T(8,128)(2,1)S(1)}, u32[]{:S(2)}) copy-start(bf16[1024,768]{0,1:T(8,128)(2,1)S(1)} %convolution_convert_fusion.5) | copy-start | bytes 4718596
  406.5 50.2 %copy-start.107 = (bf16[12,64,512]{2,1,0:T(8,128)(2,1)}, bf16[12,64,512]{2,1,0:T(8,128)(2,1)S(1)}, u32[]{:S(2)}) copy-start(bf16[12,64,512]{2,1,0:T(8,128)(2,1)S(1)} %fusion.170) | copy-start | bytes 2359300
  462.1 388.2 %copy-start.8 = (bf16[1024,768]{0,1:T(8,128)(2,1)}, bf16[1024,768]{0,1:T(8,128)(2,1)S(1)}, u32[]{:S(2)}) copy-start(bf16[1024,768]{0,1:T(8,128)(2,1)S(1)} %multiply_convert_fusion.4) | copy-start | bytes 4718596
  490.0 311.0 %copy-start.46 = (bf16[1,768,768]{2,1,0:T(8,128)(2,1)S(1)}, bf16[1,768,768]{2,1,0:T(8,128)(2,1)}, u32[]{:S(2)}) copy-start(bf16[1,768,768]{2,1,0:T(8,128)(2,1)} %param.42) | copy-start | bytes 3538948
  801.0 20.4 copy-start.44
  844.4 318.3 %all-to-all-start.1 = ((bf16[32,288,768]{2,1,0:T(8,128)(2,1)}), bf16[32,288,768]{2,1,0:T(8,128)(2,1)}, u32[]{:S(2)}, u32[]{:S(2)}) async-start(bf16[32,288,768]{2,1,0:T(8,128)(2,1)} %bitcast.266), calls=%async_computation.1 | async-start | bytes 28311552 | tf_op jit(solution)/shard_map/all_to_all | solution.py:220
  848.9 321.6 %copy-start.41 = (bf16[768,8]{1,0:T(8,128)(2,1)}, bf16[768,8]{1,0:T(8,128)(2,1)S(1)}, u32[]{:S(2)}) copy-start(bf16[768,8]{1,0:T(8,128)(2,1)S(1)} %reshape.491) | copy-start | bytes 36868
  850.3 323.6 %copy-start.2 = (s32[2048]{0:T(1024)}, s32[2048]{0:T(1024)S(1)}, u32[]{:S(2)}) copy-start(s32[2048]{0:T(1024)S(1)} %broadcast_clamp_fusion) | copy-start | bytes 24580
  850.7 319.8 %copy-start.53 = (f32[1024,2]{0,1:T(2,128)}, f32[1024,2]{0,1:T(2,128)S(1)}, u32[]{:S(2)}) copy-start(f32[1024,2]{0,1:T(2,128)S(1)} %select_reduce_fusion.2) | copy-start | bytes 24580
  850.7 319.8 %copy-start.67 = (f32[1024]{0:T(1024)}, f32[1024]{0:T(1024)S(1)}, u32[]{:S(2)}) copy-start(f32[1024]{0:T(1024)S(1)} %reduce_max.38) | copy-start | bytes 12292
  850.8 319.8 %copy-start.74 = (f32[1024]{0:T(1024)}, f32[1024]{0:T(1024)S(1)}, u32[]{:S(2)}) copy-start(f32[1024]{0:T(1024)S(1)} %fusion.220) | copy-start | bytes 12292
  851.0 319.5 %copy-start.27 = (f32[1024,2]{1,0:T(8,128)}, f32[1024,2]{1,0:T(8,128)S(1)}, u32[]{:S(2)}) copy-start(f32[1024,2]{1,0:T(8,128)S(1)} %copy.141) | copy-start | bytes 24580
  1506.1 310.5 %copy-start.45 = (bf16[1,768,768]{2,1,0:T(8,128)(2,1)S(1)}, bf16[1,768,768]{2,1,0:T(8,128)(2,1)}, u32[]{:S(2)}) copy-start(bf16[1,768,768]{2,1,0:T(8,128)(2,1)} %param.43) | copy-start | bytes 3538948
  1867.8 318.1 %all-to-all-start.3 = ((bf16[32,288,768]{2,1,0:T(8,128)(2,1)}), bf16[32,288,768]{2,1,0:T(8,128)(2,1)}, u32[]{:S(2)}, u32[]{:S(2)}) async-start(bf16[32,288,768]{2,1,0:T(8,128)(2,1)} %bitcast.267), calls=%async_computation.3 | async-start | bytes 28311552 | tf_op jit(solution)/shard_map/all_to_all | solution.py:339
  1871.8 783.0 %reduce-scatter.5.cloned.1.call-start = ((), (), s32[]{:S(2)}) async-start(), calls=%async_computation.8 | async-start | bytes 9732096 | tf_op jit(solution)/shard_map/reduce_scatter | solution.py:426
  1871.9 19.5 copy-start.54
  1871.9 19.5 copy-start.68
  1871.9 19.5 copy-start.75
  1872.0 19.6 copy-start.65
  1891.6 343.7 %copy-start.58 = (bf16[1024,8]{0,1:T(8,128)(2,1)}, bf16[1024,8]{0,1:T(8,128)(2,1)S(1)}, u32[]{:S(2)}) copy-start(bf16[1024,8]{0,1:T(8,128)(2,1)S(1)} %select_reduce_fusion.1) | copy-start | bytes 49156
  2246.9 20.4 copy-start.20
  2376.3 952.5 %reduce-scatter.7.cloned.1.call-start = ((), (), s32[]{:S(2)}) async-start(), calls=%async_computation.9 | async-start | bytes 101376000
  2525.0 74.5 %slice-start = ((s8[12582912]{0:T(1024)(128)(4,1)}), s8[4194304]{0:T(1024)(128)(4,1)S(1)}, s32[]{:S(2)}) async-start(s8[12582912]{0:T(1024)(128)(4,1)} %bitcast.250), calls=%async_computation.10 | async-start | bytes 8388608
  2547.9 51.5 %slice-start.1 = ((s8[12582912]{0:T(1024)(128)(4,1)}), s8[4194304]{0:T(1024)(128)(4,1)S(1)}, s32[]{:S(2)}) async-start(s8[12582912]{0:T(1024)(128)(4,1)} %bitcast.250), calls=%async_computation.11 | async-start | bytes 8388608
  2547.9 51.5 %slice-start.2 = ((s8[12582912]{0:T(1024)(128)(4,1)}), s8[4194304]{0:T(1024)(128)(4,1)S(1)}, s32[]{:S(2)}) async-start(s8[12582912]{0:T(1024)(128)(4,1)} %bitcast.250), calls=%async_computation.12 | async-start | bytes 8388608
  2577.9 21.6 copy-start.38
  2599.5 16.6 copy-start.90
  2599.5 16.5 copy-start.91
  2615.9 760.9 %copy-start.98 = (f32[192]{0:T(256)S(1)}, f32[192]{0:T(256)}, u32[]{:S(2)}) copy-start(f32[192]{0:T(256)} %param.49) | copy-start | bytes 2308
  2615.9 760.9 %copy-start.99 = (f32[192]{0:T(256)S(1)}, f32[192]{0:T(256)}, u32[]{:S(2)}) copy-start(f32[192]{0:T(256)} %param.48) | copy-start | bytes 2308
  2615.9 760.9 %copy-start.104 = (bf16[192]{0:T(256)(128)(2,1)S(1)}, bf16[192]{0:T(256)(128)(2,1)}, u32[]{:S(2)}) copy-start(bf16[192]{0:T(256)(128)(2,1)} %param.40) | copy-start | bytes 1156
  2615.9 761.6 %copy-start.100 = (bf16[84]{0:T(256)(128)(2,1)S(1)}, bf16[84]{0:T(256)(128)(2,1)}, u32[]{:S(2)}) copy-start(bf16[84]{0:T(256)(128)(2,1)} %param.41) | copy-start | bytes 508
  2615.9 761.5 %copy-start.101 = (f32[84]{0:T(128)S(1)}, f32[84]{0:T(128)}, u32[]{:S(2)}) copy-start(f32[84]{0:T(128)} %param.51) | copy-start | bytes 1012
  2615.9 761.5 %copy-start.102 = (f32[84]{0:T(128)S(1)}, f32[84]{0:T(128)}, u32[]{:S(2)}) copy-start(f32[84]{0:T(128)} %param.50) | copy-start | bytes 1012
  2615.9 762.1 %copy-start.34 = (f32[1,768,768]{2,1,0:T(8,128)S(1)}, f32[1,768,768]{2,1,0:T(8,128)}, u32[]{:S(2)}) copy-start(f32[1,768,768]{2,1,0:T(8,128)} %param.55) | copy-start | bytes 7077892
  3378.1 12.0 copy-start.16
  3378.1 12.9 copy-start.32
  3378.1 13.8 copy-start.33
  (108 other events, 441.8 us)
Sparse Core Ops, SparseCore 0:
  10.9 273.6 all-gather.2
  287.5 61.8 all-gather.4
  2376.4 131.3 reduce-scatter.4
  2522.9 805.8 reduce-scatter.6
where the time goes:
time: 3420 us; the launch traced here: 3410 us
  waiting for transfers between devices  1470 us (43%)
  blocking collectives  743 us (22%)
  matrix products  570 us (17%)
  other arithmetic  374 us (11%)
  local copies, waits for them, and re-layouts  212 us (6%)
    unnamed x5, waiting for transfers between devices  674 us
    all_to_all x1, blocking collectives, local(): lax.all_to_all(outgoing, 'fsdp', split_axis=0, concat_axis=0, tiled=True)  311 us
    all_to_all x1, waiting for transfers between devices, local(): lax.all_to_all(partial_out.reshape(devices, capacity, model_width), 'fsdp...  311 us
    all_to_all x1, blocking collectives, local(): lax.all_to_all(grad_slots, 'fsdp', split_axis=0, concat_axis=0, tiled=True)  311 us
    all_to_all x1, waiting for transfers between devices, local(): lax.all_to_all(grad_rows.reshape(devices, capacity, model_width), 'fsdp',...  294 us
    all_gather x1, waiting for transfers between devices, local(): lax.all_gather(embedding, 'fsdp', axis=0, tiled=True)  152 us
    scatter-add x1, other arithmetic, local(): table_parts.reshape(vocab_rows, model_width).at[token_ids]  131 us
    unnamed x2, blocking collectives  82.3 us
  transfers between devices with their start and end apart: 6, of which 5 were waited for; matrix products, arithmetic and copies ran while one was open for 11% of the time, Pallas kernels for 0%

commit v1 on v0

v1 whole, which is shorter than its diff:
```python
import functools
import math

import jax
import jax.numpy as jnp
from jax import lax
from jax.experimental import pallas as pl
from jax.experimental.pallas import tpu as pltpu
from jax.sharding import PartitionSpec as P

HEADS = 12
NB = 32
SPLIT = 4
STEP = 10
ASK = 48
BLOCK = 4
WINDOW = 3
NT = (((1,), (1,)), ((), ()))
TN = (((0,), (0,)), ((), ()))
MESH = pl.DeviceIdType.MESH


bucket_marks = (16, 23, 32, 45, 64, 91, 128, 181, 256, 362, 512, 724, 1024, 1448, 2048, 2896)
learn_rate = 0.02
weight_decay = 0.1
clip_base = 8.0


def rms_norm(values, gains):
    return values * lax.rsqrt(jnp.mean(values * values, axis=-1, keepdims=True) + 1e-06) * gains


def bucket_of(distance):
    distance = jnp.maximum(distance, 0)
    bucket = jnp.minimum(distance, 15)
    for border in bucket_marks:
        bucket = bucket + (distance >= border).astype(jnp.int32)
    return bucket


def tree_layout(segments, parents):
    segment_count = parents.shape[0]
    identity_rows = jnp.eye(segment_count, dtype=jnp.float32)
    parent_rows = (parents[:, None] == jnp.arange(segment_count, dtype=jnp.int32)[None, :]).astype(
        jnp.float32
    )
    ancestry = jnp.minimum(identity_rows + parent_rows, 1.0)
    reached = 1
    while reached < segment_count - 1:
        ancestry = jnp.minimum(jnp.dot(ancestry, ancestry), 1.0)
        reached = 2 * reached
    member = (segments[:, None] == jnp.arange(segment_count, dtype=jnp.int32)[None, :]).astype(
        jnp.int32
    )
    lengths = jnp.sum(member, axis=0)
    starts = jnp.cumsum(lengths) - lengths
    before = jnp.sum((ancestry - identity_rows).astype(jnp.int32) * lengths[None, :], axis=1)
    tree_depth = jnp.sum(member * (before - starts)[None, :], axis=1) + jnp.arange(
        segments.shape[0], dtype=jnp.int32
    )
    reach_rows = jnp.dot(member.astype(jnp.float32), ancestry)
    linked = jnp.dot(reach_rows, member.astype(jnp.float32).T) > 0.5
    order = jnp.arange(segments.shape[0], dtype=jnp.int32)
    allowed = linked & (order[None, :] <= order[:, None])
    buckets = jnp.where(allowed, bucket_of(tree_depth[:, None] - tree_depth[None, :]), NB)
    prefix = (tree_depth[:, None] <= order[None, :]).astype(jnp.bfloat16)
    begins = jnp.asarray(tuple(range(16)) + bucket_marks, jnp.int32)
    edges = jnp.pad(
        tree_depth[:, None] - begins[None, :], ((0, 0), (0, 128 - NB)), constant_values=-1
    )
    return (buckets.astype(jnp.int32), prefix, edges)


def swap_kernel(peers, stride, src, dst, send_sems, recv_sems, own_sem):
    me = lax.axis_index("fsdp")
    spot, lane = me // stride, lax.rem(me, stride)
    barrier = pltpu.get_barrier_semaphore()

    def greet(step, carry):
        other = lax.rem(spot + step, peers) * stride + lane
        pl.semaphore_signal(barrier, inc=1, device_id=(other,), device_id_type=MESH)
        return carry

    lax.fori_loop(1, peers, greet, 0)
    pl.semaphore_wait(barrier, peers - 1)

    def transfer(step):
        other = lax.rem(spot + step, peers)
        return pltpu.make_async_remote_copy(
            src_ref=src.at[other],
            dst_ref=dst.at[spot],
            send_sem=send_sems.at[step],
            recv_sem=recv_sems.at[step],
            device_id=(other * stride + lane,),
            device_id_type=MESH,
        )

    def begin(step, carry):
        transfer(step).start()
        return carry

    lax.fori_loop(1, peers, begin, 0)
    own = pltpu.make_async_copy(src.at[spot], dst.at[spot], own_sem)
    own.start()

    def finish(step, carry):
        origin = lax.rem(spot + peers - step, peers)
        transfer(step).wait_send()
        pltpu.make_async_remote_copy(
            src_ref=src.at[origin],
            dst_ref=dst.at[origin],
            send_sem=send_sems.at[step],
            recv_sem=recv_sems.at[step],
            device_id=(origin * stride + lane,),
            device_id_type=MESH,
        ).wait_recv()
        return carry

    lax.fori_loop(1, peers, finish, 0)
    own.wait()


def swap_blocks(blocks, stride, call_id):
    peers = blocks.shape[0]
    return pl.pallas_call(
        functools.partial(swap_kernel, peers, stride),
        out_shape=jax.ShapeDtypeStruct(blocks.shape, blocks.dtype),
        in_specs=[pl.BlockSpec(memory_space=pl.ANY)],
        out_specs=pl.BlockSpec(memory_space=pl.ANY),
        scratch_shapes=[
            pltpu.SemaphoreType.DMA((peers,)),
            pltpu.SemaphoreType.DMA((peers,)),
            pltpu.SemaphoreType.DMA,
        ],
        compiler_params=pltpu.CompilerParams(collective_id=call_id, has_side_effects=True),
    )(blocks)


def around(step, size, at):
    return lax.rem(at + step, size)


def meet(others):
    barrier = pltpu.get_barrier_semaphore()
    for other in others:
        pl.semaphore_signal(barrier, inc=1, device_id=(other,), device_id_type=MESH)
    pl.semaphore_wait(barrier, len(others))


def chip_place(chips):
    me = lax.axis_index("fsdp")
    core = lax.rem(me, 2)
    chip = me // 2
    layers = chips // BLOCK
    layer, col = chip // BLOCK, lax.rem(chip, BLOCK)

    def device(other_layer, other_col):
        return (other_layer * BLOCK + other_col) * 2 + core

    others = [device(around(step, layers, layer), col) for step in range(1, layers)]
    others += [device(layer, around(turn, BLOCK, col)) for turn in range(1, BLOCK)]
    return layers, layer, col, device, others


def spread_kernel(chips, src, dst, layer_send, layer_recv, col_send, col_recv, own_sem):
    layers, layer, col, device, others = chip_place(chips)
    meet(others)
    chip = layer * BLOCK + col

    def to_layer(step, source, at):
        return pltpu.make_async_remote_copy(
            src_ref=source,
            dst_ref=dst.at[at],
            send_sem=layer_send.at[step],
            recv_sem=layer_recv.at[step],
            device_id=(device(around(step, layers, layer), col),),
            device_id_type=MESH,
        )

    def to_col(step, turn, source, at):
        return pltpu.make_async_remote_copy(
            src_ref=source,
            dst_ref=dst.at[at],
            send_sem=col_send.at[step, turn],
            recv_sem=col_recv.at[step, turn],
            device_id=(device(layer, around(turn, BLOCK, col)),),
            device_id_type=MESH,
        )

    for step in range(1, layers):
        to_layer(step, src, chip).start()
    for turn in range(1, BLOCK):
        to_col(0, turn, src, chip).start()
    own = pltpu.make_async_copy(src, dst.at[chip], own_sem)
    own.start()
    for step in range(1, layers):
        origin = around(layers - step, layers, layer) * BLOCK + col
        to_layer(step, src, origin).wait_recv()
        for turn in range(1, BLOCK):
            to_col(step, turn, dst.at[origin], origin).start()
    for step in range(layers):
        for turn in range(1, BLOCK):
            at = around(layers - step, layers, layer) * BLOCK + around(BLOCK - turn, BLOCK, col)
            to_col(step, turn, dst.at[at], at).wait_recv()
    for step in range(1, layers):
        to_layer(step, src, chip).wait_send()
    for step in range(layers):
        for turn in range(1, BLOCK):
            to_col(step, turn, src, chip).wait_send()
    own.wait()


def spread_rows(block, chips, call_id):
    layers = chips // BLOCK
    return pl.pallas_call(
        functools.partial(spread_kernel, chips),
        out_shape=jax.ShapeDtypeStruct((chips, *block.shape), block.dtype),
        in_specs=[pl.BlockSpec(memory_space=pl.ANY)],
        out_specs=pl.BlockSpec(memory_space=pl.ANY),
        scratch_shapes=[
            pltpu.SemaphoreType.DMA((layers,)),
            pltpu.SemaphoreType.DMA((layers,)),
            pltpu.SemaphoreType.DMA((layers, BLOCK)),
            pltpu.SemaphoreType.DMA((layers, BLOCK)),
            pltpu.SemaphoreType.DMA,
        ],
        compiler_params=pltpu.CompilerParams(collective_id=call_id, has_side_effects=True),
    )(block)


def gather_sum_kernel(
    chips, src, out, col_in, layer_out, layer_in, layer_send, layer_recv, col_send, col_recv
):
    layers, layer, col, device, others = chip_place(chips)
    meet(others)

    def to_col(step, turn):
        far = around(step, layers, layer)
        return pltpu.make_async_remote_copy(
            src_ref=src.at[far * BLOCK + around(turn, BLOCK, col)],
            dst_ref=col_in.at[step, turn],
            send_sem=col_send.at[step, turn],
            recv_sem=col_recv.at[step, turn],
            device_id=(device(layer, around(turn, BLOCK, col)),),
            device_id_type=MESH,
        )

    def to_layer(step):
        return pltpu.make_async_remote_copy(
            src_ref=layer_out.at[step],
            dst_ref=layer_in.at[step],
            send_sem=layer_send.at[step],
            recv_sem=layer_recv.at[step],
            device_id=(device(around(step, layers, layer), col),),
            device_id_type=MESH,
        )

    def block_sum(step):
        for turn in range(1, BLOCK):
            to_col(step, turn).wait_recv()
        total = src[around(step, layers, layer) * BLOCK + col].astype(jnp.float32)
        for turn in range(1, BLOCK):
            total = total + col_in[step, turn].astype(jnp.float32)
        return total

    steps = list(range(1, layers)) + [0]
    for step in steps:
        for turn in range(1, BLOCK):
            to_col(step, turn).start()
    for step in range(1, layers):
        layer_out[step] = block_sum(step).astype(jnp.bfloat16)
        to_layer(step).start()
    total = block_sum(0)
    for step in range(1, layers):
        to_layer(step).wait_recv()
        total = total + layer_in[step].astype(jnp.float32)
    out[...] = total
    for step in range(1, layers):
        to_layer(step).wait_send()
    for step in range(layers):
        for turn in range(1, BLOCK):
            to_col(step, turn).wait_send()


def gather_sum(blocks, call_id):
    chips, rows, width = blocks.shape
    layers = chips // BLOCK
    return pl.pallas_call(
        functools.partial(gather_sum_kernel, chips),
        out_shape=jax.ShapeDtypeStruct((rows, width), jnp.float32),
        in_specs=[pl.BlockSpec(memory_space=pltpu.VMEM)],
        out_specs=pl.BlockSpec(memory_space=pltpu.VMEM),
        scratch_shapes=[
            pltpu.VMEM((layers, BLOCK, rows, width), jnp.bfloat16),
            pltpu.VMEM((layers, rows, width), jnp.bfloat16),
            pltpu.VMEM((layers, rows, width), jnp.bfloat16),
            pltpu.SemaphoreType.DMA((layers,)),
            pltpu.SemaphoreType.DMA((layers,)),
            pltpu.SemaphoreType.DMA((layers, BLOCK)),
            pltpu.SemaphoreType.DMA((layers, BLOCK)),
        ],
        compiler_params=pltpu.CompilerParams(
            collective_id=call_id, has_side_effects=True, vmem_limit_bytes=56 * 1024 * 1024
        ),
    )(blocks)


def gelu_parts(values):
    root = math.sqrt(2.0 / math.pi)
    squared = values * values
    bend = jnp.tanh(root * (values + 0.044715 * (squared * values)))
    half = 0.5 * (1.0 + bend)
    slope = half + 0.5 * values * (1.0 - bend * bend) * (root * (1.0 + 0.134145 * squared))
    return values * half, slope


def trade_copies(peers, src, landed, done, returned, sems):
    me = lax.axis_index("fsdp")
    spot, lane = me // SPLIT, lax.rem(me, SPLIT)
    go_send, go_recv, back_send, back_recv = sems

    def device(other):
        return (other * SPLIT + lane,)

    def ahead(step):
        return lax.rem(spot + step, peers)

    def behind(step):
        return lax.rem(spot + peers - step, peers)

    def go(step, at):
        return pltpu.make_async_remote_copy(
            src_ref=src.at[ahead(step)],
            dst_ref=landed.at[at],
            send_sem=go_send.at[step],
            recv_sem=go_recv.at[step],
            device_id=device(ahead(step)),
            device_id_type=MESH,
        )

    def back(step, source, at):
        return pltpu.make_async_remote_copy(
            src_ref=done.at[source],
            dst_ref=returned.at[at],
            send_sem=back_send.at[step],
            recv_sem=back_recv.at[step],
            device_id=device(behind(step)),
            device_id_type=MESH,
        )

    barrier = pltpu.get_barrier_semaphore()

    def greet(step, carry):
        pl.semaphore_signal(barrier, inc=1, device_id=device(ahead(step)), device_id_type=MESH)
        return carry

    lax.fori_loop(1, peers, greet, 0)
    pl.semaphore_wait(barrier, peers - 1)
    return spot, behind, ahead, go, back


def trade_loop(peers, copies, work, own_copies):
    spot, behind, ahead, go, back = copies
    window = min(WINDOW, peers - 1)

    def begin(step, carry):
        go(step, spot).start()
        return carry

    lax.fori_loop(1, window + 1, begin, 0)
    own_in, own_out = own_copies
    own_in.start()
    own_in.wait()
    work(spot)
    own_out.start()

    def visit(step, carry):
        origin = behind(step)
        go(step, origin).wait_recv()

        @pl.when(step + window < peers)
        def _():
            go(step + window, spot).start()

        work(origin)
        back(step, origin, spot).start()
        return carry

    lax.fori_loop(1, peers, visit, 0)

    def finish(step, carry):
        go(step, spot).wait_send()
        back(step, behind(step), spot).wait_send()
        back(step, spot, ahead(step)).wait_recv()
        return carry

    lax.fori_loop(1, peers, finish, 0)
    own_out.wait()


def experts_kernel(peers, src, inward, outward, landed, returned, done, *sems):
    copies = trade_copies(peers, src, landed, done, returned, sems[:4])
    spot = copies[0]
    f32 = jnp.float32

    def work(at):
        rows = landed[at]
        total = jnp.zeros(rows.shape, f32)
        for quarter in range(SPLIT):
            before = jnp.dot(rows, inward[quarter], preferred_element_type=f32)
            hidden = gelu_parts(before)[0].astype(jnp.bfloat16)
            total = total + jnp.dot(hidden, outward[quarter], preferred_element_type=f32).astype(
                jnp.bfloat16
            ).astype(f32)
        done[at] = total.astype(jnp.bfloat16)

    trade_loop(
        peers,
        copies,
        work,
        (
            pltpu.make_async_copy(src.at[spot], landed.at[spot], sems[4]),
            pltpu.make_async_copy(done.at[spot], returned.at[spot], sems[5]),
        ),
    )


def experts_back_kernel(
    peers, src, rows_ref, inward, outward, returned, inward_grad, outward_grad, landed, done, *sems
):
    copies = trade_copies(peers, src, landed, done, returned, sems[:4])
    spot = copies[0]
    f32 = jnp.float32
    inward_grad[...] = jnp.zeros_like(inward_grad)
    outward_grad[...] = jnp.zeros_like(outward_grad)

    def work(at):
        rows = rows_ref[at]
        grads = landed[at]
        total = jnp.zeros(rows.shape, f32)
        for quarter in range(SPLIT):
            before = jnp.dot(rows, inward[quarter], preferred_element_type=f32)
            hidden, slope = gelu_parts(before)
            grad_hidden = lax.dot_general(grads, outward[quarter], NT, preferred_element_type=f32)
            grad_before = (grad_hidden * slope).astype(jnp.bfloat16)
            total = total + lax.dot_general(
                grad_before, inward[quarter], NT, preferred_element_type=f32
            ).astype(jnp.bfloat16).astype(f32)
            inward_grad[quarter] += lax.dot_general(
                rows, grad_before, TN, preferred_element_type=f32
            )
            outward_grad[quarter] += lax.dot_general(
                hidden.astype(jnp.bfloat16), grads, TN, preferred_element_type=f32
            )
        done[at] = total.astype(jnp.bfloat16)

    trade_loop(
        peers,
        copies,
        work,
        (
            pltpu.make_async_copy(src.at[spot], landed.at[spot], sems[4]),
            pltpu.make_async_copy(done.at[spot], returned.at[spot], sems[5]),
        ),
    )


def trade_call(body, call_id, outgoing, operands, outs, scratch):
    peers = outgoing.shape[0]
    anywhere = pl.BlockSpec(memory_space=pl.ANY)
    near = pl.BlockSpec(memory_space=pltpu.VMEM)
    return pl.pallas_call(
        functools.partial(body, peers),
        out_shape=[shape for shape, _ in outs],
        in_specs=[anywhere] + [near] * len(operands),
        out_specs=[near if inside else anywhere for _, inside in outs],
        scratch_shapes=scratch
        + [pltpu.SemaphoreType.DMA((peers,))] * 4
        + [pltpu.SemaphoreType.DMA] * 2,
        compiler_params=pltpu.CompilerParams(
            collective_id=call_id, has_side_effects=True, vmem_limit_bytes=60 * 1024 * 1024
        ),
    )(outgoing, *operands)


def run_experts(outgoing, inward, outward, call_id):
    same = jax.ShapeDtypeStruct(outgoing.shape, outgoing.dtype)
    return trade_call(
        experts_kernel,
        call_id,
        outgoing,
        (inward, outward),
        [(same, True), (same, False)],
        [pltpu.VMEM(outgoing.shape, outgoing.dtype)],
    )


def run_experts_back(outgoing, rows, inward, outward, call_id):
    same = jax.ShapeDtypeStruct(outgoing.shape, outgoing.dtype)
    wide = jax.ShapeDtypeStruct(inward.shape, jnp.float32)
    block = pltpu.VMEM(outgoing.shape, outgoing.dtype)
    return trade_call(
        experts_back_kernel,
        call_id,
        outgoing,
        (rows, inward, outward),
        [(same, False), (wide, True), (wide, True)],
        [block, block],
    )


def meet_all(devices):
    me = lax.axis_index("fsdp")
    barrier = pltpu.get_barrier_semaphore()

    def greet(step, carry):
        other = lax.rem(me + step, devices)
        pl.semaphore_signal(barrier, inc=1, device_id=(other,), device_id_type=MESH)
        return carry

    lax.fori_loop(1, devices, greet, 0)
    pl.semaphore_wait(barrier, devices - 1)


def swap_parts(devices, src, dst, send_sems, recv_sems, own_sem):
    me = lax.axis_index("fsdp")

    def transfer(step, at):
        other = lax.rem(me + step, devices)
        return pltpu.make_async_remote_copy(
            src_ref=src.at[other],
            dst_ref=dst.at[at],
            send_sem=send_sems.at[step],
            recv_sem=recv_sems.at[step],
            device_id=(other,),
            device_id_type=MESH,
        )

    own = pltpu.make_async_copy(src.at[me], dst.at[me], own_sem)

    def begin():
        def one(step, carry):
            transfer(step, me).start()
            return carry

        lax.fori_loop(1, devices, one, 0)
        own.start()

    def finish():
        def one(step, carry):
            transfer(step, me).wait_send()
            transfer(step, lax.rem(me + devices - step, devices)).wait_recv()
            return carry

        lax.fori_loop(1, devices, one, 0)
        own.wait()

    return begin, finish


def tail_kernel(
    chips,
    token_src,
    small_src,
    src,
    token_dst,
    small_dst,
    out,
    core_in,
    col_out,
    col_in,
    layer_out,
    layer_in,
    core_send,
    core_recv,
    layer_send,
    layer_recv,
    col_send,
    col_recv,
    *swap_sems,
):
    layers, layer, col, device, _ = chip_place(chips)
    me = lax.axis_index("fsdp")
    core = lax.rem(me, 2)
    f32 = jnp.float32
    token_begin, token_finish = swap_parts(2 * chips, token_src, token_dst, *swap_sems[:3])
    small_begin, small_finish = swap_parts(2 * chips, small_src, small_dst, *swap_sems[3:])
    meet_all(2 * chips)

    def place(step, turn):
        return around(step, layers, layer) * BLOCK + around(turn, BLOCK, col)

    def to_core(step, turn):
        return pltpu.make_async_remote_copy(
            src_ref=src.at[place(step, turn), 1 - core],
            dst_ref=core_in.at[step, turn],
            send_sem=core_send.at[step, turn],
            recv_sem=core_recv.at[step, turn],
            device_id=(me + 1 - 2 * core,),
            device_id_type=MESH,
        )

    def to_col(step, turn):
        return pltpu.make_async_remote_copy(
            src_ref=col_out.at[step, turn],
            dst_ref=col_in.at[step, turn],
            send_sem=col_send.at[step, turn],
            recv_sem=col_recv.at[step, turn],
            device_id=(device(layer, around(turn, BLOCK, col)),),
            device_id_type=MESH,
        )

    def to_layer(step):
        return pltpu.make_async_remote_copy(
            src_ref=layer_out.at[step],
            dst_ref=layer_in.at[step],
            send_sem=layer_send.at[step],
            recv_sem=layer_recv.at[step],
            device_id=(device(around(step, layers, layer), col),),
            device_id_type=MESH,
        )

    def chip_sum(step, turn):
        to_core(step, turn).wait_recv()
        return src[place(step, turn), core].astype(f32) + core_in[step, turn].astype(f32)

    def block_sum(step):
        total = chip_sum(step, 0)
        for turn in range(1, BLOCK):
            to_col(step, turn).wait_recv()
            total = total + col_in[step, turn].astype(f32)
        return total

    def step_of(number):
        return lax.rem(number + 1, layers)

    def core_begin(number, carry):
        for turn in range(BLOCK):
            to_core(step_of(number), lax.rem(turn + 1, BLOCK)).start()
        return carry

    def col_begin(number, carry):
        step = step_of(number)
        for turn in range(1, BLOCK):
            col_out[step, turn] = chip_sum(step, turn).astype(jnp.bfloat16)
            to_col(step, turn).start()
        return carry

    def layer_begin(step, carry):
        layer_out[step] = block_sum(step).astype(jnp.bfloat16)
        to_layer(step).start()
        return carry

    lax.fori_loop(0, layers, core_begin, 0)
    small_begin()
    token_begin()
    lax.fori_loop(0, layers, col_begin, 0)
    lax.fori_loop(1, layers, layer_begin, 0)
    out[...] = block_sum(0)

    def layer_finish(step, carry):
        to_layer(step).wait_recv()
        out[...] += layer_in[step].astype(f32)
        to_layer(step).wait_send()
        return carry

    def send_finish(step, carry):
        for turn in range(BLOCK):
            to_core(step, turn).wait_send()
        for turn in range(1, BLOCK):
            to_col(step, turn).wait_send()
        return carry

    lax.fori_loop(1, layers, layer_finish, 0)
    lax.fori_loop(0, layers, send_finish, 0)
    small_finish()
    token_finish()


def tail_exchange(tokens, small, blocks, call_id):
    chips, _, rows, width = blocks.shape
    layers = chips // BLOCK
    devices = 2 * chips
    near = pl.BlockSpec(memory_space=pltpu.VMEM)
    anywhere = pl.BlockSpec(memory_space=pl.ANY)
    grid_block = pltpu.VMEM((layers, BLOCK, rows, width), jnp.bfloat16)
    line_block = pltpu.VMEM((layers, rows, width), jnp.bfloat16)
    return pl.pallas_call(
        functools.partial(tail_kernel, chips),
        out_shape=[
            jax.ShapeDtypeStruct(tokens.shape, tokens.dtype),
            jax.ShapeDtypeStruct(small.shape, small.dtype),
            jax.ShapeDtypeStruct((rows, width), jnp.float32),
        ],
        in_specs=[anywhere, anywhere, near],
        out_specs=[anywhere, anywhere, near],
        scratch_shapes=[grid_block] * 3
        + [line_block] * 2
        + [pltpu.SemaphoreType.DMA((layers, BLOCK))] * 2
        + [pltpu.SemaphoreType.DMA((layers,))] * 2
        + [pltpu.SemaphoreType.DMA((layers, BLOCK))] * 2
        + [
            pltpu.SemaphoreType.DMA((devices,)),
            pltpu.SemaphoreType.DMA((devices,)),
            pltpu.SemaphoreType.DMA,
        ]
        * 2,
        compiler_params=pltpu.CompilerParams(
            collective_id=call_id, has_side_effects=True, vmem_limit_bytes=48 * 1024 * 1024
        ),
    )(tokens, small, blocks)


def head_kernel(
    chips,
    token_src,
    src,
    token_dst,
    dst,
    core_send,
    core_recv,
    layer_send,
    layer_recv,
    col_send,
    col_recv,
    own_sem,
    *swap_sems,
):
    layers, layer, col, device, _ = chip_place(chips)
    me = lax.axis_index("fsdp")
    core = lax.rem(me, 2)
    chip = layer * BLOCK + col
    token_begin, token_finish = swap_parts(2 * chips, token_src, token_dst, *swap_sems)
    meet_all(2 * chips)

    def to_layer(step, at):
        return pltpu.make_async_remote_copy(
            src_ref=src,
            dst_ref=dst.at[at, core],
            send_sem=layer_send.at[step],
            recv_sem=layer_recv.at[step],
            device_id=(device(around(step, layers, layer), col),),
            device_id_type=MESH,
        )

    def to_col(step, turn, source, at):
        return pltpu.make_async_remote_copy(
            src_ref=source,
            dst_ref=dst.at[at, core],
            send_sem=col_send.at[step, turn],
            recv_sem=col_recv.at[step, turn],
            device_id=(device(layer, around(turn, BLOCK, col)),),
            device_id_type=MESH,
        )

    def to_core(step, turn, source, at, side):
        return pltpu.make_async_remote_copy(
            src_ref=source,
            dst_ref=dst.at[at, side],
            send_sem=core_send.at[step, turn],
            recv_sem=core_recv.at[step, turn],
            device_id=(me + 1 - 2 * core,),
            device_id_type=MESH,
        )

    def origin(step, turn):
        return around(layers - step, layers, layer) * BLOCK + around(BLOCK - turn, BLOCK, col)

    def layer_start(step, carry):
        to_layer(step, chip).start()
        return carry

    lax.fori_loop(1, layers, layer_start, 0)
    for turn in range(1, BLOCK):
        to_col(0, turn, src, chip).start()
    to_core(0, 0, src, chip, core).start()
    own = pltpu.make_async_copy(src, dst.at[chip, core], own_sem)
    own.start()
    token_begin()

    def layer_pass(step, carry):
        at = origin(step, 0)
        to_layer(step, at).wait_recv()
        for turn in range(1, BLOCK):
            to_col(step, turn, dst.at[at, core], at).start()
        to_core(step, 0, dst.at[at, core], at, core).start()
        return carry

    lax.fori_loop(1, layers, layer_pass, 0)

    def col_pass(step, carry):
        for turn in range(1, BLOCK):
            at = origin(step, turn)
            to_col(step, turn, dst.at[at, core], at).wait_recv()
            to_core(step, turn, dst.at[at, core], at, core).start()
        return carry

    lax.fori_loop(0, layers, col_pass, 0)

    def layer_done(step, carry):
        to_layer(step, chip).wait_send()
        return carry

    def done(step, carry):
        for turn in range(BLOCK):
            if turn:
                to_col(step, turn, src, chip).wait_send()
            at = origin(step, turn)
            to_core(step, turn, src, at, 1 - core).wait_recv()
            to_core(step, turn, src, at, core).wait_send()
        return carry

    lax.fori_loop(1, layers, layer_done, 0)
    lax.fori_loop(0, layers, done, 0)
    own.wait()
    token_finish()


def head_exchange(tokens, block, call_id):
    devices = tokens.shape[0]
    chips = devices // 2
    layers = chips // BLOCK
    anywhere = pl.BlockSpec(memory_space=pl.ANY)
    return pl.pallas_call(
        functools.partial(head_kernel, chips),
        out_shape=[
            jax.ShapeDtypeStruct(tokens.shape, tokens.dtype),
            jax.ShapeDtypeStruct((chips, 2, *block.shape), block.dtype),
        ],
        in_specs=[anywhere] * 2,
        out_specs=[anywhere] * 2,
        scratch_shapes=[pltpu.SemaphoreType.DMA((layers, BLOCK))] * 2
        + [pltpu.SemaphoreType.DMA((layers,))] * 2
        + [pltpu.SemaphoreType.DMA((layers, BLOCK))] * 2
        + [
            pltpu.SemaphoreType.DMA,
            pltpu.SemaphoreType.DMA((devices,)),
            pltpu.SemaphoreType.DMA((devices,)),
            pltpu.SemaphoreType.DMA,
        ],
        compiler_params=pltpu.CompilerParams(collective_id=call_id, has_side_effects=True),
    )(tokens, block)


def pack_blocks(parts, devices):
    flat = jnp.concatenate(
        [jnp.broadcast_to(part, (devices, part.shape[-1])) for part in parts], axis=1
    )
    rows = -(-flat.shape[1] // 1024) * 8
    flat = jnp.pad(flat, ((0, 0), (0, rows * 128 - flat.shape[1])))
    return flat.reshape(devices, rows, 128)


def take_rows(mask, rows):
    return jnp.dot(mask.astype(jnp.bfloat16), rows, preferred_element_type=jnp.float32)


def take_rows_wide(mask, rows):
    high = lax.reduce_precision(rows, 8, 7)
    both = jnp.concatenate([high, rows - high], axis=1).astype(jnp.bfloat16)
    picked = take_rows(mask, both)
    width = rows.shape[1]
    return picked[:, :width] + picked[:, width:]


def bias_tile(table_row, buckets):
    rows, cols = buckets.shape
    spread = jnp.broadcast_to(table_row, (rows, 128))
    return jnp.concatenate(
        [
            jnp.take_along_axis(
                spread, buckets[:, at : at + 128], axis=1, mode="promise_in_bounds"
            )
            for at in range(0, cols, 128)
        ],
        axis=1,
    )


def attend_kernel(block, length, q_ref, k_ref, v_ref, bucket_ref, table_ref, out_ref, log_ref):
    lower = lax.broadcasted_iota(jnp.int32, (1, 128), 1) < 64
    pair = pl.program_id(0)
    zero = jnp.zeros((), jnp.bfloat16)
    for start in range(0, length, block):
        rows = pl.ds(start, block)
        seen = start + block
        logs = []
        mixed = []
        for half in range(2):
            mine = lower if half == 0 else ~lower
            queries = jnp.where(mine, q_ref[rows, :], zero) * 0.125
            values = jnp.where(mine, v_ref[0:seen, :], zero)
            scores = lax.dot_general(
                queries, k_ref[0:seen, :], NT, preferred_element_type=jnp.float32
            )
            table_row = table_ref[pl.ds(2 * pair + half, 1), :]
            scores = scores + bias_tile(table_row, bucket_ref[rows, 0:seen])
            peak = jnp.max(scores, axis=1, keepdims=True)
            raised = jnp.exp(scores - peak)
            totals = jnp.sum(raised, axis=1, keepdims=True)
            probs = (raised * (1.0 / totals)).astype(jnp.bfloat16)
            mixed.append(jnp.dot(probs, values, preferred_element_type=jnp.float32))
            logs.append(peak + jnp.log(totals))
        out_ref[rows, :] = (mixed[0] + mixed[1]).astype(jnp.bfloat16)
        log_ref[0, rows, :] = jnp.where(lower, logs[0], logs[1])


def attend(queries, keys, values, buckets, table, block):
    length, width = queries.shape
    cols = pl.BlockSpec((length, 128), lambda pair: (0, pair))
    return pl.pallas_call(
        functools.partial(attend_kernel, block, length),
        grid=(width // 128,),
        in_specs=[
            cols,
            cols,
            cols,
            pl.BlockSpec(buckets.shape, lambda pair: (0, 0)),
            pl.BlockSpec(table.shape, lambda pair: (0, 0)),
        ],
        out_specs=[cols, pl.BlockSpec((1, length, 128), lambda pair: (pair, 0, 0))],
        out_shape=[
            jax.ShapeDtypeStruct((length, width), jnp.bfloat16),
            jax.ShapeDtypeStruct((width // 128, length, 128), jnp.float32),
        ],
        compiler_params=pltpu.CompilerParams(vmem_limit_bytes=40 * 1024 * 1024),
    )(queries, keys, values, buckets, table)


def attend_back_kernel(
    block,
    length,
    q_ref,
    k_ref,
    v_ref,
    g_ref,
    log_ref,
    bucket_ref,
    table_ref,
    prefix_ref,
    edge_ref,
    dq_ref,
    dk_ref,
    dv_ref,
    edge_sum_ref,
    dk_acc,
    dv_acc,
):
    lower = lax.broadcasted_iota(jnp.int32, (1, 128), 1) < 64
    pair = pl.program_id(0)
    zero = jnp.zeros((), jnp.bfloat16)
    f32 = jnp.float32
    dk_acc[...] = jnp.zeros_like(dk_acc)
    dv_acc[...] = jnp.zeros_like(dv_acc)
    edge_sums = [jnp.zeros((8, 128), f32)] * 2
    for start in range(0, length, block):
        rows = pl.ds(start, block)
        seen = start + block
        edges = edge_ref[rows, :]
        lane_at = edges & 127
        dq_parts = []
        for half in range(2):
            mine = lower if half == 0 else ~lower
            queries = jnp.where(mine, q_ref[rows, :], zero) * 0.125
            grads = jnp.where(mine, g_ref[rows, :], zero)
            keys = jnp.where(mine, k_ref[0:seen, :], zero)
            scores = lax.dot_general(queries, keys, NT, preferred_element_type=f32)
            table_row = table_ref[pl.ds(2 * pair + half, 1), :]
            scores = scores + bias_tile(table_row, bucket_ref[rows, 0:seen])
            probs = jnp.exp(scores - log_ref[0, rows, 64 * half : 64 * half + 1])
            grad_probs = lax.dot_general(
                grads, v_ref[0:seen, :], NT, preferred_element_type=f32
            )
            inner_sum = jnp.sum(probs * grad_probs, axis=1, keepdims=True)
            grad_scores = (probs * (grad_probs - inner_sum)).astype(jnp.bfloat16)
            dq_parts.append(jnp.dot(grad_scores, keys, preferred_element_type=f32))
            dk_acc[0:seen, :] += lax.dot_general(
                grad_scores, queries, TN, preferred_element_type=f32
            )
            dv_acc[0:seen, :] += lax.dot_general(
                probs.astype(jnp.bfloat16), grads, TN, preferred_element_type=f32
            )
            upto = jnp.dot(grad_scores, prefix_ref[0:seen, 0:seen], preferred_element_type=f32)
            for at in range(0, seen, 128):
                read = jnp.take_along_axis(
                    upto[:, at : at + 128], lane_at, axis=1, mode="promise_in_bounds"
                )
                read = jnp.where((edges >= at) & (edges < at + 128), read, 0.0)
                edge_sums[half] = edge_sums[half] + jnp.sum(
                    read.reshape(block // 8, 8, 128), axis=0
                )
        dq_ref[rows, :] = ((dq_parts[0] + dq_parts[1]) * 0.125).astype(jnp.bfloat16)
    dk_ref[...] = dk_acc[...].astype(jnp.bfloat16)
    dv_ref[...] = dv_acc[...].astype(jnp.bfloat16)
    edge_sum_ref[0] = edge_sums[0]
    edge_sum_ref[1] = edge_sums[1]


def attend_back(queries, keys, values, grads, logs, buckets, table, prefix, edges, block):
    length, width = queries.shape
    cols = pl.BlockSpec((length, 128), lambda pair: (0, pair))
    low = jax.ShapeDtypeStruct((length, width), jnp.bfloat16)
    return pl.pallas_call(
        functools.partial(attend_back_kernel, block, length),
        grid=(width // 128,),
        in_specs=[
            cols,
            cols,
            cols,
            cols,
            pl.BlockSpec((1, length, 128), lambda pair: (pair, 0, 0)),
            pl.BlockSpec(buckets.shape, lambda pair: (0, 0)),
            pl.BlockSpec(table.shape, lambda pair: (0, 0)),
            pl.BlockSpec(prefix.shape, lambda pair: (0, 0)),
            pl.BlockSpec(edges.shape, lambda pair: (0, 0)),
        ],
        out_specs=[cols, cols, cols, pl.BlockSpec((2, 8, 128), lambda pair: (pair, 0, 0))],
        out_shape=[low, low, low, jax.ShapeDtypeStruct((width // 64, 8, 128), jnp.float32)],
        scratch_shapes=[pltpu.VMEM((length, 128), jnp.float32)] * 2,
        compiler_params=pltpu.CompilerParams(vmem_limit_bytes=48 * 1024 * 1024),
    )(queries, keys, values, grads, logs, buckets, table, prefix, edges)


def adam_step(weight, moment, square, gradient, factor):
    clipped = gradient * factor
    moment_next = 0.9 * moment + 0.1 * clipped
    square_next = 0.95 * square + 0.05 * clipped * clipped
    corrected_moment = moment_next / (1.0 - 0.9**STEP)
    corrected_square = square_next / (1.0 - 0.95**STEP)
    update = -learn_rate * (
        corrected_moment / (jnp.sqrt(corrected_square) + 1e-08)
        + weight_decay * weight.astype(jnp.float32)
    )
    return (moment_next, square_next, update)


def local(
    token_ids,
    segment_ids,
    parent_segments,
    expert_choice,
    drop_order,
    loss_positions,
    target_ids,
    embedding,
    attention_weights,
    router_weights,
    small_params,
    inward_weights,
    outward_weights,
    embedding_moment,
    embedding_square,
    attention_moment,
    attention_square,
    router_moment,
    router_square,
    params_moment,
    params_square,
    inward_moment,
    inward_square,
    outward_moment,
    outward_square,
):
    devices = lax.axis_size("fsdp")
    me = lax.axis_index("fsdp")
    length = token_ids.shape[0]
    vocab_rows, model_width = embedding.shape
    rows_loss = loss_positions.shape[0]
    experts_all = devices // SPLIT
    capacity = 9 * 2 * length // (8 * experts_all)
    slots = -(-capacity // 16) * 16
    block_rows = 128
    f32 = jnp.float32
    bf16 = jnp.bfloat16
    quads = [[SPLIT * e + q for q in range(SPLIT)] for e in range(experts_all)]
    router_size = router_weights.shape[0]
    params_size = small_params.shape[0]

    owner = token_ids // vocab_rows
    place = token_ids - owner * vocab_rows
    order = jnp.arange(length, dtype=jnp.int32)
    repeated = jnp.any(
        (token_ids[:, None] == token_ids[None, :]) & (order[None, :] < order[:, None]), axis=1
    )
    fresh = ~repeated
    rank = jnp.sum(
        (
            fresh[None, :]
            & (owner[None, :] == owner[:, None])
            & (token_ids[None, :] < token_ids[:, None])
        ).astype(jnp.int32),
        axis=1,
    )
    too_many = jnp.any(rank >= ASK).astype(f32)
    ask_row = jnp.where(rank < ASK, owner * ASK + rank, devices * ASK)
    ask_lines = jnp.arange(devices * ASK, dtype=jnp.int32)
    asked = jnp.sum(
        jnp.where(
            (ask_lines[:, None] == ask_row[None, :]) & fresh[None, :], place[None, :] + 1, 0
        ),
        axis=1,
    )
    hello = pack_blocks(
        (
            asked.reshape(devices, ASK).astype(f32),
            router_weights.astype(f32)[None],
            small_params.astype(f32)[None],
            target_ids.astype(f32).reshape(1, -1),
            too_many.reshape(1, 1),
        ),
        devices,
    )
    heard = swap_blocks(hello, 1, 1).reshape(devices, -1)
    spans = [ASK, router_size, params_size, 2 * rows_loss, 1]
    edges = [sum(spans[:i]) for i in range(len(spans) + 1)]
    wanted, router_full, params_full, targets_full, crowded = [
        heard[:, edges[i] : edges[i + 1]] for i in range(len(spans))
    ]
    wanted = wanted.reshape(-1).astype(jnp.int32) - 1
    router_full = router_full.reshape(-1).astype(bf16)
    params_full = params_full.reshape(-1)
    targets_full = targets_full.reshape(-1, 2).astype(jnp.int32)
    crowded = jnp.any(crowded > 0.5)
    inward_full = lax.all_gather(inward_weights[0], "fsdp", axis=0, axis_index_groups=quads)
    outward_full = lax.all_gather(outward_weights[0], "fsdp", axis=0, axis_index_groups=quads)

    siblings = [(device, device + 1 - 2 * (device % 2)) for device in range(devices)]
    chip_table = jnp.concatenate([embedding, lax.ppermute(embedding, "fsdp", siblings)], axis=0)

    wanted_mask = wanted[:, None] == jnp.arange(vocab_rows, dtype=jnp.int32)[None, :]
    served = take_rows(wanted_mask, embedding).astype(bf16).reshape(devices, ASK, model_width)
    attention_rows = attention_weights.shape[0]
    attention_pad = -attention_rows % 16
    served, attention_full = head_exchange(
        served, jnp.pad(attention_weights, ((0, attention_pad), (0, 0))), 2
    )
    served = served.reshape(devices * ASK, model_width)
    attention_full = attention_full[:, :, :attention_rows].reshape(-1, model_width)
    ask_mask = ask_row[:, None] == ask_lines[None, :]
    embedded_low = lax.cond(
        crowded,
        lambda: lax.all_gather(embedding, "fsdp", axis=0, tiled=True)[token_ids],
        lambda: take_rows(ask_mask, served).astype(bf16),
    )
    embedded = embedded_low.astype(f32) * math.sqrt(model_width)
    gain_first = params_full[:model_width]
    gain_second = params_full[model_width : 2 * model_width]
    gain_final = params_full[2 * model_width : 3 * model_width]
    bias_table = params_full[3 * model_width :].reshape(HEADS, NB)
    router_matrix = router_full.reshape(model_width, experts_all)
    buckets, prefix, edges = tree_layout(segment_ids, parent_segments[0])
    normed_first = rms_norm(embedded, gain_first).astype(bf16)
    queries, keys_all, values_all = [
        jnp.dot(
            normed_first,
            attention_full[part * model_width : (part + 1) * model_width],
            preferred_element_type=f32,
        ).astype(bf16)
        for part in range(3)
    ]
    bias_lines = jnp.pad(
        jnp.concatenate([bias_table, jnp.full((HEADS, 1), -1e30, f32)], axis=1),
        ((0, 16 - HEADS), (0, 127 - NB)),
    )
    mixed_all, log_totals = attend(queries, keys_all, values_all, buckets, bias_lines, block_rows)
    after_attn = embedded + jnp.dot(
        mixed_all, attention_full[3 * model_width :], preferred_element_type=f32
    )
    routed_in = rms_norm(after_attn, gain_second).astype(bf16)
    route_logits = jnp.dot(routed_in, router_matrix, preferred_element_type=f32)
    choice_onehot = (
        expert_choice[:, :, None] == jnp.arange(experts_all, dtype=jnp.int32)[None, None, :]
    ).astype(f32)
    chosen = jnp.sum(choice_onehot * route_logits[:, None, :], axis=-1)
    gate_peak = jnp.max(chosen, axis=1, keepdims=True)
    raised_gate = jnp.exp(chosen - gate_peak)
    gate_weights = raised_gate / jnp.sum(raised_gate, axis=1, keepdims=True)
    drop_rank = drop_order[0]
    flat_choice = expert_choice.reshape(-1)
    slot_index = jnp.sum(
        (
            (flat_choice[None, :] == flat_choice[:, None])
            & (drop_rank[None, :] < drop_rank[:, None])
        ).astype(jnp.int32),
        axis=1,
    ).reshape(length, 2)
    target_row = jnp.where(
        slot_index < capacity, expert_choice * slots + slot_index, experts_all * slots
    )
    slot_lines = jnp.arange(experts_all * slots, dtype=jnp.int32)
    first_out = target_row[:, 0][None, :] == slot_lines[:, None]
    second_out = target_row[:, 1][None, :] == slot_lines[:, None]
    first_in = target_row[:, 0][:, None] == slot_lines[None, :]
    second_in = target_row[:, 1][:, None] == slot_lines[None, :]
    outgoing = take_rows(first_out | second_out, routed_in).astype(bf16)
    expert_rows, returned_low = run_experts(
        outgoing.reshape(experts_all, slots, model_width), inward_full, outward_full, 7
    )
    returned_low = returned_low.reshape(experts_all * slots, model_width)
    returned_first = take_rows(first_in, returned_low)
    returned_second = take_rows(second_in, returned_low)
    after_moe = (
        after_attn + gate_weights[:, 0:1] * returned_first + gate_weights[:, 1:2] * returned_second
    )
    normed_final = rms_norm(after_moe, gain_final).astype(bf16)
    loss_mask = loss_positions[:, None] == order[None, :]
    picked = take_rows(loss_mask, normed_final).astype(bf16)
    scale_rows = 1.0 / (devices * rows_loss)

    chips = devices // 2
    core = lax.rem(me, 2)
    picked_all = spread_rows(picked, chips, 5).reshape(chips * rows_loss, model_width)
    scores = jnp.einsum("rd,vd->rv", picked_all, chip_table, preferred_element_type=f32)
    targets_here = jnp.where(
        core == 0,
        targets_full.reshape(chips, 2, rows_loss, 2)[:, 0],
        targets_full.reshape(chips, 2, rows_loss, 2)[:, 1],
    ).reshape(chips * rows_loss, 2)
    own_lines = jnp.arange(vocab_rows, dtype=jnp.int32)
    vocab_lines = jnp.concatenate(
        [own_lines + me * vocab_rows, own_lines + (me + 1 - 2 * core) * vocab_rows]
    )[None, :]
    first_hit = (targets_here[:, 0:1] == vocab_lines).astype(f32)
    second_hit = (targets_here[:, 1:2] == vocab_lines).astype(f32)
    part_peak = jnp.max(scores, axis=1)
    part_total = jnp.sum(jnp.exp(scores - part_peak[:, None]), axis=1)
    part_first = jnp.sum(first_hit * scores, axis=1)
    part_second = jnp.sum(second_hit * scores, axis=1)
    parts = swap_blocks(
        pack_blocks(
            [
                part.reshape(chips, rows_loss)
                for part in (part_peak, part_total, part_first, part_second)
            ],
            chips,
        ),
        2,
        6,
    ).reshape(chips, -1)[:, : 4 * rows_loss].reshape(chips, 4, rows_loss)
    row_peak = jnp.max(parts[:, 0], axis=0)
    row_total = jnp.sum(parts[:, 1] * jnp.exp(parts[:, 0] - row_peak[None]), axis=0)
    log_rows = row_peak + jnp.log(row_total)
    target_hits = jnp.sum(parts[:, 2:], axis=0)
    loss_local = jnp.sum(log_rows - target_hits[0] + 0.3 * (log_rows - target_hits[1]))
    log_all = (
        swap_blocks(pack_blocks((log_rows[None],), chips), 2, 3)
        .reshape(chips, -1)[:, :rows_loss]
        .reshape(-1)
    )
    pull = 1.3 * jnp.exp(scores - log_all[:, None]) - first_hit - 0.3 * second_hit
    pull = (pull * scale_rows).astype(bf16)
    picked_parts = jnp.dot(pull, chip_table, preferred_element_type=f32).astype(bf16)
    picked_grad = gather_sum(picked_parts.reshape(chips, rows_loss, model_width), 4)
    chip_grad = jnp.einsum("rv,rd->vd", pull, picked_all, preferred_element_type=f32)
    table_grad = chip_grad[:vocab_rows] + lax.ppermute(
        chip_grad[vocab_rows:], "fsdp", siblings
    )
    grad_normed = take_rows_wide(loss_mask.T, picked_grad)
    _, final_back = jax.vjp(rms_norm, after_moe, gain_final)
    grad_after_moe, grad_gain_final = final_back(grad_normed)
    grad_gates = jnp.stack(
        [
            jnp.sum(returned_first * grad_after_moe, axis=-1),
            jnp.sum(returned_second * grad_after_moe, axis=-1),
        ],
        axis=1,
    )
    grad_chosen = gate_weights * (
        grad_gates - jnp.sum(gate_weights * grad_gates, axis=1, keepdims=True)
    )
    grad_route = jnp.sum(choice_onehot * grad_chosen[:, :, None], axis=1).astype(bf16)
    router_grad = jnp.einsum(
        "td,te->de", routed_in, grad_route, preferred_element_type=f32
    ).reshape(-1)
    grad_routed = jnp.einsum("te,de->td", grad_route, router_matrix, preferred_element_type=f32)
    grad_slots = take_rows(
        first_out, (gate_weights[:, 0:1] * grad_after_moe).astype(bf16)
    ) + take_rows(second_out, (gate_weights[:, 1:2] * grad_after_moe).astype(bf16))
    grad_returned, inward_parts, outward_parts = run_experts_back(
        grad_slots.astype(bf16).reshape(experts_all, slots, model_width),
        expert_rows,
        inward_full,
        outward_full,
        8,
    )
    grad_returned = grad_returned.reshape(experts_all * slots, model_width)
    inward_grad = lax.psum_scatter(
        inward_parts, "fsdp", scatter_dimension=0, axis_index_groups=quads
    )[None]
    outward_grad = lax.psum_scatter(
        outward_parts, "fsdp", scatter_dimension=0, axis_index_groups=quads
    )[None]
    grad_routed = grad_routed + take_rows(first_in | second_in, grad_returned)
    _, second_back = jax.vjp(rms_norm, after_attn, gain_second)
    grad_norm_in, grad_gain_second = second_back(grad_routed)
    grad_after_attn = grad_after_moe + grad_norm_in
    grad_attn_low = grad_after_attn.astype(bf16)
    output_grad = jnp.einsum("td,te->de", mixed_all, grad_attn_low, preferred_element_type=f32)
    grad_mixed = jnp.einsum(
        "te,de->td", grad_attn_low, attention_full[3 * model_width :], preferred_element_type=f32
    ).astype(bf16)
    grad_queries_low, grad_keys_low, grad_values_low, edge_sums = attend_back(
        queries,
        keys_all,
        values_all,
        grad_mixed,
        log_totals,
        buckets,
        bias_lines,
        prefix,
        edges,
        block_rows,
    )
    edge_sums = jnp.sum(edge_sums, axis=1)[:, :NB]
    grad_bias = edge_sums - jnp.pad(edge_sums[:, 1:], ((0, 0), (0, 1)))
    projection_grads = []
    grad_normed_first = jnp.zeros((length, model_width), f32)
    for position, gradient_low in enumerate((grad_queries_low, grad_keys_low, grad_values_low)):
        projection_grads.append(
            jnp.einsum("td,te->de", normed_first, gradient_low, preferred_element_type=f32)
        )
        grad_normed_first = grad_normed_first + jnp.einsum(
            "te,de->td",
            gradient_low,
            attention_full[position * model_width : (position + 1) * model_width],
            preferred_element_type=f32,
        )
    attention_grad = jnp.concatenate(projection_grads + [output_grad], axis=0)
    _, first_back = jax.vjp(rms_norm, embedded, gain_first)
    grad_embed_in, grad_gain_first = first_back(grad_normed_first)
    grad_embedded = (grad_after_attn + grad_embed_in) * math.sqrt(model_width)
    params_grad = jnp.concatenate(
        [grad_gain_first, grad_gain_second, grad_gain_final, grad_bias.reshape(-1)]
    )
    ask_sums = take_rows_wide(ask_mask.T, grad_embedded).astype(bf16)
    attention_blocks = jnp.pad(
        attention_grad.astype(bf16).reshape(devices // 2, 2, attention_rows, model_width),
        ((0, 0), (0, 0), (0, attention_pad), (0, 0)),
    )
    small_blocks = pack_blocks(
        (router_grad.reshape(devices, router_size), params_grad.reshape(devices, params_size)),
        devices,
    )
    ask_sums, small_sums, attention_share = tail_exchange(
        ask_sums.reshape(devices, ASK, model_width), small_blocks, attention_blocks, 9
    )
    attention_share = attention_share[:attention_rows]
    small_share = jnp.sum(small_sums.reshape(devices, -1), axis=0)

    def lookup_wide():
        whole = jnp.zeros((devices * vocab_rows, model_width), f32).at[token_ids].add(grad_embedded)
        return lax.psum_scatter(whole, "fsdp", scatter_dimension=0, tiled=True)

    table_share = table_grad + lax.cond(
        crowded,
        lookup_wide,
        lambda: take_rows(wanted_mask.T, ask_sums.reshape(devices * ASK, model_width)),
    )
    router_share = small_share[:router_size]
    params_share = small_share[router_size : router_size + params_size]
    local_square = (
        jnp.sum(table_share * table_share)
        + jnp.sum(attention_share * attention_share)
        + jnp.sum(router_share * router_share)
        + jnp.sum(params_share * params_share)
        + jnp.sum(inward_grad * inward_grad)
        + jnp.sum(outward_grad * outward_grad)
    )
    total_square = jnp.sum(
        swap_blocks(pack_blocks((local_square.reshape(1, 1),), devices), 1, 11).reshape(devices, -1)[
            :, 0
        ]
    )
    grad_norm = jnp.sqrt(total_square)
    threshold = clip_base / math.sqrt(devices * rows_loss)
    factor = jnp.minimum(1.0, threshold / grad_norm)
    loss_parts = (loss_local * scale_rows).reshape(1)
    table_m, table_s, table_u = adam_step(
        embedding, embedding_moment, embedding_square, table_share, factor
    )
    attention_m, attention_s, attention_u = adam_step(
        attention_weights, attention_moment, attention_square, attention_share, factor
    )
    router_m, router_s, router_u = adam_step(
        router_weights, router_moment, router_square, router_share, factor
    )
    params_m, params_s, params_u = adam_step(
        small_params, params_moment, params_square, params_share, factor
    )
    inward_m, inward_s, inward_u = adam_step(
        inward_weights, inward_moment, inward_square, inward_grad, factor
    )
    outward_m, outward_s, outward_u = adam_step(
        outward_weights, outward_moment, outward_square, outward_grad, factor
    )
    return (
        loss_parts,
        grad_norm,
        table_m,
        table_s,
        table_u,
        attention_m,
        attention_s,
        attention_u,
        router_m,
        router_s,
        router_u,
        params_m,
        params_s,
        params_u,
        inward_m,
        inward_s,
        inward_u,
        outward_m,
        outward_s,
        outward_u,
    )


def solution(mesh):
    placed = (
        P("fsdp"),
        P("fsdp"),
        P("fsdp", None),
        P("fsdp", None),
        P("fsdp", None),
        P("fsdp"),
        P("fsdp", None),
        P("fsdp", None),
        P("fsdp", None),
        P("fsdp"),
        P("fsdp"),
        P("fsdp", None, None),
        P("fsdp", None, None),
        P("fsdp", None),
        P("fsdp", None),
        P("fsdp", None),
        P("fsdp", None),
        P("fsdp"),
        P("fsdp"),
        P("fsdp"),
        P("fsdp"),
        P("fsdp", None, None),
        P("fsdp", None, None),
        P("fsdp", None, None),
        P("fsdp", None, None),
    )
    return jax.shard_map(
        local,
        mesh=mesh,
        in_specs=placed,
        out_specs=(
            P("fsdp"),
            P(),
            P("fsdp", None),
            P("fsdp", None),
            P("fsdp", None),
            P("fsdp", None),
            P("fsdp", None),
            P("fsdp", None),
            P("fsdp"),
            P("fsdp"),
            P("fsdp"),
            P("fsdp"),
            P("fsdp"),
            P("fsdp"),
            P("fsdp", None, None),
            P("fsdp", None, None),
            P("fsdp", None, None),
            P("fsdp", None, None),
            P("fsdp", None, None),
            P("fsdp", None, None),
        ),
        check_vma=False,
    )
```

time: 3420 us -> 1170 us (0.34)
  waiting for transfers between devices: 1470 us -> 137 us
  blocking collectives: 743 us -> 0 us
  Pallas kernels: 0 us -> 735 us
  matrix products: 570 us -> 129 us
  other arithmetic: 374 us -> 81.6 us
  local copies, waits for them, and re-layouts: 212 us -> 54.4 us
    pallas_call x0 -> x12, Pallas kernels: none -> 735 us  [the longest x2 371 us: trade_call(): pl.pallas_call(functools.partial(body, peers), out_shape=[shape for shape...]
    unnamed x5 -> x4, waiting for transfers between devices: 674 us -> 1.77 us
    all_to_all x2 -> x0, blocking collectives: 622 us -> none  [the longest x1 311 us: local(): lax.all_to_all(outgoing, 'fsdp', split_axis=0, concat_axis=0, tiled=True)]
    all_to_all x2 -> x0, waiting for transfers between devices: 605 us -> none  [the longest x1 311 us: local(): lax.all_to_all(partial_out.reshape(devices, capacity, model_width), 'fsdp...]
    dot_general x65 -> x26, matrix products: 557 us -> 116 us  [the longest x12 59.9 us: take_rows(): jnp.dot(mask.astype(jnp.bfloat16), rows, preferred_element_type=jnp.float32)]
    all_gather x2, waiting for transfers between devices: 195 us -> 0.01 us  [the longest x1 0.01 us: local(): lax.all_gather(inward_weights[0], 'fsdp', axis=0, axis_index_groups=quads)]
    scatter-add x3 -> x0, other arithmetic: 153 us -> none  [the longest x1 131 us: local(): table_parts.reshape(vocab_rows, model_width).at[token_ids]]
    reduce_scatter x1 -> x2, waiting for transfers between devices: 0.01 us -> 131 us  [the longest x1 77.6 us: local(): lax.psum_scatter(outward_parts, 'fsdp', scatter_dimension=0, axis_index_g...]
  transfers between devices with their start and end apart: 6 -> 6, of which waited for: 5 -> 3; matrix products, arithmetic and copies ran while one was open for 11% -> 7% of each run, Pallas kernels for 0% -> 3%
where the time goes in v1:
time: 1170 us; the launch traced here: 1160 us
  Pallas kernels  735 us (63%)
  waiting for transfers between devices  137 us (12%)
  matrix products  129 us (11%)
  other arithmetic  81.6 us (7%)
  local copies, waits for them, and re-layouts  54.4 us (5%)
  between operations  26.4 us (2%)
    pallas_call x2, Pallas kernels, trade_call(): pl.pallas_call(functools.partial(body, peers), out_shape=[shape for shape...  371 us
    pallas_call x1, Pallas kernels, tail_exchange(): pl.pallas_call(functools.partial(tail_kernel, chips), out_shape=[jax.Shap...  79.1 us
    reduce_scatter x1, waiting for transfers between devices, local(): lax.psum_scatter(outward_parts, 'fsdp', scatter_dimension=0, axis_index_g...  77.6 us
    pallas_call x1, Pallas kernels, attend_back(): pl.pallas_call(functools.partial(attend_back_kernel, block, length), grid...  70 us
    pallas_call x1, Pallas kernels, head_exchange(): pl.pallas_call(functools.partial(head_kernel, chips), out_shape=[jax.Shap...  67 us
    dot_general x12, matrix products, take_rows(): jnp.dot(mask.astype(jnp.bfloat16), rows, preferred_element_type=jnp.float32)  59.9 us
    reduce_scatter x1, waiting for transfers between devices, local(): lax.psum_scatter(inward_parts, 'fsdp', scatter_dimension=0, axis_index_gr...  53.9 us
    pallas_call x1, Pallas kernels, gather_sum(): pl.pallas_call(functools.partial(gather_sum_kernel, chips), out_shape=jax...  39.2 us
  transfers between devices with their start and end apart: 6, of which 3 were waited for; matrix products, arithmetic and copies ran while one was open for 7% of the time, Pallas kernels for 3%

profile of v1, /device:TPU:0, one launch (start us, length us, event | category | flops | bytes accessed | tf_op | source)
XLA Modules:
  0.0 1164.4 jit_solution(17420702342939638073)
XLA Ops:
  18.9 11.0 shard_map.401
  33.6 4.2 convolution_convert_fusion.1
  37.8 67.0 %shard_map.402 = (bf16[32,48,768]{2,1,0:T(8,128)(2,1)}, bf16[16,2,96,768]{3,2,1,0:T(8,128)(2,1)}) custom-call(bf16[32,48,768]{2,1,0:T(8,128)(2,1)} %bitcast.140, bf16[96,768]{1,0:T(8,128)(2,1)} %src.1), custom_call_target="tpu_custom_call" | custom-call | tf_op jit(solution)/shard_map/pallas_call | solution.py:824
  104.9 8.3 conditional.2
  104.9 5.9 fusion
  119.7 4.2 fusion.146
  127.3 3.4 convert_reduce_fusion
  133.4 3.4 convert_element_type.275
  136.8 4.3 convolution_convert_fusion.6.q_ref
  141.1 6.9 fusion.63.bucket_ref
  151.6 36.1 %shard_map.403 = (bf16[1024,768]{1,0:T(8,128)(2,1)S(1)}, f32[6,1024,128]{2,1,0:T(8,128)S(1)}) custom-call(bf16[1024,768]{1,0:T(8,128)(2,1)S(1)} %copy-done.3, bf16[1024,768]{1,0:T(8,128)(2,1)S(1)} %convolution_convert_fusion.5.k_ref, bf16[1024,768]{1,0:T(8,128)(2,1)S(1)} %convolution_convert_fusion.4.v_ref, s32[1024,1024]{1,0:T(8,128)S(1)} %copy-done, ...), custom_call_target="tpu_custom_call" | custom-call | tf_op jit(solution)/shard_map/pallas_call | solution.py:911
  202.6 6.4 fusion.35
  209.0 2.6 constant_dynamic-update-slice_fusion
  211.6 182.8 %shard_map.404 = (bf16[8,288,768]{2,1,0:T(8,128)(2,1)}, bf16[8,288,768]{2,1,0:T(8,128)(2,1)}) custom-call(bf16[8,288,768]{2,1,0:T(8,128)(2,1)} %bitcast.135, bf16[4,768,768]{2,1,0:T(8,128)(2,1)} %all-gather.6.cloned.1.call-done.inward, bf16[4,768,768]{2,1,0:T(8,128)(2,1)} %all-gather.8.cloned.1.call-done.outward), custom_call_target="tpu_custom_call" | custom-call | tf_op jit(solution)/shard_map/pallas_call | solution.py:472
  394.4 6.5 fusion.13
  401.0 6.5 multiply_reduce_fusion.8
  410.6 36.2 %shard_map.405 = bf16[16,128,768]{2,1,0:T(8,128)(2,1)} custom-call(bf16[128,768]{1,0:T(8,128)(2,1)} %fusion.86.src), custom_call_target="tpu_custom_call" | custom-call | tf_op jit(solution)/shard_map/pallas_call | solution.py:215
  446.7 9.9 fusion.151
  456.7 6.5 fusion.2
  463.8 7.9 shard_map.406
  474.0 7.9 shard_map.407
  482.8 9.5 fusion.6
  492.3 12.8 %convolution_convert_fusion.2 = bf16[2048,768]{1,0:T(8,128)(2,1)} fusion(bf16[2048,2000]{0,1:T(8,128)(2,1)S(1)} %fusion.6, bf16[2000,768]{1,0:T(8,128)(2,1)} %constant_dynamic-update-slice_fusion), kind=kOutput, calls=%fused_computation.101 | convolution fusion | flops 6293028864 | bytes 14409728 | tf_op jit(solution)/shard_map/dot_general | solution.py:1252
  505.1 39.2 %shard_map.408 = f32[128,768]{1,0:T(8,128)} custom-call(bf16[16,128,768]{2,1,0:T(8,128)(2,1)} %bitcast.139), custom_call_target="tpu_custom_call" | custom-call | tf_op jit(solution)/shard_map/pallas_call | solution.py:288
  550.1 2.6 multiply_reduce_fusion.6
  554.6 4.6 fusion.10
  559.2 6.0 add_convert_fusion
  565.1 187.9 %shard_map.409 = (bf16[8,288,768]{2,1,0:T(8,128)(2,1)}, f32[4,768,768]{2,1,0:T(8,128)}, f32[4,768,768]{2,1,0:T(8,128)}) custom-call(bf16[8,288,768]{2,1,0:T(8,128)(2,1)} %bitcast.136, bf16[8,288,768]{2,1,0:T(8,128)(2,1)} %get-tuple-element.72.rows_ref, bf16[4,768,768]{2,1,0:T(8,128)(2,1)} %all-gather.6.cloned.1.call-done.inward, ...), custom_call_target="tpu_custom_call" | custom-call | tf_op jit(solution)/shard_map/pallas_call | solution.py:472
  753.1 6.9 fusion.16
  763.3 2.5 convolution_convert_fusion.7
  765.8 2.6 convolution_convert_fusion.3.g_ref
  768.4 70.0 %shard_map.410 = (bf16[1024,768]{1,0:T(8,128)(2,1)S(1)}, bf16[1024,768]{1,0:T(8,128)(2,1)S(1)}, bf16[1024,768]{1,0:T(8,128)(2,1)S(1)}, f32[12,8,128]{2,1,0:T(8,128)S(1)}) custom-call(bf16[1024,768]{1,0:T(8,128)(2,1)} %convolution_convert_fusion.6.q_ref, bf16[1024,768]{1,0:T(8,128)(2,1)} %copy-done.2, bf16[1024,768]{1,0:T(8,128)(2,1)} %copy-done.1, ...), custom_call_target="tpu_custom_call" | custom-call | tf_op jit(solution)/shard_map/pallas_call | solution.py:1003
  855.2 5.7 fusion.72
  865.7 79.1 %shard_map.411 = (bf16[32,48,768]{2,1,0:T(8,128)(2,1)S(1)}, f32[32,8,128]{2,1,0:T(8,128)S(1)}, f32[96,768]{1,0:T(8,128)S(1)}) custom-call(bf16[32,48,768]{2,1,0:T(8,128)(2,1)S(1)} %bitcast.127, f32[32,8,128]{2,1,0:T(8,128)S(1)} %bitcast.128, bf16[16,2,96,768]{3,2,1,0:T(8,128)(2,1)} %bitcast.129), custom_call_target="tpu_custom_call" | custom-call | tf_op jit(solution)/shard_map/pallas_call | solution.py:688
  944.8 4.6 conditional.3
  944.8 4.6 fusion.152
  950.7 9.9 fusion.154
  960.6 3.9 copy-done.27
  969.3 4.0 collective-permute-done.1
  973.2 5.8 multiply_reduce_fusion.11
  981.8 53.9 %reduce-scatter.8.cloned.1.call-done = f32[1,768,768]{2,1,0:T(8,128)} async-done(((f32[4,768,768]{2,1,0:T(8,128)}), f32[1,768,768]{2,1,0:T(8,128)}) %reduce-scatter.8.cloned.1.call-update) | async-done | bytes 2359312 | tf_op jit(solution)/shard_map/reduce_scatter | solution.py:1287
  1035.6 2.9 multiply_reduce_fusion.13
  1039.2 77.6 %reduce-scatter.10.cloned.1.call-done = f32[1,768,768]{2,1,0:T(8,128)} async-done(((f32[4,768,768]{2,1,0:T(8,128)}), f32[1,768,768]{2,1,0:T(8,128)}) %reduce-scatter.10.cloned.1.call-update) | async-done | bytes 2359312 | tf_op jit(solution)/shard_map/reduce_scatter | solution.py:1290
  1116.8 2.9 multiply_reduce_fusion.12
  1121.0 9.4 shard_map.412
  1135.0 9.0 add_multiply_fusion
  1144.0 4.3 add_multiply_fusion.1
  1150.0 4.1 add_multiply_fusion.2
  (303 shorter events, 96.6 us)
Async XLA Ops:
  8.0 25.6 %copy-start.17 = (bf16[1000,768]{1,0:T(8,128)(2,1)S(1)}, bf16[1000,768]{1,0:T(8,128)(2,1)}, u32[]{:S(2)}) copy-start(bf16[1000,768]{1,0:T(8,128)(2,1)} %param.37) | copy-start | bytes 4608004
  13.7 24.1 %copy-start.65 = (s32[1024]{0:T(1024)}, s32[1024]{0:T(1024)S(1)}, u32[]{:S(2)}) copy-start(s32[1024]{0:T(1024)S(1)} %get-tuple-element.152) | copy-start | bytes 12292
  33.6 71.3 %copy-start.59 = (s32[1024]{0:T(1024)S(1)}, s32[1024]{0:T(1024)}, u32[]{:S(2)}) copy-start(s32[1024]{0:T(1024)} %param.30) | copy-start | bytes 12292
  104.9 10.3 copy-start.56
  104.9 11.3 copy-start.67
  104.9 11.5 copy-start.78
  113.3 10.6 copy-start.7
  113.3 98.3 %all-gather.6.cloned.1.call-start = ((), (), s32[]{:S(2)}) async-start(), calls=%async_computation.5 | async-start | bytes 5898240 | tf_op jit(solution)/shard_map/all_gather | solution.py:1124
  113.9 97.8 %all-gather.8.cloned.1.call-start = ((), (), s32[]{:S(2)}) async-start(), calls=%async_computation.6 | async-start | bytes 5898240 | tf_op jit(solution)/shard_map/all_gather | solution.py:1125
  114.4 94.6 %collective-permute-start = (bf16[1000,768]{1,0:T(8,128)(2,1)}, bf16[1000,768]{1,0:T(8,128)(2,1)}, u32[]{:S(2)}, u32[]{:S(2)}) collective-permute-start(bf16[1000,768]{1,0:T(8,128)(2,1)} %param.37), channel_id=1, source_target_pairs={{0,1},{1,0},{2,3},{3,2},{4,5},{5,4},{6,7},{7,6},{8,9},{9,8},{10,11... | collective-permute-start | bytes 4608008 | tf_op jit(solution)/shard_map/ppermute | solution.py:1128
  115.2 8.7 copy-start.61
  117.4 6.5 copy-start.57
  119.1 4.8 copy-start.62
  125.7 22.2 %copy-start.1 = (bf16[1024,768]{1,0:T(8,128)(2,1)}, bf16[1024,768]{1,0:T(8,128)(2,1)S(1)}, u32[]{:S(2)}) copy-start(bf16[1024,768]{1,0:T(8,128)(2,1)S(1)} %convolution_convert_fusion.4.v_ref) | copy-start | bytes 4718596
  125.8 4.9 slice-start
  127.3 20.7 %copy-start.2 = (bf16[1024,768]{1,0:T(8,128)(2,1)}, bf16[1024,768]{1,0:T(8,128)(2,1)S(1)}, u32[]{:S(2)}) copy-start(bf16[1024,768]{1,0:T(8,128)(2,1)S(1)} %convolution_convert_fusion.5.k_ref) | copy-start | bytes 4718596
  151.6 36.2 %copy-start.8 = (f32[1024,768]{0,1:T(8,128)S(1)}, f32[1024,768]{0,1:T(8,128)}, u32[]{:S(2)}) copy-start(f32[1024,768]{0,1:T(8,128)} %copy-done.7) | copy-start | bytes 9437188
  151.6 36.2 %copy-start.32 = (bf16[4,2,96,768]{3,2,1,0:T(8,128)(2,1)S(1)}, bf16[4,2,96,768]{3,2,1,0:T(8,128)(2,1)}, u32[]{:S(2)}) copy-start(bf16[4,2,96,768]{3,2,1,0:T(8,128)(2,1)} %get-tuple-element.135) | copy-start | bytes 3538948
  394.4 6.5 copy-start.12
  394.4 6.5 copy-start.76
  400.9 6.6 copy-start.34
  400.9 8.2 copy-start.68
  456.7 6.5 copy-start.10
  492.3 12.8 %copy-start.26 = (bf16[2048,2000]{0,1:T(8,128)(2,1)}, bf16[2048,2000]{0,1:T(8,128)(2,1)S(1)}, u32[]{:S(2)}) copy-start(bf16[2048,2000]{0,1:T(8,128)(2,1)S(1)} %fusion.6) | copy-start | bytes 24576004
  552.7 6.4 copy-start.21
  753.1 6.9 copy-start.13
  768.4 70.0 %copy-start.43 = (bf16[1024,768]{0,1:T(8,128)(2,1)S(1)}, bf16[1024,768]{0,1:T(8,128)(2,1)}, u32[]{:S(2)}) copy-start(bf16[1024,768]{0,1:T(8,128)(2,1)} %copy-done.42) | copy-start | bytes 4718596
  865.7 79.1 %copy-start.41 = (pred[1536,1000]{1,0:T(32,128)(4,1)S(1)}, pred[1536,1000]{1,0:T(32,128)(4,1)}, u32[]{:S(2)}) copy-start(pred[1536,1000]{1,0:T(32,128)(4,1)} %iota_compare_fusion.9) | copy-start | bytes 4608004
  865.7 79.1 %copy-start.60 = (s32[1024]{0:T(1024)S(1)}, s32[1024]{0:T(1024)}, u32[]{:S(2)}) copy-start(s32[1024]{0:T(1024)} %param.30) | copy-start | bytes 12292
  949.4 86.2 %reduce-scatter.8.cloned.1.call-start = ((), (), s32[]{:S(2)}) async-start(), calls=%async_computation.7 | async-start | bytes 11796480 | tf_op jit(solution)/shard_map/reduce_scatter | solution.py:1287
  950.0 166.8 %reduce-scatter.10.cloned.1.call-start = ((), (), s32[]{:S(2)}) async-start(), calls=%async_computation.8 | async-start | bytes 11796480 | tf_op jit(solution)/shard_map/reduce_scatter | solution.py:1290
  966.6 6.6 collective-permute-start.1
  979.0 153.7 %copy-start.70 = (bf16[84]{0:T(256)(128)(2,1)S(1)}, bf16[84]{0:T(256)(128)(2,1)}, u32[]{:S(2)}) copy-start(bf16[84]{0:T(256)(128)(2,1)} %param.40) | copy-start | bytes 508
  979.0 153.7 %copy-start.74 = (f32[84]{0:T(128)S(1)}, f32[84]{0:T(128)}, u32[]{:S(2)}) copy-start(f32[84]{0:T(128)} %param.50) | copy-start | bytes 1012
  979.0 153.7 %copy-start.75 = (f32[84]{0:T(128)S(1)}, f32[84]{0:T(128)}, u32[]{:S(2)}) copy-start(f32[84]{0:T(128)} %param.49) | copy-start | bytes 1012
  979.0 154.3 %copy-start.69 = (bf16[192]{0:T(256)(128)(2,1)S(1)}, bf16[192]{0:T(256)(128)(2,1)}, u32[]{:S(2)}) copy-start(bf16[192]{0:T(256)(128)(2,1)} %param.39) | copy-start | bytes 1156
  979.0 154.3 %copy-start.71 = (f32[192]{0:T(256)S(1)}, f32[192]{0:T(256)}, u32[]{:S(2)}) copy-start(f32[192]{0:T(256)} %param.48) | copy-start | bytes 2308
  979.0 154.3 %copy-start.72 = (f32[192]{0:T(256)S(1)}, f32[192]{0:T(256)}, u32[]{:S(2)}) copy-start(f32[192]{0:T(256)} %param.47) | copy-start | bytes 2308
  979.0 154.9 %copy-start.51 = (bf16[96,768]{1,0:T(8,128)(2,1)S(1)}, bf16[96,768]{1,0:T(8,128)(2,1)}, u32[]{:S(2)}) copy-start(bf16[96,768]{1,0:T(8,128)(2,1)} %src.1) | copy-start | bytes 442372
  979.0 154.9 %copy-start.52 = (f32[96,768]{1,0:T(8,128)S(1)}, f32[96,768]{1,0:T(8,128)}, u32[]{:S(2)}) copy-start(f32[96,768]{1,0:T(8,128)} %param.46) | copy-start | bytes 884740
  979.0 154.9 %copy-start.53 = (f32[96,768]{1,0:T(8,128)S(1)}, f32[96,768]{1,0:T(8,128)}, u32[]{:S(2)}) copy-start(f32[96,768]{1,0:T(8,128)} %param.45) | copy-start | bytes 884740
  981.8 153.2 %copy-start.19 = (bf16[1000,768]{1,0:T(8,128)(2,1)S(1)}, bf16[1000,768]{1,0:T(8,128)(2,1)}, u32[]{:S(2)}) copy-start(bf16[1000,768]{1,0:T(8,128)(2,1)} %param.37) | copy-start | bytes 4608004
  1135.0 9.0 copy-start.24
  1135.0 9.0 copy-start.30
  1135.0 9.0 copy-start.37
  1135.0 9.0 copy-start.38
  1144.0 5.1 copy-start.39
  1144.0 6.0 copy-start.40
  (37 other events, 88.2 us)
Sparse Core Ops, SparseCore 1:
  115.4 45.5 all-gather.5
  162.5 37.3 all-gather.7
  952.7 82.9 reduce-scatter.7
  1038.4 78.3 reduce-scatter.9

commit v2 on v1

--- a/solution.py
+++ b/solution.py
@@ -162,15 +162,70 @@
     return layers, layer, col, device, others
 
 
-def spread_kernel(chips, src, dst, layer_send, layer_recv, col_send, col_recv, own_sem):
-    layers, layer, col, device, others = chip_place(chips)
-    meet(others)
+def loss_kernel(
+    chips,
+    scale,
+    picked,
+    table,
+    table_t,
+    ids,
+    targets,
+    out,
+    table_grad,
+    loss_rows,
+    rows,
+    scores,
+    pulls,
+    picks,
+    stat_out,
+    stat_in,
+    log_out,
+    log_in,
+    col_in,
+    layer_out,
+    layer_in,
+    own_sem,
+    layer_send,
+    layer_recv,
+    col_send,
+    col_recv,
+    sum_layer_send,
+    sum_layer_recv,
+    sum_col_send,
+    sum_col_recv,
+    stat_send,
+    stat_recv,
+    log_send,
+    log_recv,
+):
+    layers, layer, col, device, _ = chip_place(chips)
+    core = lax.rem(lax.axis_index("fsdp"), 2)
     chip = layer * BLOCK + col
-
-    def to_layer(step, source, at):
+    f32 = jnp.float32
+    bf16 = jnp.bfloat16
+    count, width = picked.shape
+    group = BLOCK * count
+    lines_all = table.shape[0]
+    lines_step = min(512, lines_all)
+    line_steps = lines_all // lines_step
+    barrier = pltpu.get_barrier_semaphore()
+
+    def far_chip(shift):
+        return lax.rem(chip + shift, chips)
+
+    def greet(shift, carry):
+        pl.semaphore_signal(
+            barrier, inc=1, device_id=(far_chip(shift) * 2 + core,), device_id_type=MESH
+        )
+        return carry
+
+    lax.fori_loop(1, chips, greet, 0)
+    pl.semaphore_wait(barrier, chips - 1)
+
+    def to_layer(step, at):
         return pltpu.make_async_remote_copy(
-            src_ref=source,
-            dst_ref=dst.at[at],
+            src_ref=picked,
+            dst_ref=rows.at[at],
             send_sem=layer_send.at[step],
             recv_sem=layer_recv.at[step],
             device_id=(device(around(step, layers, layer), col),),
@@ -180,129 +235,293 @@
     def to_col(step, turn, source, at):
         return pltpu.make_async_remote_copy(
             src_ref=source,
-            dst_ref=dst.at[at],
+            dst_ref=rows.at[at],
             send_sem=col_send.at[step, turn],
             recv_sem=col_recv.at[step, turn],
             device_id=(device(layer, around(turn, BLOCK, col)),),
             device_id_type=MESH,
         )
 
-    for step in range(1, layers):
-        to_layer(step, src, chip).start()
+    def origin(step, turn):
+        return around(layers - step, layers, layer) * BLOCK + around(BLOCK - turn, BLOCK, col)
+
+    def layer_start(step, carry):
+        to_layer(step, chip).start()
+        return carry
+
+    lax.fori_loop(1, layers, layer_start, 0)
     for turn in range(1, BLOCK):
-        to_col(0, turn, src, chip).start()
-    own = pltpu.make_async_copy(src, dst.at[chip], own_sem)
+        to_col(0, turn, picked, chip).start()
+    own = pltpu.make_async_copy(picked, rows.at[chip], own_sem)
     own.start()
-    for step in range(1, layers):
-        origin = around(layers - step, layers, layer) * BLOCK + col
-        to_layer(step, src, origin).wait_recv()
+    table_grad[...] = jnp.zeros_like(table_grad)
+    stat_out[...] = jnp.zeros_like(stat_out)
+    own.wait()
+
+    def lines_of(number):
+        return pl.ds(pl.multiple_of(number * lines_step, lines_step), lines_step)
+
+    def layer_rows(far):
+        return rows[pl.ds(far * BLOCK, BLOCK)].reshape(group, width)
+
+    def score(lines, block):
+        values = lax.dot_general(table[lines, :], block, NT, preferred_element_type=f32)
+        return jnp.where(ids[lines, :] >= 0, values, -1e30)
+
+    def to_owner(at):
+        return pltpu.make_async_remote_copy(
+            src_ref=stat_out.at[at],
+            dst_ref=stat_in.at[chip],
+            send_sem=stat_send.at[at],
+            recv_sem=stat_recv.at[chip],
+            device_id=(at * 2 + core,),
+            device_id_type=MESH,
+        )
+
+    def from_chip(at):
+        return pltpu.make_async_remote_copy(
+            src_ref=stat_out.at[at],
+            dst_ref=stat_in.at[at],
+            send_sem=stat_send.at[at],
+            recv_sem=stat_recv.at[at],
+            device_id=(at * 2 + core,),
+            device_id_type=MESH,
+        )
+
+    def measure(step, far):
+        block = layer_rows(far)
+        first = targets[far, 0:1, :]
+        second = targets[far, 1:2, :]
+
+        def peak_of(number, peak):
+            lines = lines_of(number)
+            values = score(lines, block)
+            scores[lines, :] = values
+            return jnp.maximum(peak, jnp.max(values, axis=0, keepdims=True))
+
+        peak = lax.fori_loop(0, line_steps, peak_of, jnp.full((1, group), -1e30, f32))
+
+        def total_of(number, carry):
+            total, first_sum, second_sum = carry
+            lines = lines_of(number)
+            values = scores[lines, :]
+            vocab = ids[lines, :]
+            total = total + jnp.sum(jnp.exp(values - peak), axis=0, keepdims=True)
+            first_sum = first_sum + jnp.sum(
+                jnp.where(vocab == first, values, 0.0), axis=0, keepdims=True
+            )
+            second_sum = second_sum + jnp.sum(
+                jnp.where(vocab == second, values, 0.0), axis=0, keepdims=True
+            )
+            return total, first_sum, second_sum
+
+        zero = jnp.zeros((1, group), f32)
+        sums = lax.fori_loop(0, line_steps, total_of, (zero, zero, zero))
+        for part in range(BLOCK):
+            lanes = slice(part * count, (part + 1) * count)
+            at = far * BLOCK + part
+            stat_out[at, 0:1, :] = peak[:, lanes]
+            for number in range(3):
+                stat_out[at, number + 1 : number + 2, :] = sums[number][:, lanes]
+
+            @pl.when(jnp.logical_or(step != 0, part != col))
+            def _():
+                to_owner(at).start()
+
+    def layer_pass(step, carry):
+        at = origin(step, 0)
+
+        @pl.when(step > 0)
+        def _():
+            to_layer(step, at).wait_recv()
+            for turn in range(1, BLOCK):
+                to_col(step, turn, rows.at[at], at).start()
+
+        return carry
+
+    def layer_measure(step, carry):
         for turn in range(1, BLOCK):
-            to_col(step, turn, dst.at[origin], origin).start()
-    for step in range(layers):
-        for turn in range(1, BLOCK):
-            at = around(layers - step, layers, layer) * BLOCK + around(BLOCK - turn, BLOCK, col)
-            to_col(step, turn, dst.at[at], at).wait_recv()
-    for step in range(1, layers):
-        to_layer(step, src, chip).wait_send()
-    for step in range(layers):
-        for turn in range(1, BLOCK):
-            to_col(step, turn, src, chip).wait_send()
-    own.wait()
-
-
-def spread_rows(block, chips, call_id):
-    layers = chips // BLOCK
-    return pl.pallas_call(
-        functools.partial(spread_kernel, chips),
-        out_shape=jax.ShapeDtypeStruct((chips, *block.shape), block.dtype),
-        in_specs=[pl.BlockSpec(memory_space=pl.ANY)],
-        out_specs=pl.BlockSpec(memory_space=pl.ANY),
-        scratch_shapes=[
-            pltpu.SemaphoreType.DMA((layers,)),
-            pltpu.SemaphoreType.DMA((layers,)),
-            pltpu.SemaphoreType.DMA((layers, BLOCK)),
-            pltpu.SemaphoreType.DMA((layers, BLOCK)),
-            pltpu.SemaphoreType.DMA,
-        ],
-        compiler_params=pltpu.CompilerParams(collective_id=call_id, has_side_effects=True),
-    )(block)
-
-
-def gather_sum_kernel(
-    chips, src, out, col_in, layer_out, layer_in, layer_send, layer_recv, col_send, col_recv
-):
-    layers, layer, col, device, others = chip_place(chips)
-    meet(others)
-
-    def to_col(step, turn):
+            at = origin(step, turn)
+            to_col(step, turn, rows.at[at], at).wait_recv()
+        measure(step, around(layers - step, layers, layer))
+        return carry
+
+    lax.fori_loop(0, layers, layer_pass, 0)
+    lax.fori_loop(0, layers, layer_measure, 0)
+    stat_in[chip] = stat_out[chip]
+
+    def stat_wait(shift, carry):
+        from_chip(far_chip(shift)).wait_recv()
+        return carry
+
+    lax.fori_loop(1, chips, stat_wait, 0)
+    peaks = stat_in[:, 0, :]
+    peak = jnp.max(peaks, axis=0, keepdims=True)
+    total = jnp.sum(stat_in[:, 1, :] * jnp.exp(peaks - peak), axis=0, keepdims=True)
+    first_hit = jnp.sum(stat_in[:, 2, :], axis=0, keepdims=True)
+    second_hit = jnp.sum(stat_in[:, 3, :], axis=0, keepdims=True)
+    log_rows = peak + jnp.log(total)
+    loss_rows[...] = jnp.broadcast_to(
+        log_rows - first_hit + 0.3 * (log_rows - second_hit), loss_rows.shape
+    )
+    log_out[...] = jnp.broadcast_to(log_rows, log_out.shape)
+    log_in[chip] = log_out[...]
+
+    def to_chip(shift, at):
+        return pltpu.make_async_remote_copy(
+            src_ref=log_out,
+            dst_ref=log_in.at[at],
+            send_sem=log_send.at[shift],
+            recv_sem=log_recv.at[at],
+            device_id=(far_chip(shift) * 2 + core,),
+            device_id_type=MESH,
+        )
+
+    def log_begin(shift, carry):
+        to_chip(shift, chip).start()
+        return carry
+
+    def log_wait(shift, carry):
+        to_chip(shift, far_chip(shift)).wait_recv()
+        return carry
+
+    lax.fori_loop(1, chips, log_begin, 0)
+    lax.fori_loop(1, chips, log_wait, 0)
+
+    def pull_back(step):
         far = around(step, layers, layer)
+        block = layer_rows(far)
+        first = targets[far, 0:1, :]
+        second = targets[far, 1:2, :]
+        logs = jnp.concatenate(
+            [log_in[far * BLOCK + part, 0:1, :] for part in range(BLOCK)], axis=1
+        )
+
+        def pull_of(number, carry):
+            lines = lines_of(number)
+            vocab = ids[lines, :]
+            pull = (
+                1.3 * jnp.exp(score(lines, block) - logs)
+                - (vocab == first).astype(f32)
+                - 0.3 * (vocab == second).astype(f32)
+            )
+            pull = (pull * scale).astype(bf16)
+            pulls[lines, :] = pull
+            table_grad[lines, :] += jnp.dot(pull, block, preferred_element_type=f32)
+            return carry
+
+        lax.fori_loop(0, line_steps, pull_of, 0)
+        grads = jnp.dot(table_t[...], pulls[...], preferred_element_type=f32).astype(bf16)
+        for part in range(BLOCK):
+            picks[step, part] = grads[:, part * count : (part + 1) * count]
+
+    def sum_to_col(step, turn):
         return pltpu.make_async_remote_copy(
-            src_ref=src.at[far * BLOCK + around(turn, BLOCK, col)],
+            src_ref=picks.at[step, around(turn, BLOCK, col)],
             dst_ref=col_in.at[step, turn],
-            send_sem=col_send.at[step, turn],
-            recv_sem=col_recv.at[step, turn],
+            send_sem=sum_col_send.at[step, turn],
+            recv_sem=sum_col_recv.at[step, turn],
             device_id=(device(layer, around(turn, BLOCK, col)),),
             device_id_type=MESH,
         )
 
-    def to_layer(step):
+    def sum_to_layer(step):
         return pltpu.make_async_remote_copy(
             src_ref=layer_out.at[step],
             dst_ref=layer_in.at[step],
-            send_sem=layer_send.at[step],
-            recv_sem=layer_recv.at[step],
+            send_sem=sum_layer_send.at[step],
+            recv_sem=sum_layer_recv.at[step],
             device_id=(device(around(step, layers, layer), col),),
             device_id_type=MESH,
         )
 
     def block_sum(step):
+        total = picks[step, col].astype(f32)
         for turn in range(1, BLOCK):
-            to_col(step, turn).wait_recv()
-        total = src[around(step, layers, layer) * BLOCK + col].astype(jnp.float32)
+            sum_to_col(step, turn).wait_recv()
+            total = total + col_in[step, turn].astype(f32)
+        return total
+
+    def pull_pass(number, carry):
+        step = lax.rem(number + 1, layers)
+        pull_back(step)
         for turn in range(1, BLOCK):
-            total = total + col_in[step, turn].astype(jnp.float32)
-        return total
-
-    steps = list(range(1, layers)) + [0]
-    for step in steps:
+            sum_to_col(step, turn).start()
+
+        @pl.when(number > 0)
+        def _():
+            layer_out[number] = block_sum(number).astype(bf16)
+            sum_to_layer(number).start()
+
+        return carry
+
+    lax.fori_loop(0, layers, pull_pass, 0)
+    out[...] = block_sum(0)
+
+    def layer_finish(step, carry):
+        sum_to_layer(step).wait_recv()
+        out[...] += layer_in[step].astype(f32)
+        sum_to_layer(step).wait_send()
+        to_layer(step, chip).wait_send()
+        return carry
+
+    def col_finish(step, carry):
         for turn in range(1, BLOCK):
-            to_col(step, turn).start()
-    for step in range(1, layers):
-        layer_out[step] = block_sum(step).astype(jnp.bfloat16)
-        to_layer(step).start()
-    total = block_sum(0)
-    for step in range(1, layers):
-        to_layer(step).wait_recv()
-        total = total + layer_in[step].astype(jnp.float32)
-    out[...] = total
-    for step in range(1, layers):
-        to_layer(step).wait_send()
-    for step in range(layers):
-        for turn in range(1, BLOCK):
-            to_col(step, turn).wait_send()
-
-
-def gather_sum(blocks, call_id):
-    chips, rows, width = blocks.shape
+            to_col(step, turn, picked, chip).wait_send()
+            sum_to_col(step, turn).wait_send()
+        return carry
+
+    def small_finish(shift, carry):
+        from_chip(far_chip(shift)).wait_send()
+        to_chip(shift, chip).wait_send()
+        return carry
+
+    lax.fori_loop(1, layers, layer_finish, 0)
+    lax.fori_loop(0, layers, col_finish, 0)
+    lax.fori_loop(1, chips, small_finish, 0)
+
+
+def loss_exchange(picked, table, ids, targets, chips, scale, call_id):
+    count, width = picked.shape
     layers = chips // BLOCK
+    group = BLOCK * count
+    lines_all = table.shape[0]
+    f32 = jnp.float32
+    bf16 = jnp.bfloat16
+    near = pl.BlockSpec(memory_space=pltpu.VMEM)
     return pl.pallas_call(
-        functools.partial(gather_sum_kernel, chips),
-        out_shape=jax.ShapeDtypeStruct((rows, width), jnp.float32),
-        in_specs=[pl.BlockSpec(memory_space=pltpu.VMEM)],
-        out_specs=pl.BlockSpec(memory_space=pltpu.VMEM),
+        functools.partial(loss_kernel, chips, scale),
+        out_shape=[
+            jax.ShapeDtypeStruct((width, count), f32),
+            jax.ShapeDtypeStruct((lines_all, width), f32),
+            jax.ShapeDtypeStruct((8, count), f32),
+        ],
+        in_specs=[pl.BlockSpec(memory_space=pl.ANY)] + [near] * 4,
+        out_specs=[near] * 3,
         scratch_shapes=[
-            pltpu.VMEM((layers, BLOCK, rows, width), jnp.bfloat16),
-            pltpu.VMEM((layers, rows, width), jnp.bfloat16),
-            pltpu.VMEM((layers, rows, width), jnp.bfloat16),
-            pltpu.SemaphoreType.DMA((layers,)),
-            pltpu.SemaphoreType.DMA((layers,)),
-            pltpu.SemaphoreType.DMA((layers, BLOCK)),
-            pltpu.SemaphoreType.DMA((layers, BLOCK)),
-        ],
+            pltpu.VMEM((chips, count, width), bf16),
+            pltpu.VMEM((lines_all, group), f32),
+            pltpu.VMEM((lines_all, group), bf16),
+            pltpu.VMEM((layers, BLOCK, width, count), bf16),
+            pltpu.VMEM((chips, 8, count), f32),
+            pltpu.VMEM((chips, 8, count), f32),
+            pltpu.VMEM((8, count), f32),
+            pltpu.VMEM((chips, 8, count), f32),
+            pltpu.VMEM((layers, BLOCK, width, count), bf16),
+            pltpu.VMEM((layers, width, count), bf16),
+            pltpu.VMEM((layers, width, count), bf16),
+            pltpu.SemaphoreType.DMA,
+        ]
+        + (
+            [pltpu.SemaphoreType.DMA((layers,))] * 2
+            + [pltpu.SemaphoreType.DMA((layers, BLOCK))] * 2
+        )
+        * 2
+        + [pltpu.SemaphoreType.DMA((chips,))] * 4,
         compiler_params=pltpu.CompilerParams(
-            collective_id=call_id, has_side_effects=True, vmem_limit_bytes=56 * 1024 * 1024
+            collective_id=call_id, has_side_effects=True, vmem_limit_bytes=60 * 1024 * 1024
         ),
-    )(blocks)
+    )(picked, table, table.T, ids, targets)
 
 
 def gelu_parts(values):
@@ -1125,7 +1344,20 @@
     outward_full = lax.all_gather(outward_weights[0], "fsdp", axis=0, axis_index_groups=quads)
 
     siblings = [(device, device + 1 - 2 * (device % 2)) for device in range(devices)]
-    chip_table = jnp.concatenate([embedding, lax.ppermute(embedding, "fsdp", siblings)], axis=0)
+    chips = devices // 2
+    core = lax.rem(me, 2)
+    vocab_pad = -(-vocab_rows // 256) * 256
+    fill = ((0, vocab_pad - vocab_rows), (0, 0))
+    chip_table = jnp.concatenate(
+        [jnp.pad(embedding, fill), jnp.pad(lax.ppermute(embedding, "fsdp", siblings), fill)], axis=0
+    )
+    vocab_lines = jnp.arange(vocab_pad, dtype=jnp.int32)
+    chip_ids = jnp.concatenate(
+        [
+            jnp.where(vocab_lines < vocab_rows, vocab_lines + side * vocab_rows, -1)
+            for side in (me, me + 1 - 2 * core)
+        ]
+    )[:, None]
 
     wanted_mask = wanted[:, None] == jnp.arange(vocab_rows, dtype=jnp.int32)[None, :]
     served = take_rows(wanted_mask, embedding).astype(bf16).reshape(devices, ASK, model_width)
@@ -1207,55 +1439,20 @@
     picked = take_rows(loss_mask, normed_final).astype(bf16)
     scale_rows = 1.0 / (devices * rows_loss)
 
-    chips = devices // 2
-    core = lax.rem(me, 2)
-    picked_all = spread_rows(picked, chips, 5).reshape(chips * rows_loss, model_width)
-    scores = jnp.einsum("rd,vd->rv", picked_all, chip_table, preferred_element_type=f32)
     targets_here = jnp.where(
         core == 0,
         targets_full.reshape(chips, 2, rows_loss, 2)[:, 0],
         targets_full.reshape(chips, 2, rows_loss, 2)[:, 1],
-    ).reshape(chips * rows_loss, 2)
-    own_lines = jnp.arange(vocab_rows, dtype=jnp.int32)
-    vocab_lines = jnp.concatenate(
-        [own_lines + me * vocab_rows, own_lines + (me + 1 - 2 * core) * vocab_rows]
-    )[None, :]
-    first_hit = (targets_here[:, 0:1] == vocab_lines).astype(f32)
-    second_hit = (targets_here[:, 1:2] == vocab_lines).astype(f32)
-    part_peak = jnp.max(scores, axis=1)
-    part_total = jnp.sum(jnp.exp(scores - part_peak[:, None]), axis=1)
-    part_first = jnp.sum(first_hit * scores, axis=1)
-    part_second = jnp.sum(second_hit * scores, axis=1)
-    parts = swap_blocks(
-        pack_blocks(
-            [
-                part.reshape(chips, rows_loss)
-                for part in (part_peak, part_total, part_first, part_second)
-            ],
-            chips,
-        ),
-        2,
-        6,
-    ).reshape(chips, -1)[:, : 4 * rows_loss].reshape(chips, 4, rows_loss)
-    row_peak = jnp.max(parts[:, 0], axis=0)
-    row_total = jnp.sum(parts[:, 1] * jnp.exp(parts[:, 0] - row_peak[None]), axis=0)
-    log_rows = row_peak + jnp.log(row_total)
-    target_hits = jnp.sum(parts[:, 2:], axis=0)
-    loss_local = jnp.sum(log_rows - target_hits[0] + 0.3 * (log_rows - target_hits[1]))
-    log_all = (
-        swap_blocks(pack_blocks((log_rows[None],), chips), 2, 3)
-        .reshape(chips, -1)[:, :rows_loss]
-        .reshape(-1)
-    )
-    pull = 1.3 * jnp.exp(scores - log_all[:, None]) - first_hit - 0.3 * second_hit
-    pull = (pull * scale_rows).astype(bf16)
-    picked_parts = jnp.dot(pull, chip_table, preferred_element_type=f32).astype(bf16)
-    picked_grad = gather_sum(picked_parts.reshape(chips, rows_loss, model_width), 4)
-    chip_grad = jnp.einsum("rv,rd->vd", pull, picked_all, preferred_element_type=f32)
+    ).reshape(chips // BLOCK, BLOCK * rows_loss, 2)
+    targets_here = jnp.pad(targets_here.swapaxes(1, 2), ((0, 0), (0, 6), (0, 0)))
+    picked_grad, chip_grad, loss_rows = loss_exchange(
+        picked, chip_table, chip_ids, targets_here, chips, scale_rows, 5
+    )
+    loss_local = jnp.sum(loss_rows[0])
     table_grad = chip_grad[:vocab_rows] + lax.ppermute(
-        chip_grad[vocab_rows:], "fsdp", siblings
-    )
-    grad_normed = take_rows_wide(loss_mask.T, picked_grad)
+        chip_grad[vocab_pad : vocab_pad + vocab_rows], "fsdp", siblings
+    )
+    grad_normed = take_rows_wide(loss_mask.T, picked_grad.T)
     _, final_back = jax.vjp(rms_norm, after_moe, gain_final)
     grad_after_moe, grad_gain_final = final_back(grad_normed)
     grad_gates = jnp.stack(
@@ -1311,6 +1508,11 @@
         edges,
         block_rows,
     )
+    grad_queries_low, grad_keys_low, grad_values_low, edge_sums, inward_grad = (
+        lax.optimization_barrier(
+            (grad_queries_low, grad_keys_low, grad_values_low, edge_sums, inward_grad)
+        )
+    )
     edge_sums = jnp.sum(edge_sums, axis=1)[:, :NB]
     grad_bias = edge_sums - jnp.pad(edge_sums[:, 1:], ((0, 0), (0, 1)))
     projection_grads = []
@@ -1343,6 +1545,9 @@
     )
     ask_sums, small_sums, attention_share = tail_exchange(
         ask_sums.reshape(devices, ASK, model_width), small_blocks, attention_blocks, 9
+    )
+    ask_sums, small_sums, attention_share, outward_grad = lax.optimization_barrier(
+        (ask_sums, small_sums, attention_share, outward_grad)
     )
     attention_share = attention_share[:attention_rows]
     small_share = jnp.sum(small_sums.reshape(devices, -1), axis=0)

time: 1170 us -> 1020 us (0.87)
  waiting for transfers between devices: 137 us -> 1.34 us
  matrix products: 129 us -> 96.9 us
  Pallas kernels: 735 us -> 762 us
    reduce_scatter x1, waiting for transfers between devices: 77.6 us -> 0.03 us  [local(): lax.psum_scatter(outward_parts, 'fsdp', scatter_dimension=0, axis_index_g...]
    reduce_scatter x1, waiting for transfers between devices: 53.9 us -> 0.01 us  [local(): lax.psum_scatter(inward_parts, 'fsdp', scatter_dimension=0, axis_index_gr...]
    dot_general x3 -> x0, matrix products: 32.6 us -> none  [the longest x1 12.8 us: local(): jnp.dot(pull, chip_table, preferred_element_type=f32).astype(bf16)]
    pallas_call x2 -> x1, Pallas kernels: 75.3 us -> 101 us  [loss_exchange(): pl.pallas_call(functools.partial(loss_kernel, chips, scale), out_shape=[j...]
    pallas_call x4 -> x2, Pallas kernels: 36.3 us -> 22.1 us  [swap_blocks(): pl.pallas_call(functools.partial(swap_kernel, peers, stride), out_shape=j...]
    unnamed x168 -> x141, local copies, waits for them, and re-layouts: 29.1 us -> 24.7 us
  transfers between devices with their start and end apart: 6 -> 6, of which waited for: 3 -> 0; matrix products, arithmetic and copies ran while one was open for 7% -> 12% of each run, Pallas kernels for 3% -> 20%
where the time goes in v2:
time: 1020 us
  Pallas kernels  762 us (75%)
  matrix products  96.9 us (10%)
  other arithmetic  75.5 us (7%)
  local copies, waits for them, and re-layouts  58 us (6%)
  between operations  25.8 us (3%)
    pallas_call x2, Pallas kernels, trade_call(): pl.pallas_call(functools.partial(body, peers), out_shape=[shape for shape...  371 us
    pallas_call x1, Pallas kernels, loss_exchange(): pl.pallas_call(functools.partial(loss_kernel, chips, scale), out_shape=[j...  101 us
    pallas_call x1, Pallas kernels, tail_exchange(): pl.pallas_call(functools.partial(tail_kernel, chips), out_shape=[jax.Shap...  83.8 us
    pallas_call x1, Pallas kernels, attend_back(): pl.pallas_call(functools.partial(attend_back_kernel, block, length), grid...  70 us
    pallas_call x1, Pallas kernels, head_exchange(): pl.pallas_call(functools.partial(head_kernel, chips), out_shape=[jax.Shap...  67 us
    dot_general x12, matrix products, take_rows(): jnp.dot(mask.astype(jnp.bfloat16), rows, preferred_element_type=jnp.float32)  62.9 us
    pallas_call x1, Pallas kernels, attend(): pl.pallas_call(functools.partial(attend_kernel, block, length), grid=(wid...  47.5 us
    unnamed x141, local copies, waits for them, and re-layouts  24.7 us
  transfers between devices with their start and end apart: 6, of which 0 were waited for; matrix products, arithmetic and copies ran while one was open for 12% of the time, Pallas kernels for 20%

profile of v2, /device:TPU:0, one launch (start us, length us, event | category | flops | bytes accessed | tf_op | source)
XLA Modules:
  0.0 1020.9 jit_solution(14003715323596880090)
XLA Ops:
  10.1 2.3 convert_reduce_fusion.1
  18.9 11.0 %shard_map.401 = f32[32,8,128]{2,1,0:T(8,128)} custom-call(f32[32,8,128]{2,1,0:T(8,128)} %bitcast.102), custom_call_target="tpu_custom_call" | custom-call | tf_op jit(solution)/shard_map/pallas_call | solution.py:125
  33.7 4.2 convolution_convert_fusion.1
  37.9 67.0 %shard_map.402 = (bf16[32,48,768]{2,1,0:T(8,128)(2,1)}, bf16[16,2,96,768]{3,2,1,0:T(8,128)(2,1)}) custom-call(bf16[32,48,768]{2,1,0:T(8,128)(2,1)} %bitcast.97, bf16[96,768]{1,0:T(8,128)(2,1)} %src.1), custom_call_target="tpu_custom_call" | custom-call | tf_op jit(solution)/shard_map/pallas_call | solution.py:1043
  105.0 8.3 conditional.2
  105.0 5.9 fusion
  110.9 2.4 copy.147
  118.8 3.4 convert_element_type.264
  122.2 3.4 convert_reduce_fusion
  125.6 2.7 slice_select_fusion
  128.6 2.7 copy.131
  137.7 4.3 fusion.138
  145.1 2.6 convolution_convert_fusion.3.v_ref
  147.7 6.9 fusion.59.bucket_ref
  154.6 2.2 copy-done
  158.3 47.5 %shard_map.403 = (bf16[1024,768]{1,0:T(8,128)(2,1)S(1)}, f32[6,1024,128]{2,1,0:T(8,128)S(1)}) custom-call(bf16[1024,768]{1,0:T(8,128)(2,1)S(1)} %convolution_convert_fusion.5.q_ref, bf16[1024,768]{1,0:T(8,128)(2,1)S(1)} %convolution_convert_fusion.4.k_ref, bf16[1024,768]{1,0:T(8,128)(2,1)S(1)} %copy-done.3, s32[1024,1024]{1,0:T(8,128)S(1)} %copy-done, ...), custom_call_target="tpu_custom_call" | custom-call | tf_op jit(solution)/shard_map/pallas_call | solution.py:1130
  212.0 7.6 fusion.31
  219.6 2.6 copy.132
  222.2 4.5 fusion.130
  226.7 4.7 copy.135.table
  231.4 181.2 %shard_map.404 = (bf16[8,288,768]{2,1,0:T(8,128)(2,1)}, bf16[8,288,768]{2,1,0:T(8,128)(2,1)}) custom-call(bf16[8,288,768]{2,1,0:T(8,128)(2,1)} %bitcast.95, bf16[4,768,768]{2,1,0:T(8,128)(2,1)} %all-gather.6.cloned.1.call-done.inward, bf16[4,768,768]{2,1,0:T(8,128)(2,1)} %all-gather.8.cloned.1.call-done.outward), custom_call_target="tpu_custom_call" | custom-call | tf_op jit(solution)/shard_map/pallas_call | solution.py:691
  412.6 6.5 fusion.7
  419.1 6.6 multiply_reduce_fusion.8
  428.9 101.3 %shard_map.405 = (f32[768,128]{1,0:T(8,128)}, f32[2048,768]{1,0:T(8,128)}, f32[8,128]{1,0:T(8,128)}) custom-call(bf16[128,768]{1,0:T(8,128)(2,1)} %fusion.82.picked, bf16[2048,768]{1,0:T(8,128)(2,1)} %copy.135.table, bf16[768,2048]{1,0:T(8,128)(2,1)} %get-tuple-element.158.table_t, s32[2048,1]{1,0:T(8,128)} %copy.136.ids, s32[4,8,512]{2,1,0:T(8,128)} %pad.44.targets), custom_call_target="tpu_custom_call" | custom-call | tf_op jit(solution)/shard_map/pallas_call | solution.py:492
  536.0 2.6 multiply_reduce_fusion.6
  538.7 4.6 fusion.4
  543.3 6.2 add_convert_fusion
  549.5 189.3 %shard_map.406 = (bf16[8,288,768]{2,1,0:T(8,128)(2,1)}, f32[4,768,768]{2,1,0:T(8,128)}, f32[4,768,768]{2,1,0:T(8,128)}) custom-call(bf16[8,288,768]{2,1,0:T(8,128)(2,1)} %bitcast.96, bf16[8,288,768]{2,1,0:T(8,128)(2,1)} %get-tuple-element.87.rows_ref, bf16[4,768,768]{2,1,0:T(8,128)(2,1)} %all-gather.6.cloned.1.call-done.inward, ...), custom_call_target="tpu_custom_call" | custom-call | tf_op jit(solution)/shard_map/pallas_call | solution.py:691
  741.6 2.4 iota_compare_fusion.11
  744.8 4.7 slice.144
  751.5 7.0 fusion.10
  761.7 2.6 convolution_convert_fusion.2.g_ref
  764.3 70.0 %shard_map.407 = (bf16[1024,768]{1,0:T(8,128)(2,1)S(1)}, bf16[1024,768]{1,0:T(8,128)(2,1)S(1)}, bf16[1024,768]{1,0:T(8,128)(2,1)S(1)}, f32[12,8,128]{2,1,0:T(8,128)S(1)}) custom-call(bf16[1024,768]{1,0:T(8,128)(2,1)} %copy-done.1, bf16[1024,768]{1,0:T(8,128)(2,1)} %copy-done.2, bf16[1024,768]{1,0:T(8,128)(2,1)} %convolution_convert_fusion.3.v_ref, ...), custom_call_target="tpu_custom_call" | custom-call | tf_op jit(solution)/shard_map/pallas_call | solution.py:1222
  836.6 2.5 convolution_convert_fusion.6
  839.2 3.0 fusion.143
  845.2 3.5 multiply_reduce_fusion.2
  848.8 4.6 reduce-precision_convert_fusion
  860.4 2.7 pad_maximum_fusion
  863.2 5.4 fusion.69
  869.1 83.8 %shard_map.408 = (bf16[32,48,768]{2,1,0:T(8,128)(2,1)}, f32[32,8,128]{2,1,0:T(8,128)S(1)}, f32[96,768]{1,0:T(8,128)S(1)}) custom-call(bf16[32,48,768]{2,1,0:T(8,128)(2,1)S(1)} %bitcast.87, f32[32,8,128]{2,1,0:T(8,128)S(1)} %bitcast.88, bf16[16,2,96,768]{3,2,1,0:T(8,128)(2,1)} %bitcast.89), custom_call_target="tpu_custom_call" | custom-call | tf_op jit(solution)/shard_map/pallas_call | solution.py:907
  953.0 6.5 conditional.3
  953.0 6.3 fusion.141
  961.5 2.9 multiply_reduce_fusion.13
  965.6 5.2 multiply_reduce_fusion.11
  975.4 11.1 %shard_map.409 = f32[32,8,128]{2,1,0:T(8,128)} custom-call(f32[32,8,128]{2,1,0:T(8,128)} %pad.50.src), custom_call_target="tpu_custom_call" | custom-call | tf_op jit(solution)/shard_map/pallas_call | solution.py:125
  992.1 7.6 add_multiply_fusion.2
  999.8 4.3 add_multiply_fusion.1
  1005.6 5.3 add_multiply_fusion
  (261 shorter events, 73.7 us)
Async XLA Ops:
  8.0 25.6 %copy-start.22 = (bf16[1000,768]{1,0:T(8,128)(2,1)S(1)}, bf16[1000,768]{1,0:T(8,128)(2,1)}, u32[]{:S(2)}) copy-start(bf16[1000,768]{1,0:T(8,128)(2,1)} %param.37) | copy-start | bytes 4608004
  13.1 24.7 %copy-start.54 = (s32[1024]{0:T(1024)}, s32[1024]{0:T(1024)S(1)}, u32[]{:S(2)}) copy-start(s32[1024]{0:T(1024)S(1)} %get-tuple-element.169) | copy-start | bytes 12292
  33.6 71.3 %copy-start.52 = (s32[1024]{0:T(1024)S(1)}, s32[1024]{0:T(1024)}, u32[]{:S(2)}) copy-start(s32[1024]{0:T(1024)} %param.30) | copy-start | bytes 12292
  104.9 9.9 copy-start.51
  113.3 24.1 %copy-start.12 = (f32[1024,768]{0,1:T(8,128)}, f32[1024,768]{0,1:T(8,128)S(1)}, u32[]{:S(2)}) copy-start(f32[1024,768]{0,1:T(8,128)S(1)} %get-tuple-element.118) | copy-start | bytes 9437188
  113.3 3.0 copy-start.56
  113.3 3.1 copy-start.67
  113.3 118.0 %all-gather.6.cloned.1.call-start = ((), (), s32[]{:S(2)}) async-start(), calls=%async_computation.5 | async-start | bytes 5898240 | tf_op jit(solution)/shard_map/all_gather | solution.py:1343
  113.9 117.4 %all-gather.8.cloned.1.call-start = ((), (), s32[]{:S(2)}) async-start(), calls=%async_computation.6 | async-start | bytes 5898240 | tf_op jit(solution)/shard_map/all_gather | solution.py:1344
  114.0 105.6 %collective-permute-start = (bf16[1000,768]{1,0:T(8,128)(2,1)}, bf16[1000,768]{1,0:T(8,128)(2,1)}, u32[]{:S(2)}, u32[]{:S(2)}) collective-permute-start(bf16[1000,768]{1,0:T(8,128)(2,1)} %param.37), channel_id=1, source_target_pairs={{0,1},{1,0},{2,3},{3,2},{4,5},{5,4},{6,7},{7,6},{8,9},{9,8},{10,11... | collective-permute-start | bytes 4608008 | tf_op jit(solution)/shard_map/ppermute | solution.py:1352
  114.5 724.6 %reduce-scatter.8.cloned.1.call-start = ((), (), s32[]{:S(2)}) async-start(), calls=%async_computation.7 | async-start | bytes 11796480 | tf_op jit(solution)/shard_map/reduce_scatter | solution.py:1484
  115.9 6.3 copy-start.66
  137.7 7.3 copy-start.43
  143.6 11.0 %copy-start.1 = (bf16[1024,768]{1,0:T(8,128)(2,1)}, bf16[1024,768]{1,0:T(8,128)(2,1)S(1)}, u32[]{:S(2)}) copy-start(bf16[1024,768]{1,0:T(8,128)(2,1)S(1)} %convolution_convert_fusion.5.q_ref) | copy-start | bytes 4718596
  145.0 9.6 copy-start.2
  158.2 47.5 %copy-start.13 = (f32[1024,768]{0,1:T(8,128)S(1)}, f32[1024,768]{0,1:T(8,128)}, u32[]{:S(2)}) copy-start(f32[1024,768]{0,1:T(8,128)} %copy-done.12) | copy-start | bytes 9437188
  158.3 47.5 %copy-start.33 = (bf16[4,2,96,768]{3,2,1,0:T(8,128)(2,1)S(1)}, bf16[4,2,96,768]{3,2,1,0:T(8,128)(2,1)}, u32[]{:S(2)}) copy-start(bf16[4,2,96,768]{3,2,1,0:T(8,128)(2,1)} %get-tuple-element.154) | copy-start | bytes 3538948
  207.9 211.2 %copy-start.15 = (f32[1024,768]{0,1:T(8,128)}, f32[1024,768]{0,1:T(8,128)S(1)}, u32[]{:S(2)}) copy-start(f32[1024,768]{0,1:T(8,128)S(1)} %get-tuple-element.174) | copy-start | bytes 9437188
  412.6 6.5 copy-start.65
  419.1 6.7 copy-start.35
  419.1 8.4 copy-start.57
  538.7 4.6 copy-start.26
  738.9 214.1 %reduce-scatter.10.cloned.1.call-start = ((), (), s32[]{:S(2)}) async-start(), calls=%async_computation.8 | async-start | bytes 11796480 | tf_op jit(solution)/shard_map/reduce_scatter | solution.py:1487
  739.6 4.5 copy-start.21
  749.5 216.0 %collective-permute-start.1 = (f32[1000,768]{1,0:T(8,128)}, f32[1000,768]{1,0:T(8,128)}, u32[]{:S(2)}, u32[]{:S(2)}) collective-permute-start(f32[1000,768]{1,0:T(8,128)} %slice.144), channel_id=1, source_target_pairs={{0,1},{1,0},{2,3},{3,2},{4,5},{5,4},{6,7},{7,6},{8,9},{9,8},{10,11... | collective-permute-start | bytes 9216008 | tf_op jit(solution)/shard_map/ppermute | solution.py:1452
  751.5 7.0 copy-start.16
  761.7 72.6 %copy-start.25 = (f32[1024,768]{0,1:T(8,128)}, f32[1024,768]{0,1:T(8,128)S(1)}, u32[]{:S(2)}) copy-start(f32[1024,768]{0,1:T(8,128)S(1)} %fusion.65) | copy-start | bytes 9437188
  764.3 72.3 %copy-start.6 = (bf16[1024,768]{1,0:T(8,128)(2,1)S(1)}, bf16[1024,768]{1,0:T(8,128)(2,1)}, u32[]{:S(2)}) copy-start(bf16[1024,768]{1,0:T(8,128)(2,1)} %copy-done.5) | copy-start | bytes 4718596
  839.2 3.0 copy-start.10
  839.2 3.0 copy-start.46
  853.5 4.0 copy-start.17
  869.1 83.9 %copy-start.42 = (pred[1536,1000]{1,0:T(32,128)(4,1)S(1)}, pred[1536,1000]{1,0:T(32,128)(4,1)}, u32[]{:S(2)}) copy-start(pred[1536,1000]{1,0:T(32,128)(4,1)} %iota_compare_fusion.11) | copy-start | bytes 4608004
  869.1 83.9 %copy-start.53 = (s32[1024]{0:T(1024)S(1)}, s32[1024]{0:T(1024)}, u32[]{:S(2)}) copy-start(s32[1024]{0:T(1024)} %param.30) | copy-start | bytes 12292
  959.5 4.8 copy-start.28
  965.5 23.2 %copy-start.50 = (bf16[96,768]{1,0:T(8,128)(2,1)S(1)}, bf16[96,768]{1,0:T(8,128)(2,1)}, u32[]{:S(2)}) copy-start(bf16[96,768]{1,0:T(8,128)(2,1)} %src.1) | copy-start | bytes 442372
  965.5 25.3 %copy-start.58 = (bf16[192]{0:T(256)(128)(2,1)S(1)}, bf16[192]{0:T(256)(128)(2,1)}, u32[]{:S(2)}) copy-start(bf16[192]{0:T(256)(128)(2,1)} %param.39) | copy-start | bytes 1156
  965.5 25.3 %copy-start.60 = (f32[192]{0:T(256)S(1)}, f32[192]{0:T(256)}, u32[]{:S(2)}) copy-start(f32[192]{0:T(256)} %param.48) | copy-start | bytes 2308
  965.5 25.3 %copy-start.61 = (f32[192]{0:T(256)S(1)}, f32[192]{0:T(256)}, u32[]{:S(2)}) copy-start(f32[192]{0:T(256)} %param.47) | copy-start | bytes 2308
  965.5 25.9 %copy-start.59 = (bf16[84]{0:T(256)(128)(2,1)S(1)}, bf16[84]{0:T(256)(128)(2,1)}, u32[]{:S(2)}) copy-start(bf16[84]{0:T(256)(128)(2,1)} %param.40) | copy-start | bytes 508
  965.6 25.9 %copy-start.63 = (f32[84]{0:T(128)S(1)}, f32[84]{0:T(128)}, u32[]{:S(2)}) copy-start(f32[84]{0:T(128)} %param.50) | copy-start | bytes 1012
  965.6 25.9 %copy-start.64 = (f32[84]{0:T(128)S(1)}, f32[84]{0:T(128)}, u32[]{:S(2)}) copy-start(f32[84]{0:T(128)} %param.49) | copy-start | bytes 1012
  992.1 7.7 copy-start.29
  992.1 7.7 copy-start.32
  992.1 7.7 copy-start.40
  992.1 7.7 copy-start.41
  999.8 4.3 copy-start.23
  999.8 4.3 copy-start.38
  999.8 5.8 copy-start.39
  (25 other events, 47.0 us)
Sparse Core Ops, SparseCore 1:
  115.4 45.6 all-gather.5
  162.6 37.2 all-gather.7
  739.0 77.4 reduce-scatter.7
  819.2 122.3 reduce-scatter.9

commit v3 on v2

--- a/solution.py
+++ b/solution.py
@@ -167,7 +167,6 @@
     scale,
     picked,
     table,
-    table_t,
     ids,
     targets,
     out,
@@ -184,6 +183,7 @@
     col_in,
     layer_out,
     layer_in,
+    table_t,
     own_sem,
     layer_send,
     layer_recv,
@@ -256,6 +256,9 @@
     own.start()
     table_grad[...] = jnp.zeros_like(table_grad)
     stat_out[...] = jnp.zeros_like(stat_out)
+    for number in range(line_steps):
+        lines = slice(number * lines_step, (number + 1) * lines_step)
+        table_t[:, lines] = table[lines, :].T
     own.wait()
 
     def lines_of(number):
@@ -496,7 +499,7 @@
             jax.ShapeDtypeStruct((lines_all, width), f32),
             jax.ShapeDtypeStruct((8, count), f32),
         ],
-        in_specs=[pl.BlockSpec(memory_space=pl.ANY)] + [near] * 4,
+        in_specs=[pl.BlockSpec(memory_space=pl.ANY)] + [near] * 3,
         out_specs=[near] * 3,
         scratch_shapes=[
             pltpu.VMEM((chips, count, width), bf16),
@@ -510,6 +513,7 @@
             pltpu.VMEM((layers, BLOCK, width, count), bf16),
             pltpu.VMEM((layers, width, count), bf16),
             pltpu.VMEM((layers, width, count), bf16),
+            pltpu.VMEM((width, lines_all), bf16),
             pltpu.SemaphoreType.DMA,
         ]
         + (
@@ -521,7 +525,7 @@
         compiler_params=pltpu.CompilerParams(
             collective_id=call_id, has_side_effects=True, vmem_limit_bytes=60 * 1024 * 1024
         ),
-    )(picked, table, table.T, ids, targets)
+    )(picked, table, ids, targets)
 
 
 def gelu_parts(values):
@@ -578,52 +582,83 @@
     return spot, behind, ahead, go, back
 
 
-def trade_loop(peers, copies, work, own_copies):
+def trade_loop(peers, copies, build, work, collect):
     spot, behind, ahead, go, back = copies
     window = min(WINDOW, peers - 1)
 
     def begin(step, carry):
+        build(ahead(step))
         go(step, spot).start()
         return carry
 
     lax.fori_loop(1, window + 1, begin, 0)
-    own_in, own_out = own_copies
-    own_in.start()
-    own_in.wait()
-    work(spot)
-    own_out.start()
+    build(spot)
+    work(spot, True)
 
     def visit(step, carry):
         origin = behind(step)
-        go(step, origin).wait_recv()
 
         @pl.when(step + window < peers)
         def _():
+            build(ahead(step + window))
             go(step + window, spot).start()
 
-        work(origin)
+        go(step, origin).wait_recv()
+        work(origin, False)
         back(step, origin, spot).start()
         return carry
 
     lax.fori_loop(1, peers, visit, 0)
+    collect(spot, True)
 
     def finish(step, carry):
+        back(step, spot, ahead(step)).wait_recv()
+        collect(ahead(step), False)
+        return carry
+
+    def close(step, carry):
         go(step, spot).wait_send()
         back(step, behind(step), spot).wait_send()
-        back(step, spot, ahead(step)).wait_recv()
         return carry
 
     lax.fori_loop(1, peers, finish, 0)
-    own_out.wait()
-
-
-def experts_kernel(peers, src, inward, outward, landed, returned, done, *sems):
-    copies = trade_copies(peers, src, landed, done, returned, sems[:4])
+    lax.fori_loop(1, peers, close, 0)
+
+
+def slot_mask(marks, at, slots):
+    slot = at * slots + lax.broadcasted_iota(jnp.int32, (slots, 1), 0)
+    return [jnp.where(mark == slot, 1.0, 0.0).astype(jnp.bfloat16) for mark in marks]
+
+
+def experts_kernel(
+    peers,
+    tokens,
+    marks,
+    places,
+    inward,
+    outward,
+    landed,
+    first_out,
+    second_out,
+    src,
+    done,
+    returned,
+    *sems,
+):
+    copies = trade_copies(peers, src, landed, done, returned, sems)
     spot = copies[0]
     f32 = jnp.float32
-
-    def work(at):
-        rows = landed[at]
+    slots = src.shape[1]
+
+    def build(at):
+        first, second = slot_mask((marks[0:1, :], marks[1:2, :]), at, slots)
+        block = jnp.dot(first + second, tokens[...], preferred_element_type=f32)
+        src[at] = block.astype(jnp.bfloat16)
+
+    def work(at, own):
+        rows = src[at] if own else landed[at]
+        if own:
+            landed[at] = rows
         total = jnp.zeros(rows.shape, f32)
         for quarter in range(SPLIT):
             before = jnp.dot(rows, inward[quarter], preferred_element_type=f32)
@@ -633,29 +668,51 @@
             ).astype(f32)
         done[at] = total.astype(jnp.bfloat16)
 
-    trade_loop(
-        peers,
-        copies,
-        work,
-        (
-            pltpu.make_async_copy(src.at[spot], landed.at[spot], sems[4]),
-            pltpu.make_async_copy(done.at[spot], returned.at[spot], sems[5]),
-        ),
-    )
+    def collect(at, own):
+        rows = done[at] if own else returned[at]
+        slot = at * slots + lax.broadcasted_iota(jnp.int32, (1, slots), 1)
+        for number, out in enumerate((first_out, second_out)):
+            mask = jnp.where(places[:, number : number + 1] == slot, 1.0, 0.0).astype(jnp.bfloat16)
+            picked = jnp.dot(mask, rows, preferred_element_type=f32)
+            if own:
+                out[...] = picked
+            else:
+                out[...] += picked
+
+    trade_loop(peers, copies, build, work, collect)
 
 
 def experts_back_kernel(
-    peers, src, rows_ref, inward, outward, returned, inward_grad, outward_grad, landed, done, *sems
+    peers,
+    first_grads,
+    second_grads,
+    marks,
+    rows_ref,
+    inward,
+    outward,
+    returned,
+    inward_grad,
+    outward_grad,
+    src,
+    landed,
+    done,
+    own_sem,
+    *sems,
 ):
-    copies = trade_copies(peers, src, landed, done, returned, sems[:4])
+    copies = trade_copies(peers, src, landed, done, returned, sems)
     spot = copies[0]
     f32 = jnp.float32
-    inward_grad[...] = jnp.zeros_like(inward_grad)
-    outward_grad[...] = jnp.zeros_like(outward_grad)
-
-    def work(at):
+    slots = src.shape[1]
+
+    def build(at):
+        first, second = slot_mask((marks[0:1, :], marks[1:2, :]), at, slots)
+        block = jnp.dot(first, first_grads[...], preferred_element_type=f32)
+        block = block + jnp.dot(second, second_grads[...], preferred_element_type=f32)
+        src[at] = block.astype(jnp.bfloat16)
+
+    def work(at, own):
         rows = rows_ref[at]
-        grads = landed[at]
+        grads = src[at] if own else landed[at]
         total = jnp.zeros(rows.shape, f32)
         for quarter in range(SPLIT):
             before = jnp.dot(rows, inward[quarter], preferred_element_type=f32)
@@ -665,66 +722,65 @@
             total = total + lax.dot_general(
                 grad_before, inward[quarter], NT, preferred_element_type=f32
             ).astype(jnp.bfloat16).astype(f32)
-            inward_grad[quarter] += lax.dot_general(
-                rows, grad_before, TN, preferred_element_type=f32
-            )
-            outward_grad[quarter] += lax.dot_general(
-                hidden.astype(jnp.bfloat16), grads, TN, preferred_element_type=f32
-            )
+            for grad, left, right in (
+                (inward_grad, rows, grad_before),
+                (outward_grad, hidden.astype(jnp.bfloat16), grads),
+            ):
+                part = lax.dot_general(left, right, TN, preferred_element_type=f32)
+                if own:
+                    grad[quarter] = part
+                else:
+                    grad[quarter] += part
         done[at] = total.astype(jnp.bfloat16)
 
-    trade_loop(
-        peers,
-        copies,
-        work,
-        (
-            pltpu.make_async_copy(src.at[spot], landed.at[spot], sems[4]),
-            pltpu.make_async_copy(done.at[spot], returned.at[spot], sems[5]),
-        ),
-    )
-
-
-def trade_call(body, call_id, outgoing, operands, outs, scratch):
-    peers = outgoing.shape[0]
+    def collect(at, own):
+        if own:
+            copy = pltpu.make_async_copy(done.at[at], returned.at[at], own_sem)
+            copy.start()
+            copy.wait()
+
+    trade_loop(peers, copies, build, work, collect)
+
+
+def experts_call(body, call_id, operands, outs, scratch, peers):
     anywhere = pl.BlockSpec(memory_space=pl.ANY)
     near = pl.BlockSpec(memory_space=pltpu.VMEM)
     return pl.pallas_call(
         functools.partial(body, peers),
         out_shape=[shape for shape, _ in outs],
-        in_specs=[anywhere] + [near] * len(operands),
+        in_specs=[near] * len(operands),
         out_specs=[near if inside else anywhere for _, inside in outs],
-        scratch_shapes=scratch
-        + [pltpu.SemaphoreType.DMA((peers,))] * 4
-        + [pltpu.SemaphoreType.DMA] * 2,
+        scratch_shapes=scratch + [pltpu.SemaphoreType.DMA((peers,))] * 4,
         compiler_params=pltpu.CompilerParams(
             collective_id=call_id, has_side_effects=True, vmem_limit_bytes=60 * 1024 * 1024
         ),
-    )(outgoing, *operands)
-
-
-def run_experts(outgoing, inward, outward, call_id):
-    same = jax.ShapeDtypeStruct(outgoing.shape, outgoing.dtype)
-    return trade_call(
+    )(*operands)
+
+
+def run_experts(tokens, marks, places, inward, outward, peers, slots, call_id):
+    block = (peers, slots, tokens.shape[1])
+    low = jax.ShapeDtypeStruct(block, tokens.dtype)
+    wide = jax.ShapeDtypeStruct(tokens.shape, jnp.float32)
+    return experts_call(
         experts_kernel,
         call_id,
-        outgoing,
-        (inward, outward),
-        [(same, True), (same, False)],
-        [pltpu.VMEM(outgoing.shape, outgoing.dtype)],
-    )
-
-
-def run_experts_back(outgoing, rows, inward, outward, call_id):
-    same = jax.ShapeDtypeStruct(outgoing.shape, outgoing.dtype)
+        (tokens, marks, places, inward, outward),
+        [(low, True), (wide, True), (wide, True)],
+        [pltpu.VMEM(block, tokens.dtype)] * 3,
+        peers,
+    )
+
+
+def run_experts_back(first_grads, second_grads, marks, rows, inward, outward, call_id):
+    low = jax.ShapeDtypeStruct(rows.shape, rows.dtype)
     wide = jax.ShapeDtypeStruct(inward.shape, jnp.float32)
-    block = pltpu.VMEM(outgoing.shape, outgoing.dtype)
-    return trade_call(
+    return experts_call(
         experts_back_kernel,
         call_id,
-        outgoing,
-        (rows, inward, outward),
-        [(same, False), (wide, True), (wide, True)],
-        [block, block],
+        (first_grads, second_grads, marks, rows, inward, outward),
+        [(low, False), (wide, True), (wide, True)],
+        [pltpu.VMEM(rows.shape, rows.dtype)] * 3 + [pltpu.SemaphoreType.DMA],
+        rows.shape[0],
     )
 
 
@@ -1420,17 +1476,12 @@
         slot_index < capacity, expert_choice * slots + slot_index, experts_all * slots
     )
     slot_lines = jnp.arange(experts_all * slots, dtype=jnp.int32)
-    first_out = target_row[:, 0][None, :] == slot_lines[:, None]
-    second_out = target_row[:, 1][None, :] == slot_lines[:, None]
     first_in = target_row[:, 0][:, None] == slot_lines[None, :]
     second_in = target_row[:, 1][:, None] == slot_lines[None, :]
-    outgoing = take_rows(first_out | second_out, routed_in).astype(bf16)
-    expert_rows, returned_low = run_experts(
-        outgoing.reshape(experts_all, slots, model_width), inward_full, outward_full, 7
-    )
-    returned_low = returned_low.reshape(experts_all * slots, model_width)
-    returned_first = take_rows(first_in, returned_low)
-    returned_second = take_rows(second_in, returned_low)
+    marks = jnp.pad(target_row.T, ((0, 6), (0, 0)), constant_values=-1)
+    expert_rows, returned_first, returned_second = run_experts(
+        routed_in, marks, target_row, inward_full, outward_full, experts_all, slots, 7
+    )
     after_moe = (
         after_attn + gate_weights[:, 0:1] * returned_first + gate_weights[:, 1:2] * returned_second
     )
@@ -1470,11 +1521,10 @@
         "td,te->de", routed_in, grad_route, preferred_element_type=f32
     ).reshape(-1)
     grad_routed = jnp.einsum("te,de->td", grad_route, router_matrix, preferred_element_type=f32)
-    grad_slots = take_rows(
-        first_out, (gate_weights[:, 0:1] * grad_after_moe).astype(bf16)
-    ) + take_rows(second_out, (gate_weights[:, 1:2] * grad_after_moe).astype(bf16))
     grad_returned, inward_parts, outward_parts = run_experts_back(
-        grad_slots.astype(bf16).reshape(experts_all, slots, model_width),
+        (gate_weights[:, 0:1] * grad_after_moe).astype(bf16),
+        (gate_weights[:, 1:2] * grad_after_moe).astype(bf16),
+        marks,
         expert_rows,
         inward_full,
         outward_full,

time: 1020 us -> 991 us (0.972)
  matrix products: 96.9 us -> 64.8 us
    dot_general x12 -> x7, matrix products: 62.9 us -> 30.3 us  [take_rows(): jnp.dot(mask.astype(jnp.bfloat16), rows, preferred_element_type=jnp.float32)]
    pallas_call x1, Pallas kernels: 47.5 us -> 36.4 us  [attend(): pl.pallas_call(functools.partial(attend_kernel, block, length), grid=(wid...]
    pallas_call x2, Pallas kernels: 371 us -> 381 us  [experts_call(): pl.pallas_call(functools.partial(body, peers), out_shape=[shape for shape...]
    unnamed x141 -> x132, local copies, waits for them, and re-layouts: 24.7 us -> 24.3 us
  transfers between devices with their start and end apart: 6 -> 6, of which waited for: 0 -> 0; matrix products, arithmetic and copies ran while one was open for 12% -> 11% of each run, Pallas kernels for 20% -> 19%
where the time goes in v3:
time: 991 us; the launch traced here: 983 us
  Pallas kernels  762 us (77%)
  other arithmetic  78 us (8%)
  matrix products  64.8 us (7%)
  local copies, waits for them, and re-layouts  50 us (5%)
  between operations  26 us (3%)
    pallas_call x2, Pallas kernels, experts_call(): pl.pallas_call(functools.partial(body, peers), out_shape=[shape for shape...  381 us
    pallas_call x1, Pallas kernels, loss_exchange(): pl.pallas_call(functools.partial(loss_kernel, chips, scale), out_shape=[j...  102 us
    pallas_call x1, Pallas kernels, tail_exchange(): pl.pallas_call(functools.partial(tail_kernel, chips), out_shape=[jax.Shap...  83.6 us
    pallas_call x1, Pallas kernels, attend_back(): pl.pallas_call(functools.partial(attend_back_kernel, block, length), grid...  70 us
    pallas_call x1, Pallas kernels, head_exchange(): pl.pallas_call(functools.partial(head_kernel, chips), out_shape=[jax.Shap...  67 us
    pallas_call x1, Pallas kernels, attend(): pl.pallas_call(functools.partial(attend_kernel, block, length), grid=(wid...  36.4 us
    dot_general x7, matrix products, take_rows(): jnp.dot(mask.astype(jnp.bfloat16), rows, preferred_element_type=jnp.float32)  30.3 us
    unnamed x132, local copies, waits for them, and re-layouts  24.3 us
  transfers between devices with their start and end apart: 6, of which 0 were waited for; matrix products, arithmetic and copies ran while one was open for 11% of the time, Pallas kernels for 19%

profile of v3, /device:TPU:0, one launch (start us, length us, event | category | flops | bytes accessed | tf_op | source)
XLA Modules:
  0.0 982.8 jit_solution(2225951689350123880)
XLA Ops:
  10.1 2.3 convert_reduce_fusion.1
  18.9 11.0 %shard_map.401 = f32[32,8,128]{2,1,0:T(8,128)} custom-call(f32[32,8,128]{2,1,0:T(8,128)} %bitcast.95), custom_call_target="tpu_custom_call" | custom-call | tf_op jit(solution)/shard_map/pallas_call | solution.py:125
  31.5 2.2 iota_compare_fusion.5
  34.5 4.2 convolution_convert_fusion.1
  38.7 67.0 %shard_map.402 = (bf16[32,48,768]{2,1,0:T(8,128)(2,1)}, bf16[16,2,96,768]{3,2,1,0:T(8,128)(2,1)}) custom-call(bf16[32,48,768]{2,1,0:T(8,128)(2,1)} %bitcast.88, bf16[96,768]{1,0:T(8,128)(2,1)} %src.1), custom_call_target="tpu_custom_call" | custom-call | tf_op jit(solution)/shard_map/pallas_call | solution.py:1099
  105.8 4.8 conditional.2
  105.8 4.7 fusion
  115.7 3.6 convert_reduce_fusion
  121.8 3.4 convert_element_type.252
  126.0 4.9 fusion.120
  133.7 2.5 convolution_convert_fusion.3.v_ref
  136.3 6.9 fusion.43.bucket_ref
  143.2 2.2 copy-done
  146.8 36.4 %shard_map.403 = (bf16[1024,768]{1,0:T(8,128)(2,1)S(1)}, f32[6,1024,128]{2,1,0:T(8,128)S(1)}) custom-call(bf16[1024,768]{1,0:T(8,128)(2,1)S(1)} %convolution_convert_fusion.5.q_ref, bf16[1024,768]{1,0:T(8,128)(2,1)S(1)} %convolution_convert_fusion.4.k_ref, bf16[1024,768]{1,0:T(8,128)(2,1)S(1)} %copy-done.3, s32[1024,1024]{1,0:T(8,128)S(1)} %copy-done, ...), custom_call_target="tpu_custom_call" | custom-call | tf_op jit(solution)/shard_map/pallas_call | solution.py:1186
  184.4 2.8 copy-done.13
  187.2 1.6 multiply_reduce_fusion.9
  191.7 1.6 copy.104
  196.7 3.2 fusion.52.table
  199.9 189.5 %shard_map.404 = (bf16[8,288,768]{2,1,0:T(8,128)(2,1)}, f32[1024,768]{1,0:T(8,128)}, f32[1024,768]{1,0:T(8,128)}) custom-call(bf16[1024,768]{1,0:T(8,128)(2,1)} %copy-done.23, s32[8,1024]{1,0:T(8,128)} %pad.46.marks, s32[1024,2]{1,0:T(8,128)} %copy.102.places, bf16[4,768,768]{2,1,0:T(8,128)(2,1)} %all-gather.6.cloned.1.call-done.inward, ...), custom_call_target="tpu_custom_call" | custom-call | tf_op jit(solution)/shard_map/pallas_call | solution.py:748
  389.5 3.9 multiply_reduce_fusion.8
  393.4 1.7 copy-done.17
  396.4 102.1 %shard_map.405 = (f32[768,128]{1,0:T(8,128)}, f32[2048,768]{1,0:T(8,128)}, f32[8,128]{1,0:T(8,128)}) custom-call(bf16[128,768]{1,0:T(8,128)(2,1)} %fusion.63.picked, bf16[2048,768]{1,0:T(8,128)(2,1)} %fusion.52.table, s32[2048,1]{1,0:T(8,128)} %copy.105.ids, s32[4,8,512]{2,1,0:T(8,128)} %pad.49.targets), custom_call_target="tpu_custom_call" | custom-call | tf_op jit(solution)/shard_map/pallas_call | solution.py:495
  504.3 2.0 multiply_reduce_fusion.6
  506.4 2.4 multiply_convert_fusion
  509.0 191.5 %shard_map.406 = (bf16[8,288,768]{2,1,0:T(8,128)(2,1)}, f32[4,768,768]{2,1,0:T(8,128)}, f32[4,768,768]{2,1,0:T(8,128)}) custom-call(bf16[1024,768]{1,0:T(8,128)(2,1)} %get-tuple-element.148.first_grads, bf16[1024,768]{1,0:T(8,128)(2,1)} %get-tuple-element.147.second_grads, s32[8,1024]{1,0:T(8,128)} %pad.46.marks, ...), custom_call_target="tpu_custom_call" | custom-call | tf_op jit(solution)/shard_map/pallas_call | solution.py:748
  701.6 1.7 fusion.47.prefix_ref
  703.3 2.4 iota_compare_fusion.6
  706.6 4.7 slice.140
  713.2 7.2 fusion.3
  723.5 2.6 convolution_convert_fusion.2.g_ref
  726.1 70.0 %shard_map.407 = (bf16[1024,768]{1,0:T(8,128)(2,1)S(1)}, bf16[1024,768]{1,0:T(8,128)(2,1)S(1)}, bf16[1024,768]{1,0:T(8,128)(2,1)S(1)}, f32[12,8,128]{2,1,0:T(8,128)S(1)}) custom-call(bf16[1024,768]{1,0:T(8,128)(2,1)} %copy-done.1, bf16[1024,768]{1,0:T(8,128)(2,1)} %copy-done.2, bf16[1024,768]{1,0:T(8,128)(2,1)} %convolution_convert_fusion.3.v_ref, ...), custom_call_target="tpu_custom_call" | custom-call | tf_op jit(solution)/shard_map/pallas_call | solution.py:1278
  798.4 2.5 convolution_convert_fusion.6
  801.1 3.0 fusion.126
  807.0 3.8 multiply_reduce_fusion.2
  810.9 4.6 reduce-precision_convert_fusion
  816.0 2.2 copy-done.43
  822.6 2.7 pad_maximum_fusion
  825.4 5.5 fusion.53
  831.5 83.6 %shard_map.408 = (bf16[32,48,768]{2,1,0:T(8,128)(2,1)}, f32[32,8,128]{2,1,0:T(8,128)S(1)}, f32[96,768]{1,0:T(8,128)S(1)}) custom-call(bf16[32,48,768]{2,1,0:T(8,128)(2,1)S(1)} %bitcast.82, f32[32,8,128]{2,1,0:T(8,128)S(1)} %bitcast.83, bf16[16,2,96,768]{3,2,1,0:T(8,128)(2,1)} %bitcast.84), custom_call_target="tpu_custom_call" | custom-call | tf_op jit(solution)/shard_map/pallas_call | solution.py:963
  915.2 6.5 conditional.3
  915.2 6.3 fusion.124
  923.6 2.9 multiply_reduce_fusion.13
  927.7 5.2 multiply_reduce_fusion.11
  937.5 10.6 %shard_map.409 = f32[32,8,128]{2,1,0:T(8,128)} custom-call(f32[32,8,128]{2,1,0:T(8,128)} %pad.55.src), custom_call_target="tpu_custom_call" | custom-call | tf_op jit(solution)/shard_map/pallas_call | solution.py:125
  950.4 2.1 add_multiply_fusion.3
  953.8 7.6 add_multiply_fusion.2
  961.5 4.3 add_multiply_fusion.1
  967.3 5.3 add_multiply_fusion
  (247 shorter events, 62.1 us)
Async XLA Ops:
  8.0 26.5 %copy-start.25 = (bf16[1000,768]{1,0:T(8,128)(2,1)S(1)}, bf16[1000,768]{1,0:T(8,128)(2,1)}, u32[]{:S(2)}) copy-start(bf16[1000,768]{1,0:T(8,128)(2,1)} %param.37) | copy-start | bytes 4608004
  34.5 71.3 %copy-start.53 = (s32[1024]{0:T(1024)S(1)}, s32[1024]{0:T(1024)}, u32[]{:S(2)}) copy-start(s32[1024]{0:T(1024)} %param.30) | copy-start | bytes 12292
  105.8 6.4 copy-start.54
  105.8 6.5 copy-start.64
  105.8 7.5 copy-start.52
  110.6 15.1 %copy-start.12 = (f32[1024,768]{1,0:T(8,128)}, f32[1024,768]{1,0:T(8,128)S(1)}, u32[]{:S(2)}) copy-start(f32[1024,768]{1,0:T(8,128)S(1)} %get-tuple-element.172) | copy-start | bytes 9437188
  110.6 5.1 copy-start.63
  110.6 89.3 %all-gather.6.cloned.1.call-start = ((), (), s32[]{:S(2)}) async-start(), calls=%async_computation.5 | async-start | bytes 5898240 | tf_op jit(solution)/shard_map/all_gather | solution.py:1399
  111.2 88.8 %all-gather.8.cloned.1.call-start = ((), (), s32[]{:S(2)}) async-start(), calls=%async_computation.6 | async-start | bytes 5898240 | tf_op jit(solution)/shard_map/all_gather | solution.py:1400
  111.2 85.5 %collective-permute-start = (bf16[1000,768]{1,0:T(8,128)(2,1)}, bf16[1000,768]{1,0:T(8,128)(2,1)}, u32[]{:S(2)}, u32[]{:S(2)}) collective-permute-start(bf16[1000,768]{1,0:T(8,128)(2,1)} %param.37), channel_id=1, source_target_pairs={{0,1},{1,0},{2,3},{3,2},{4,5},{5,4},{6,7},{7,6},{8,9},{9,8},{10,11... | collective-permute-start | bytes 4608008 | tf_op jit(solution)/shard_map/ppermute | solution.py:1408
  111.7 689.1 %reduce-scatter.8.cloned.1.call-start = ((), (), s32[]{:S(2)}) async-start(), calls=%async_computation.7 | async-start | bytes 11796480 | tf_op jit(solution)/shard_map/reduce_scatter | solution.py:1534
  126.0 7.7 copy-start.42
  130.9 2.9 copy-start.34
  132.3 10.9 %copy-start.1 = (bf16[1024,768]{1,0:T(8,128)(2,1)}, bf16[1024,768]{1,0:T(8,128)(2,1)S(1)}, u32[]{:S(2)}) copy-start(bf16[1024,768]{1,0:T(8,128)(2,1)S(1)} %convolution_convert_fusion.5.q_ref) | copy-start | bytes 4718596
  133.7 9.5 copy-start.2
  146.8 36.5 %copy-start.33 = (s32[16,2,128,2]{3,2,1,0:T(8,128)S(1)}, s32[16,2,128,2]{3,2,1,0:T(8,128)}, u32[]{:S(2)}) copy-start(s32[16,2,128,2]{3,2,1,0:T(8,128)} %convert_element_type.252) | copy-start | bytes 98308
  146.8 37.6 %copy-start.48 = (bf16[4,2,96,768]{3,2,1,0:T(8,128)(2,1)S(1)}, bf16[4,2,96,768]{3,2,1,0:T(8,128)(2,1)}, u32[]{:S(2)}) copy-start(bf16[4,2,96,768]{3,2,1,0:T(8,128)(2,1)} %get-tuple-element.143) | copy-start | bytes 3538948
  183.2 5.6 copy-start.4
  183.2 5.6 copy-start.5
  183.2 3.9 copy-start.13
  188.8 200.7 %copy-start.15 = (f32[1024,768]{1,0:T(8,128)}, f32[1024,768]{1,0:T(8,128)S(1)}, u32[]{:S(2)}) copy-start(f32[1024,768]{1,0:T(8,128)S(1)} %get-tuple-element.165) | copy-start | bytes 9437188
  389.5 5.7 copy-start.55
  700.5 214.6 %reduce-scatter.10.cloned.1.call-start = ((), (), s32[]{:S(2)}) async-start(), calls=%async_computation.8 | async-start | bytes 11796480 | tf_op jit(solution)/shard_map/reduce_scatter | solution.py:1537
  701.3 4.5 copy-start.24
  711.3 216.5 %collective-permute-start.1 = (f32[1000,768]{1,0:T(8,128)}, f32[1000,768]{1,0:T(8,128)}, u32[]{:S(2)}, u32[]{:S(2)}) collective-permute-start(f32[1000,768]{1,0:T(8,128)} %slice.140), channel_id=1, source_target_pairs={{0,1},{1,0},{2,3},{3,2},{4,5},{5,4},{6,7},{7,6},{8,9},{9,8},{10,11... | collective-permute-start | bytes 9216008 | tf_op jit(solution)/shard_map/ppermute | solution.py:1503
  713.2 7.2 copy-start.16
  723.5 72.6 %copy-start.28 = (f32[1024,768]{1,0:T(8,128)}, f32[1024,768]{1,0:T(8,128)S(1)}, u32[]{:S(2)}) copy-start(f32[1024,768]{1,0:T(8,128)S(1)} %fusion.49) | copy-start | bytes 9437188
  726.1 72.3 %copy-start.6 = (bf16[1024,768]{1,0:T(8,128)(2,1)S(1)}, bf16[1024,768]{1,0:T(8,128)(2,1)}, u32[]{:S(2)}) copy-start(bf16[1024,768]{1,0:T(8,128)(2,1)} %copy-done.5) | copy-start | bytes 4718596
  801.1 3.0 copy-start.10
  801.1 3.0 copy-start.45
  804.1 2.9 copy-start.35
  815.5 4.0 copy-start.21
  831.4 83.7 %copy-start.41 = (pred[1536,1000]{1,0:T(32,128)(4,1)S(1)}, pred[1536,1000]{1,0:T(32,128)(4,1)}, u32[]{:S(2)}) copy-start(pred[1536,1000]{1,0:T(32,128)(4,1)} %iota_compare_fusion.6) | copy-start | bytes 4608004
  921.7 4.8 copy-start.31
  927.7 22.7 %copy-start.51 = (bf16[96,768]{1,0:T(8,128)(2,1)S(1)}, bf16[96,768]{1,0:T(8,128)(2,1)}, u32[]{:S(2)}) copy-start(bf16[96,768]{1,0:T(8,128)(2,1)} %src.1) | copy-start | bytes 442372
  927.7 24.9 %copy-start.56 = (bf16[192]{0:T(256)(128)(2,1)S(1)}, bf16[192]{0:T(256)(128)(2,1)}, u32[]{:S(2)}) copy-start(bf16[192]{0:T(256)(128)(2,1)} %param.39) | copy-start | bytes 1156
  927.7 24.9 %copy-start.58 = (f32[192]{0:T(256)S(1)}, f32[192]{0:T(256)}, u32[]{:S(2)}) copy-start(f32[192]{0:T(256)} %param.48) | copy-start | bytes 2308
  927.7 24.9 %copy-start.59 = (f32[192]{0:T(256)S(1)}, f32[192]{0:T(256)}, u32[]{:S(2)}) copy-start(f32[192]{0:T(256)} %param.47) | copy-start | bytes 2308
  927.7 25.4 %copy-start.57 = (bf16[84]{0:T(256)(128)(2,1)S(1)}, bf16[84]{0:T(256)(128)(2,1)}, u32[]{:S(2)}) copy-start(bf16[84]{0:T(256)(128)(2,1)} %param.40) | copy-start | bytes 508
  927.7 25.4 %copy-start.61 = (f32[84]{0:T(128)S(1)}, f32[84]{0:T(128)}, u32[]{:S(2)}) copy-start(f32[84]{0:T(128)} %param.50) | copy-start | bytes 1012
  927.7 25.4 %copy-start.62 = (f32[84]{0:T(128)S(1)}, f32[84]{0:T(128)}, u32[]{:S(2)}) copy-start(f32[84]{0:T(128)} %param.49) | copy-start | bytes 1012
  953.8 7.7 copy-start.32
  953.8 7.7 copy-start.36
  953.8 7.7 copy-start.39
  953.8 7.7 copy-start.40
  961.4 4.3 copy-start.26
  961.5 4.3 copy-start.37
  961.5 5.8 copy-start.38
  (21 other events, 36.6 us)
Sparse Core Ops, SparseCore 1:
  112.7 45.5 all-gather.5
  159.8 37.3 all-gather.7
  700.6 77.7 reduce-scatter.7
  781.1 121.8 reduce-scatter.9

commit v4 on v3

--- a/solution.py
+++ b/solution.py
@@ -170,7 +170,8 @@
     ids,
     targets,
     out,
-    table_grad,
+    own_grad,
+    far_grad,
     loss_rows,
     rows,
     scores,
@@ -206,7 +207,8 @@
     count, width = picked.shape
     group = BLOCK * count
     lines_all = table.shape[0]
-    lines_step = min(512, lines_all)
+    half_lines = lines_all // 2
+    lines_step = min(512, half_lines)
     line_steps = lines_all // lines_step
     barrier = pltpu.get_barrier_semaphore()
 
@@ -254,7 +256,8 @@
         to_col(0, turn, picked, chip).start()
     own = pltpu.make_async_copy(picked, rows.at[chip], own_sem)
     own.start()
-    table_grad[...] = jnp.zeros_like(table_grad)
+    own_grad[...] = jnp.zeros_like(own_grad)
+    far_grad[...] = jnp.zeros_like(far_grad)
     stat_out[...] = jnp.zeros_like(stat_out)
     for number in range(line_steps):
         lines = slice(number * lines_step, (number + 1) * lines_step)
@@ -400,8 +403,11 @@
             [log_in[far * BLOCK + part, 0:1, :] for part in range(BLOCK)], axis=1
         )
 
-        def pull_of(number, carry):
-            lines = lines_of(number)
+        for number in range(line_steps):
+            start = number * lines_step
+            lines = slice(start, start + lines_step)
+            grad = own_grad if start < half_lines else far_grad
+            place = slice(start % half_lines, start % half_lines + lines_step)
             vocab = ids[lines, :]
             pull = (
                 1.3 * jnp.exp(score(lines, block) - logs)
@@ -410,10 +416,7 @@
             )
             pull = (pull * scale).astype(bf16)
             pulls[lines, :] = pull
-            table_grad[lines, :] += jnp.dot(pull, block, preferred_element_type=f32)
-            return carry
-
-        lax.fori_loop(0, line_steps, pull_of, 0)
+            grad[place, :] += jnp.dot(pull, block, preferred_element_type=f32)
         grads = jnp.dot(table_t[...], pulls[...], preferred_element_type=f32).astype(bf16)
         for part in range(BLOCK):
             picks[step, part] = grads[:, part * count : (part + 1) * count]
@@ -496,11 +499,12 @@
         functools.partial(loss_kernel, chips, scale),
         out_shape=[
             jax.ShapeDtypeStruct((width, count), f32),
-            jax.ShapeDtypeStruct((lines_all, width), f32),
+            jax.ShapeDtypeStruct((lines_all // 2, width), f32),
+            jax.ShapeDtypeStruct((lines_all // 2, width), f32),
             jax.ShapeDtypeStruct((8, count), f32),
         ],
         in_specs=[pl.BlockSpec(memory_space=pl.ANY)] + [near] * 3,
-        out_specs=[near] * 3,
+        out_specs=[near] * 4,
         scratch_shapes=[
             pltpu.VMEM((chips, count, width), bf16),
             pltpu.VMEM((lines_all, group), f32),
@@ -1496,13 +1500,11 @@
         targets_full.reshape(chips, 2, rows_loss, 2)[:, 1],
     ).reshape(chips // BLOCK, BLOCK * rows_loss, 2)
     targets_here = jnp.pad(targets_here.swapaxes(1, 2), ((0, 0), (0, 6), (0, 0)))
-    picked_grad, chip_grad, loss_rows = loss_exchange(
+    picked_grad, own_grad, far_grad, loss_rows = loss_exchange(
         picked, chip_table, chip_ids, targets_here, chips, scale_rows, 5
     )
     loss_local = jnp.sum(loss_rows[0])
-    table_grad = chip_grad[:vocab_rows] + lax.ppermute(
-        chip_grad[vocab_pad : vocab_pad + vocab_rows], "fsdp", siblings
-    )
+    table_grad = (own_grad + lax.ppermute(far_grad, "fsdp", siblings))[:vocab_rows]
     grad_normed = take_rows_wide(loss_mask.T, picked_grad.T)
     _, final_back = jax.vjp(rms_norm, after_moe, gain_final)
     grad_after_moe, grad_gain_final = final_back(grad_normed)

time: 991 us -> 990 us (level)
    unnamed x132 -> x136, local copies, waits for them, and re-layouts: 24.3 us -> 23.2 us
  transfers between devices with their start and end apart: 6 -> 6, of which waited for: 0 -> 0; matrix products, arithmetic and copies ran while one was open for 11% -> 10% of each run, Pallas kernels for 19% -> 20%
where the time goes in v4:
time: 990 us; the launch traced here: 981 us
  Pallas kernels  768 us (78%)
  other arithmetic  76.7 us (8%)
  matrix products  63.4 us (6%)
  local copies, waits for them, and re-layouts  44.2 us (4%)
  between operations  26.1 us (3%)
    pallas_call x2, Pallas kernels, experts_call(): pl.pallas_call(functools.partial(body, peers), out_shape=[shape for shape...  380 us
    pallas_call x1, Pallas kernels, loss_exchange(): pl.pallas_call(functools.partial(loss_kernel, chips, scale), out_shape=[j...  100 us
    pallas_call x1, Pallas kernels, tail_exchange(): pl.pallas_call(functools.partial(tail_kernel, chips), out_shape=[jax.Shap...  91.1 us
    pallas_call x1, Pallas kernels, attend_back(): pl.pallas_call(functools.partial(attend_back_kernel, block, length), grid...  70.8 us
    pallas_call x1, Pallas kernels, head_exchange(): pl.pallas_call(functools.partial(head_kernel, chips), out_shape=[jax.Shap...  67 us
    pallas_call x1, Pallas kernels, attend(): pl.pallas_call(functools.partial(attend_kernel, block, length), grid=(wid...  36.4 us
    dot_general x7, matrix products, take_rows(): jnp.dot(mask.astype(jnp.bfloat16), rows, preferred_element_type=jnp.float32)  30.4 us
    unnamed x136, local copies, waits for them, and re-layouts  23.2 us
  transfers between devices with their start and end apart: 6, of which 0 were waited for; matrix products, arithmetic and copies ran while one was open for 10% of the time, Pallas kernels for 20%

profile of v4, /device:TPU:0, one launch (start us, length us, event | category | flops | bytes accessed | tf_op | source)
XLA Modules:
  0.0 981.0 jit_solution(273863807173977347)
XLA Ops:
  10.1 2.3 convert_reduce_fusion.1
  18.9 11.0 %shard_map.401 = f32[32,8,128]{2,1,0:T(8,128)} custom-call(f32[32,8,128]{2,1,0:T(8,128)} %bitcast.95), custom_call_target="tpu_custom_call" | custom-call | tf_op jit(solution)/shard_map/pallas_call | solution.py:125
  31.5 2.2 iota_compare_fusion.5
  34.5 4.2 convolution_convert_fusion.1
  38.7 67.0 %shard_map.402 = (bf16[32,48,768]{2,1,0:T(8,128)(2,1)}, bf16[16,2,96,768]{3,2,1,0:T(8,128)(2,1)}) custom-call(bf16[32,48,768]{2,1,0:T(8,128)(2,1)} %bitcast.88, bf16[96,768]{1,0:T(8,128)(2,1)} %src.1), custom_call_target="tpu_custom_call" | custom-call | tf_op jit(solution)/shard_map/pallas_call | solution.py:1103
  105.8 4.8 conditional.2
  105.8 4.7 fusion
  115.7 3.6 convert_reduce_fusion
  121.8 3.4 convert_element_type.252
  126.0 4.8 fusion.122
  133.7 2.5 convolution_convert_fusion.3.v_ref
  136.3 6.9 fusion.43.bucket_ref
  143.2 2.2 copy-done
  146.8 36.4 %shard_map.403 = (bf16[1024,768]{1,0:T(8,128)(2,1)S(1)}, f32[6,1024,128]{2,1,0:T(8,128)S(1)}) custom-call(bf16[1024,768]{1,0:T(8,128)(2,1)S(1)} %convolution_convert_fusion.5.q_ref, bf16[1024,768]{1,0:T(8,128)(2,1)S(1)} %convolution_convert_fusion.4.k_ref, bf16[1024,768]{1,0:T(8,128)(2,1)S(1)} %copy-done.3, s32[1024,1024]{1,0:T(8,128)S(1)} %copy-done, ...), custom_call_target="tpu_custom_call" | custom-call | tf_op jit(solution)/shard_map/pallas_call | solution.py:1190
  184.4 2.8 copy-done.12
  187.2 1.6 multiply_reduce_fusion.9
  191.7 1.6 copy.104
  196.7 3.2 fusion.52.table
  199.9 189.5 %shard_map.404 = (bf16[8,288,768]{2,1,0:T(8,128)(2,1)}, f32[1024,768]{1,0:T(8,128)}, f32[1024,768]{1,0:T(8,128)}) custom-call(bf16[1024,768]{1,0:T(8,128)(2,1)} %copy-done.22, s32[8,1024]{1,0:T(8,128)} %pad.46.marks, s32[1024,2]{1,0:T(8,128)} %copy.102.places, bf16[4,768,768]{2,1,0:T(8,128)(2,1)} %all-gather.6.cloned.1.call-done.inward, ...), custom_call_target="tpu_custom_call" | custom-call | tf_op jit(solution)/shard_map/pallas_call | solution.py:752
  389.4 3.9 multiply_reduce_fusion.8
  393.4 1.7 copy-done.16
  396.4 100.1 %shard_map.405 = (f32[768,128]{1,0:T(8,128)}, f32[1024,768]{1,0:T(8,128)}, f32[1024,768]{1,0:T(8,128)}, f32[8,128]{1,0:T(8,128)}) custom-call(bf16[128,768]{1,0:T(8,128)(2,1)} %fusion.64.picked, bf16[2048,768]{1,0:T(8,128)(2,1)} %fusion.52.table, s32[2048,1]{1,0:T(8,128)} %copy.105.ids, s32[4,8,512]{2,1,0:T(8,128)} %pad.49.targets), custom_call_target="tpu_custom_call" | custom-call | tf_op jit(solution)/shard_map/pallas_call | solution.py:498
  502.3 2.0 multiply_reduce_fusion.6
  504.3 2.4 multiply_convert_fusion
  506.9 191.0 %shard_map.406 = (bf16[8,288,768]{2,1,0:T(8,128)(2,1)}, f32[4,768,768]{2,1,0:T(8,128)}, f32[4,768,768]{2,1,0:T(8,128)}) custom-call(bf16[1024,768]{1,0:T(8,128)(2,1)} %get-tuple-element.150.first_grads, bf16[1024,768]{1,0:T(8,128)(2,1)} %get-tuple-element.149.second_grads, s32[8,1024]{1,0:T(8,128)} %pad.46.marks, ...), custom_call_target="tpu_custom_call" | custom-call | tf_op jit(solution)/shard_map/pallas_call | solution.py:752
  699.0 1.7 fusion.47.prefix_ref
  700.7 2.4 iota_compare_fusion.6
  706.0 7.3 fusion.3
  716.7 2.6 convolution_convert_fusion.2.g_ref
  719.3 70.8 %shard_map.407 = (bf16[1024,768]{1,0:T(8,128)(2,1)S(1)}, bf16[1024,768]{1,0:T(8,128)(2,1)S(1)}, bf16[1024,768]{1,0:T(8,128)(2,1)S(1)}, f32[12,8,128]{2,1,0:T(8,128)S(1)}) custom-call(bf16[1024,768]{1,0:T(8,128)(2,1)} %copy-done.1, bf16[1024,768]{1,0:T(8,128)(2,1)} %copy-done.2, bf16[1024,768]{1,0:T(8,128)(2,1)} %convolution_convert_fusion.3.v_ref, ...), custom_call_target="tpu_custom_call" | custom-call | tf_op jit(solution)/shard_map/pallas_call | solution.py:1282
  792.4 2.5 convolution_convert_fusion.6
  795.0 3.1 fusion.128
  800.4 2.2 multiply_reduce_fusion.2
  802.6 2.0 reduce-precision_convert_fusion
  804.6 1.5 fusion.48
  811.6 2.9 pad_maximum_fusion
  815.2 5.5 fusion.53
  821.2 91.1 %shard_map.408 = (bf16[32,48,768]{2,1,0:T(8,128)(2,1)}, f32[32,8,128]{2,1,0:T(8,128)S(1)}, f32[96,768]{1,0:T(8,128)S(1)}) custom-call(bf16[32,48,768]{2,1,0:T(8,128)(2,1)S(1)} %bitcast.82, f32[32,8,128]{2,1,0:T(8,128)S(1)} %bitcast.83, bf16[16,2,96,768]{3,2,1,0:T(8,128)(2,1)} %bitcast.84), custom_call_target="tpu_custom_call" | custom-call | tf_op jit(solution)/shard_map/pallas_call | solution.py:967
  912.4 6.5 conditional.3
  912.4 6.3 fusion.126
  920.9 2.9 multiply_reduce_fusion.13
  925.0 5.2 multiply_reduce_fusion.11
  934.8 11.6 %shard_map.409 = f32[32,8,128]{2,1,0:T(8,128)} custom-call(f32[32,8,128]{2,1,0:T(8,128)} %pad.55.src), custom_call_target="tpu_custom_call" | custom-call | tf_op jit(solution)/shard_map/pallas_call | solution.py:125
  948.7 2.1 add_multiply_fusion.3
  952.0 7.6 add_multiply_fusion.2
  959.7 4.3 add_multiply_fusion.1
  964.0 1.5 copy-done.38
  965.5 5.3 add_multiply_fusion
  (250 shorter events, 61.3 us)
Async XLA Ops:
  8.0 26.5 %copy-start.24 = (bf16[1000,768]{1,0:T(8,128)(2,1)S(1)}, bf16[1000,768]{1,0:T(8,128)(2,1)}, u32[]{:S(2)}) copy-start(bf16[1000,768]{1,0:T(8,128)(2,1)} %param.37) | copy-start | bytes 4608004
  34.5 71.3 %copy-start.55 = (s32[1024]{0:T(1024)S(1)}, s32[1024]{0:T(1024)}, u32[]{:S(2)}) copy-start(s32[1024]{0:T(1024)} %param.30) | copy-start | bytes 12292
  105.8 6.4 copy-start.56
  105.8 6.5 copy-start.66
  105.8 7.5 copy-start.54
  110.6 15.1 %copy-start.11 = (f32[1024,768]{1,0:T(8,128)}, f32[1024,768]{1,0:T(8,128)S(1)}, u32[]{:S(2)}) copy-start(f32[1024,768]{1,0:T(8,128)S(1)} %get-tuple-element.174) | copy-start | bytes 9437188
  110.6 5.1 copy-start.65
  110.6 89.3 %all-gather.6.cloned.1.call-start = ((), (), s32[]{:S(2)}) async-start(), calls=%async_computation.5 | async-start | bytes 5898240 | tf_op jit(solution)/shard_map/all_gather | solution.py:1403
  111.2 88.7 %all-gather.8.cloned.1.call-start = ((), (), s32[]{:S(2)}) async-start(), calls=%async_computation.6 | async-start | bytes 5898240 | tf_op jit(solution)/shard_map/all_gather | solution.py:1404
  111.2 85.4 %collective-permute-start = (bf16[1000,768]{1,0:T(8,128)(2,1)}, bf16[1000,768]{1,0:T(8,128)(2,1)}, u32[]{:S(2)}, u32[]{:S(2)}) collective-permute-start(bf16[1000,768]{1,0:T(8,128)(2,1)} %param.37), channel_id=1, source_target_pairs={{0,1},{1,0},{2,3},{3,2},{4,5},{5,4},{6,7},{7,6},{8,9},{9,8},{10,11... | collective-permute-start | bytes 4608008 | tf_op jit(solution)/shard_map/ppermute | solution.py:1412
  111.7 683.1 %reduce-scatter.8.cloned.1.call-start = ((), (), s32[]{:S(2)}) async-start(), calls=%async_computation.7 | async-start | bytes 11796480 | tf_op jit(solution)/shard_map/reduce_scatter | solution.py:1536
  126.0 7.7 copy-start.43
  132.3 10.9 %copy-start.1 = (bf16[1024,768]{1,0:T(8,128)(2,1)}, bf16[1024,768]{1,0:T(8,128)(2,1)S(1)}, u32[]{:S(2)}) copy-start(bf16[1024,768]{1,0:T(8,128)(2,1)S(1)} %convolution_convert_fusion.5.q_ref) | copy-start | bytes 4718596
  133.7 9.5 copy-start.2
  146.8 36.5 %copy-start.33 = (s32[16,2,128,2]{3,2,1,0:T(8,128)S(1)}, s32[16,2,128,2]{3,2,1,0:T(8,128)}, u32[]{:S(2)}) copy-start(s32[16,2,128,2]{3,2,1,0:T(8,128)} %convert_element_type.252) | copy-start | bytes 98308
  146.8 37.6 %copy-start.50 = (bf16[4,2,96,768]{3,2,1,0:T(8,128)(2,1)S(1)}, bf16[4,2,96,768]{3,2,1,0:T(8,128)(2,1)}, u32[]{:S(2)}) copy-start(bf16[4,2,96,768]{3,2,1,0:T(8,128)(2,1)} %get-tuple-element.145) | copy-start | bytes 3538948
  183.2 5.6 copy-start.4
  183.2 5.6 copy-start.5
  183.2 3.9 copy-start.12
  188.8 200.7 %copy-start.14 = (f32[1024,768]{1,0:T(8,128)}, f32[1024,768]{1,0:T(8,128)S(1)}, u32[]{:S(2)}) copy-start(f32[1024,768]{1,0:T(8,128)S(1)} %get-tuple-element.167) | copy-start | bytes 9437188
  389.4 5.6 copy-start.57
  697.9 214.4 %reduce-scatter.10.cloned.1.call-start = ((), (), s32[]{:S(2)}) async-start(), calls=%async_computation.8 | async-start | bytes 11796480 | tf_op jit(solution)/shard_map/reduce_scatter | solution.py:1539
  698.7 4.5 copy-start.23
  704.0 221.0 %collective-permute-start.1 = (f32[1024,768]{1,0:T(8,128)}, f32[1024,768]{1,0:T(8,128)}, u32[]{:S(2)}, u32[]{:S(2)}) collective-permute-start(f32[1024,768]{1,0:T(8,128)} %get-tuple-element.89), channel_id=1, source_target_pairs={{0,1},{1,0},{2,3},{3,2},{4,5},{5,4},{6,7},{7,6},{8,9},{9,8},{10,11... | collective-permute-start | bytes 9437192 | tf_op jit(solution)/shard_map/ppermute | solution.py:1507
  706.0 7.3 copy-start.15
  716.7 73.4 %copy-start.27 = (f32[1024,768]{1,0:T(8,128)}, f32[1024,768]{1,0:T(8,128)S(1)}, u32[]{:S(2)}) copy-start(f32[1024,768]{1,0:T(8,128)S(1)} %fusion.49) | copy-start | bytes 9437188
  719.3 73.1 %copy-start.6 = (bf16[1024,768]{1,0:T(8,128)(2,1)S(1)}, bf16[1024,768]{1,0:T(8,128)(2,1)}, u32[]{:S(2)}) copy-start(bf16[1024,768]{1,0:T(8,128)(2,1)} %copy-done.5) | copy-start | bytes 4718596
  795.0 3.1 copy-start.10
  795.0 3.1 copy-start.47
  804.6 4.0 copy-start.20
  811.6 3.2 copy-start.41
  811.6 3.6 copy-start.45
  821.2 91.2 %copy-start.42 = (pred[1536,1000]{1,0:T(32,128)(4,1)S(1)}, pred[1536,1000]{1,0:T(32,128)(4,1)}, u32[]{:S(2)}) copy-start(pred[1536,1000]{1,0:T(32,128)(4,1)} %iota_compare_fusion.6) | copy-start | bytes 4608004
  918.9 4.8 copy-start.31
  925.0 23.7 %copy-start.53 = (bf16[96,768]{1,0:T(8,128)(2,1)S(1)}, bf16[96,768]{1,0:T(8,128)(2,1)}, u32[]{:S(2)}) copy-start(bf16[96,768]{1,0:T(8,128)(2,1)} %src.1) | copy-start | bytes 442372
  925.0 25.8 %copy-start.58 = (bf16[192]{0:T(256)(128)(2,1)S(1)}, bf16[192]{0:T(256)(128)(2,1)}, u32[]{:S(2)}) copy-start(bf16[192]{0:T(256)(128)(2,1)} %param.39) | copy-start | bytes 1156
  925.0 25.8 %copy-start.60 = (f32[192]{0:T(256)S(1)}, f32[192]{0:T(256)}, u32[]{:S(2)}) copy-start(f32[192]{0:T(256)} %param.48) | copy-start | bytes 2308
  925.0 25.8 %copy-start.61 = (f32[192]{0:T(256)S(1)}, f32[192]{0:T(256)}, u32[]{:S(2)}) copy-start(f32[192]{0:T(256)} %param.47) | copy-start | bytes 2308
  925.0 26.4 %copy-start.59 = (bf16[84]{0:T(256)(128)(2,1)S(1)}, bf16[84]{0:T(256)(128)(2,1)}, u32[]{:S(2)}) copy-start(bf16[84]{0:T(256)(128)(2,1)} %param.40) | copy-start | bytes 508
  925.0 26.4 %copy-start.63 = (f32[84]{0:T(128)S(1)}, f32[84]{0:T(128)}, u32[]{:S(2)}) copy-start(f32[84]{0:T(128)} %param.50) | copy-start | bytes 1012
  925.0 26.4 %copy-start.64 = (f32[84]{0:T(128)S(1)}, f32[84]{0:T(128)}, u32[]{:S(2)}) copy-start(f32[84]{0:T(128)} %param.49) | copy-start | bytes 1012
  952.0 7.7 copy-start.32
  952.0 7.7 copy-start.36
  952.0 7.7 copy-start.39
  952.0 7.7 copy-start.40
  959.7 4.3 copy-start.25
  959.7 4.3 copy-start.37
  959.7 5.8 copy-start.38
  (23 other events, 42.2 us)
Sparse Core Ops, SparseCore 1:
  112.7 45.5 all-gather.5
  159.7 37.3 all-gather.7
  698.0 78.1 reduce-scatter.7
  779.0 129.2 reduce-scatter.9
